TPU v7x, 32 devices: a whole 2x2x4 slice. The times are simulated.
32 devices in a mesh: wide: 8 (over z, y), narrow: 4 (over x, core).
Axes of the slice: x: 2, y: 2, z: 4, core: 2. Of those that a mesh axis runs over, the one named last changes fastest.
Arguments:
- tokens: bfloat16 [4096, 4096], P(('wide', 'narrow')), may hold values from -6 to 6
- norm_gain: bfloat16 [4096], P('narrow'), may hold values from 0.099609375 to 1.8984375
- key_weight: bfloat16 [4096, 512], P('narrow'), may hold values from -0.09375 to 0.09375
- key_grad: bfloat16 [4096, 512], P(('wide', 'narrow')), may hold values from -6 to 6
Outputs:
- keys: bfloat16 [4096, 512], P(('wide', 'narrow'))
- weight_grad: float32 [4096, 512], P('narrow')
- gain_grad: float32 [4096], P('narrow')
All inputs are finite; a program needn't handle non-finite values.
Results may differ from a plain program's by a relative error of at most 0.0057.
Values may be sent and summed in bfloat16 or wider, within the bound.
No kernel may reach another device: no remote copies, remote signals or barrier semaphores. Data moves between devices by JAX's collectives and lax.ppermute only.
A program may use at most 64 MiB of HBM per device.

v0:
```python
import math

import jax
import jax.numpy as jnp
from jax import lax
from jax.sharding import PartitionSpec as P

KH = 4
HD = 128
KV = 512
SEQ = 4096


rope_base = 500000.0
norm_eps = 1e-05


def rope_tables(first_row, row_count, head_size):
    position = ((first_row + jnp.arange(row_count, dtype=jnp.int32)) % SEQ).astype(jnp.float32)
    halves = jnp.arange(head_size // 2, dtype=jnp.float32)
    frequency = rope_base ** (-2.0 * halves / head_size)
    angle = position[:, None] * frequency[None, :]
    return (jnp.cos(angle), jnp.sin(angle))


def rotate_keys(projected, cosine, sine_table):
    rows = projected.shape[0]
    heads = projected.reshape(rows, KH, HD)
    front_half = heads[:, :, : HD // 2]
    back_half = heads[:, :, HD // 2 :]
    cosine = cosine[:, None, :]
    sine_table = sine_table[:, None, :]
    joined = jnp.concatenate(
        [
            front_half * cosine - back_half * sine_table,
            back_half * cosine + front_half * sine_table,
        ],
        axis=2,
    )
    return joined.reshape(rows, KV)


def rotate_back(upstream, cosine, sine_table):
    rows = upstream.shape[0]
    heads = upstream.reshape(rows, KH, HD)
    grad_front = heads[:, :, : HD // 2]
    grad_back = heads[:, :, HD // 2 :]
    cosine = cosine[:, None, :]
    sine_table = sine_table[:, None, :]
    joined = jnp.concatenate(
        [
            grad_front * cosine + grad_back * sine_table,
            grad_back * cosine - grad_front * sine_table,
        ],
        axis=2,
    )
    return joined.reshape(rows, KV)


def local(tokens, norm_gain, key_weight, key_grad):
    row_count = tokens.shape[0]
    narrow_size = lax.axis_size("narrow")
    wide_size = lax.axis_size("wide")
    first_row = (lax.axis_index("wide") * narrow_size + lax.axis_index("narrow")) * row_count
    grad_scale = 1.0 / math.sqrt(row_count * narrow_size * wide_size)
    widened = tokens.astype(jnp.float32)
    inv_rms = lax.rsqrt(jnp.mean(widened * widened, axis=1, keepdims=True) + norm_eps)
    normed = widened * inv_rms
    cosine, sine_table = rope_tables(first_row, row_count, HD)
    pre_grad = rotate_back(key_grad.astype(jnp.float32), cosine, sine_table).astype(jnp.bfloat16)
    gain_wide, weight_wide = (
        lax.all_gather(norm_gain, "narrow", axis=0, tiled=True),
        lax.all_gather(key_weight, "narrow", axis=0, tiled=True),
    )
    hidden_in = (normed * gain_wide.astype(jnp.float32)[None, :]).astype(jnp.bfloat16)
    projected = jnp.dot(hidden_in, weight_wide, preferred_element_type=jnp.float32)
    hidden_grad = lax.dot_general(
        pre_grad, weight_wide, (((1,), (1,)), ((), ())), preferred_element_type=jnp.float32
    )
    keys = rotate_keys(projected, cosine, sine_table).astype(jnp.bfloat16)
    weight_term = (
        lax.dot_general(
            hidden_in, pre_grad, (((0,), (0,)), ((), ())), preferred_element_type=jnp.float32
        )
        * grad_scale
    )
    weight_part = weight_term.astype(jnp.bfloat16)
    gain_term = jnp.sum(hidden_grad * normed, axis=0) * grad_scale
    model_width = weight_part.shape[0]
    own_rows = model_width // narrow_size
    half_cols = KV // 2
    front_part = weight_part[:, :half_cols].reshape(narrow_size, own_rows, half_cols)
    back_part = weight_part[:, half_cols:].reshape(narrow_size, own_rows, half_cols)
    front_recv = lax.all_to_all(front_part, "narrow", split_axis=0, concat_axis=0, tiled=True)
    back_recv = lax.all_to_all(back_part, "narrow", split_axis=0, concat_axis=0, tiled=True)
    front_sum = jnp.sum(front_recv.astype(jnp.float32), axis=0)
    back_sum = jnp.sum(back_recv.astype(jnp.float32), axis=0)
    weight_rows = jnp.concatenate([front_sum, back_sum], axis=1)
    gain_rows = lax.psum_scatter(gain_term, "narrow", scatter_dimension=0, tiled=True)
    weight_grad, gain_grad = lax.psum((weight_rows, gain_rows), "wide")
    return (keys, weight_grad, gain_grad)


def solution(mesh):
    return jax.shard_map(
        local,
        mesh=mesh,
        in_specs=(
            P(("wide", "narrow"), None),
            P("narrow"),
            P("narrow", None),
            P(("wide", "narrow"), None),
        ),
        out_specs=(P(("wide", "narrow"), None), P("narrow", None), P("narrow")),
        check_vma=False,
    )
```

profile of v0, /device:TPU:0, one launch (start us, length us, event | category | flops | bytes accessed | tf_op | source)
XLA Modules:
  0.0 226.0 jit_solution(7904011207238140326)
XLA Ops:
  7.2 0.0 copy-start
  7.2 0.0 all-gather.2.cloned.1.call-start
  7.2 0.7 all-gather.2.cloned.1.call-update
  7.9 6.3 %all_gather.6 = bf16[4096]{0:T(1024)(128)(2,1)S(1)} all-gather(bf16[1024]{0:T(1024)(128)(2,1)} %param.5), channel_id=1, replica_groups=mesh['wide'=8,'narrow'=4] {'narrow'}, dimensions={0}, use_global_device_ids=true | all-gather | bytes 10240 | tf_op jit(solution)/shard_map/all_gather | solution.py:72
  14.2 1.0 reshape.108
  15.2 0.0 copy-done
  15.2 0.3 fusion.2
  15.5 0.3 multiply_cosine_fusion
  15.8 30.9 %all-gather.2.cloned.1.call-done = bf16[4096,512]{1,0:T(8,128)(2,1)} async-done(((bf16[1024,512]{1,0:T(8,128)(2,1)}), bf16[4096,512]{1,0:T(8,128)(2,1)}) %all-gather.2.cloned.1.call-update) | async-done | bytes 4194320 | tf_op jit(solution)/shard_map/all_gather | solution.py:73
  46.8 2.9 %fusion.5 = f32[128,512]{1,0:T(8,128)S(1)} fusion(bf16[4096,512]{1,0:T(8,128)(2,1)} %all-gather.2.cloned.1.call-done, bf16[128,4096]{1,0:T(8,128)(2,1)S(1)} %copy-done, f32[4096]{0:T(1024)S(1)} %convert_element_type.35, f32[128]{0:T(128)S(1)} %add_rsqrt_fusion), kind=kOutput, calls=%fused_computation.11 | convolution fusion | flops 538968064 | bytes 5521920 | tf_op jit(solution)/shard_map/dot_general | solution.py:76
  49.7 0.1 reshape.102
  49.8 0.4 add_convert_fusion
  50.3 0.4 pad_maximum_fusion.1
  50.6 1.4 multiply_convert_fusion
  52.0 1.6 fusion.13
  53.6 28.9 %all_to_all.10 = bf16[4,1024,256]{2,1,0:T(8,128)(2,1)} all-to-all(bf16[4,1024,256]{2,1,0:T(8,128)(2,1)S(1)} %bitcast.16), channel_id=1, replica_groups=mesh['wide'=8,'narrow'=4] {'narrow'}, dimensions={0} | all-to-all | bytes 4194304 | tf_op jit(solution)/shard_map/all_to_all | solution.py:95
  82.6 3.6 %all-to-all-start = ((bf16[4,1024,256]{2,1,0:T(8,128)(2,1)}), bf16[4,1024,256]{2,1,0:T(8,128)(2,1)S(1)}, u32[]{:S(2)}, u32[]{:S(2)}) async-start(bf16[4,1024,256]{2,1,0:T(8,128)(2,1)} %bitcast.15), calls=%async_computation | async-start | bytes 4194304 | tf_op jit(solution)/shard_map/all_to_all | solution.py:94
  86.2 0.0 all-reduce.3.cloned.1.call-start
  86.2 2.0 convert_reduce_fusion
  88.2 23.6 %all-to-all-done = bf16[4,1024,256]{2,1,0:T(8,128)(2,1)S(1)} async-done(((bf16[4,1024,256]{2,1,0:T(8,128)(2,1)}), bf16[4,1024,256]{2,1,0:T(8,128)(2,1)S(1)}, u32[]{:S(2)}, u32[]{:S(2)}) %all-to-all-start) | async-done | bytes 2097184 | tf_op jit(solution)/shard_map/all_to_all | solution.py:94
  111.8 0.3 convert_reduce_fusion.1
  112.1 1.6 pad_maximum_fusion
  113.8 0.0 all-reduce.3.cloned.1.call-update
  113.8 0.6 copy-done.2
  114.4 0.6 dynamic-slice
  115.7 0.7 copy.18
  116.3 0.0 copy-done.1
  116.4 3.7 %fusion.3 = f32[4096]{0:T(1024)S(1)} fusion(bf16[128,4096]{1,0:T(8,128)(2,1)S(1)} %copy-done.1, bf16[4096,512]{1,0:T(8,128)(2,1)} %all-gather.2.cloned.1.call-done, f32[128]{0:T(128)S(1)} %add_rsqrt_fusion, bf16[16,8,4,128]{3,2,1,0:T(4,128)(2,1)S(1)} %bitcast.20), kind=kOutput, calls=%fused_computation.10 | convolution fusion | flops 538963968 | bytes 5390848 | tf_op jit(solution)/shard_map/dot_general | solution.py:77
  120.1 10.9 %all-reduce = f32[4096]{0:T(1024)S(1)} all-reduce(f32[4096]{0:T(1024)S(1)} %broadcast_multiply_fusion), channel_id=2, replica_groups=mesh['wide'=8,'narrow'=4] {'narrow'}, use_global_device_ids=true, to_apply=%region_5.6.clone | all-reduce | flops 4096 | bytes 32768
  131.0 22.7 %psum.15 = f32[1024]{0:T(1024)} all-reduce(f32[1024]{0:T(1024)S(1)} %dynamic-slice.1), channel_id=1, replica_groups=mesh['wide'=8,'narrow'=4] {'wide'}, use_global_device_ids=true, to_apply=%region_6.7 | all-reduce | flops 1024 | bytes 8192 | tf_op jit(solution)/shard_map/psum | solution.py:100
  153.7 62.4 %all-reduce.3.cloned.1.call-done = f32[1024,512]{1,0:T(8,128)} async-done(((f32[1024,512]{1,0:T(8,128)}), f32[1024,512]{1,0:T(8,128)}) %all-reduce.3.cloned.1.call-update) | async-done | bytes 2097168 | tf_op jit(solution)/shard_map/psum | solution.py:100
  216.1 3.1 %copy.20 = f32[1024,512]{1,0:T(8,128)} copy(f32[1024,512]{1,0:T(8,128)} %all-reduce.3.cloned.1.call-done) | data formatting | bytes 4194304
  (8 shorter events, 0.0 us)
Async XLA Ops:
  7.2 8.1 %copy-start = (bf16[128,4096]{1,0:T(8,128)(2,1)S(1)}, bf16[128,4096]{1,0:T(8,128)(2,1)}, u32[]{:S(2)}) copy-start(bf16[128,4096]{1,0:T(8,128)(2,1)} %param.4) | copy-start | bytes 3145732
  7.2 39.6 %all-gather.2.cloned.1.call-start = ((), (), s32[]{:S(2)}) async-start(), calls=%async_computation.2 | async-start | bytes 5242880 | tf_op jit(solution)/shard_map/all_gather | solution.py:73
  82.6 29.3 %all-to-all-start = ((bf16[4,1024,256]{2,1,0:T(8,128)(2,1)}), bf16[4,1024,256]{2,1,0:T(8,128)(2,1)S(1)}, u32[]{:S(2)}, u32[]{:S(2)}) async-start(bf16[4,1024,256]{2,1,0:T(8,128)(2,1)} %bitcast.15), calls=%async_computation | async-start | bytes 4194304 | tf_op jit(solution)/shard_map/all_to_all | solution.py:94
  86.2 130.0 %all-reduce.3.cloned.1.call-start = ((), (), s32[]{:S(2)}) async-start(), calls=%async_computation.3 | async-start | bytes 4194304 | tf_op jit(solution)/shard_map/psum | solution.py:100
  113.8 0.7 copy-start.2
  113.8 2.6 %copy-start.1 = (bf16[128,4096]{1,0:T(8,128)(2,1)S(1)}, bf16[128,4096]{1,0:T(8,128)(2,1)}, u32[]{:S(2)}) copy-start(bf16[128,4096]{1,0:T(8,128)(2,1)} %param.4) | copy-start | bytes 3145732
Sparse Core Ops, SparseCore 0:
  9.6 37.1 all-gather.1
  113.9 102.1 all-reduce.2
where the time goes:
time: 227 us; the launch traced here: 226 us
  waiting for transfers between devices  118 us (52%)
  blocking collectives  68.8 us (30%)
  between operations  14.8 us (7%)
  matrix products  8.02 us (4%)
  local copies, waits for them, and re-layouts  7.64 us (3%)
  other arithmetic  5.37 us (2%)
  starting transfers between devices  3.69 us (2%)
    psum x1, waiting for transfers between devices, local(): weight_grad, gain_grad = lax.psum((weight_rows, gain_rows), 'wide')  62.4 us
    all_gather x1, waiting for transfers between devices, local(): lax.all_gather(key_weight, 'narrow', axis=0, tiled=True)  30.9 us
    all_to_all x1, blocking collectives, local(): lax.all_to_all(back_part, 'narrow', split_axis=0, concat_axis=0, tiled=True)  28.9 us
    all_to_all x1, waiting for transfers between devices, local(): lax.all_to_all(front_part, 'narrow', split_axis=0, concat_axis=0, tiled=T...  23.6 us
    psum x1, blocking collectives, local(): weight_grad, gain_grad = lax.psum((weight_rows, gain_rows), 'wide')  22.7 us
    unnamed x1, blocking collectives  10.9 us
    all_gather x1, blocking collectives, local(): lax.all_gather(norm_gain, 'narrow', axis=0, tiled=True)  6.27 us
    unnamed x10, local copies, waits for them, and re-layouts  4.97 us
  transfers between devices with their start and end apart: 3, of which 3 were waited for; matrix products, arithmetic and copies ran while one was open for 4% of the time, Pallas kernels for 0%

commit v1 on v0

v1 whole, which is shorter than its diff:
```python
import functools
import math

import jax
import jax.numpy as jnp
from jax import lax
from jax.experimental import pallas as pl
from jax.experimental.pallas import tpu as pltpu
from jax.sharding import PartitionSpec as P

KH = 4
HD = 128
KV = 512
SEQ = 4096
TILE = 128


rope_base = 500000.0
norm_eps = 1e-05
BF16 = jnp.bfloat16
F32 = jnp.float32
BOTH = ("wide", "narrow")


def rope_tables(first_row, row_count):
    position = ((first_row + jnp.arange(row_count, dtype=jnp.int32)) % SEQ).astype(F32)
    halves = jnp.arange(HD // 2, dtype=F32)
    frequency = rope_base ** (-2.0 * halves / HD)
    angle = position[:, None] * jnp.concatenate([frequency, frequency])[None, :]
    sign = jnp.concatenate([jnp.ones((HD // 2,), F32), -jnp.ones((HD // 2,), F32)])
    return jnp.cos(angle), jnp.sin(angle) * sign[None, :]


def swap_halves(head):
    return jnp.concatenate([head[:, HD // 2 :], head[:, : HD // 2]], axis=1)


def rotate(columns, cosine, sine, direction):
    heads = [columns[:, h * HD : (h + 1) * HD] for h in range(KH)]
    return jnp.concatenate(
        [head * cosine + direction * swap_halves(head) * sine for head in heads], axis=1
    )


def stage_bits(wide_size):
    bits = wide_size.bit_length() - 1
    first = list(range(bits))
    second = first[1:2] + first[:1] + first[2:]
    return first, second


def place(wide_size, stage):
    first, second = stage_bits(wide_size)
    wide, core = lax.axis_index("wide"), lax.axis_index("narrow") & 1
    return lax.select(core == 0, (wide >> first[stage]) & 1, (wide >> second[stage]) & 1)


def swap_wide(value, wide_size, narrow_size, stage):
    first, second = stage_bits(wide_size)
    pairs = []
    for wide in range(wide_size):
        for narrow in range(narrow_size):
            bit = (second if narrow & 1 else first)[stage]
            pairs.append((wide * narrow_size + narrow, (wide ^ (1 << bit)) * narrow_size + narrow))
    return lax.ppermute(value, BOTH, pairs)


def swap_narrow(value, narrow_size, mask):
    return lax.ppermute(value, "narrow", [(i, i ^ mask) for i in range(narrow_size)])


def call(body, outs, *operands, **more):
    whole = pl.BlockSpec(memory_space=pltpu.VMEM)
    return pl.pallas_call(
        body,
        out_shape=[jax.ShapeDtypeStruct(shape, kind) for shape, kind in outs],
        in_specs=[whole] * len(operands),
        out_specs=[whole] * len(outs),
        compiler_params=pltpu.CompilerParams(vmem_limit_bytes=32 * 1024 * 1024),
        **more,
    )(*operands)


def prepare(own, tok_ref, grad_ref, cos_ref, sin_ref, x_one, x_two, core_out, own_out, inv_out):
    rows = tok_ref.shape[0]
    narrow = lax.axis_index("narrow")
    total = jnp.zeros((rows, TILE), F32)
    for at in range(0, tok_ref.shape[1], TILE):
        part = tok_ref[:, at : at + TILE].astype(F32)
        total = total + part * part
    mean = jnp.sum(total, axis=1, keepdims=True) * (1.0 / tok_ref.shape[1])
    inv = lax.rsqrt(mean + norm_eps)
    inv_out[...] = jnp.broadcast_to(inv, (rows, TILE))
    turned = rotate(grad_ref[...].astype(F32), cos_ref[...], sin_ref[...], 1.0)
    scaled = (turned * inv).astype(BF16)

    def features(mask, chunk):
        at = pl.multiple_of((narrow ^ mask) * own + chunk * KV, KV)
        return tok_ref[:, pl.ds(at, KV)]

    x_one[0:rows] = features(2, 0)
    x_one[rows : 2 * rows] = scaled
    x_one[2 * rows :] = features(3, 0)
    x_two[0:rows] = features(2, 1)
    x_two[rows:] = features(3, 1)
    core_out[0:rows] = scaled
    core_out[rows : 2 * rows] = features(1, 0)
    core_out[2 * rows :] = features(1, 1)
    own_out[0:rows] = features(0, 0)
    own_out[rows:] = features(0, 1)


def tokens_of(chunk, rows, own_ref, x_ref, core_ref, last_ref):
    return [
        own_ref[chunk * rows : (chunk + 1) * rows],
        x_ref[0:rows],
        core_ref[(chunk + 1) * rows : (chunk + 2) * rows],
        last_ref[(1 - chunk) * rows : (2 - chunk) * rows],
    ]


def weight_terms(chunk, rows, wide_size, own_ref, sent_ref, x_ref, core_ref, last_ref, *rest):
    if chunk == 0:
        keep, send = rest
        grads = [sent_ref[0:rows], x_ref[rows : 2 * rows], core_ref[0:rows], last_ref[0:rows]]
    else:
        x_first, last_first, keep, send = rest
        grads = [sent_ref[0:rows], x_first[rows : 2 * rows], core_ref[0:rows], last_first[0:rows]]
    upstream = jnp.concatenate(grads, axis=0)
    first, second = place(wide_size, 0), place(wide_size, 1)
    for a in range(2):
        for b in range(2):
            at = pl.multiple_of(((first ^ a) * 2 + (second ^ b)) * TILE, TILE)
            parts = [
                own_ref[chunk * rows : (chunk + 1) * rows, pl.ds(at, TILE)],
                x_ref[0:rows, pl.ds(at, TILE)],
                core_ref[(chunk + 1) * rows : (chunk + 2) * rows, pl.ds(at, TILE)],
                last_ref[(1 - chunk) * rows : (2 - chunk) * rows, pl.ds(at, TILE)],
            ]
            term = lax.dot_general(
                jnp.concatenate(parts, axis=0),
                upstream,
                (((0,), (0,)), ((), ())),
                preferred_element_type=F32,
            )
            target = send if a else keep
            target[b * TILE : (b + 1) * TILE] = term.astype(target.dtype)


def projections(rows, gain_ref, weight_ref, own_ref, x_one, x_two, core_ref, last_one, last_two, keep, send):
    halves = []
    for chunk, (x_ref, last_ref) in enumerate(((x_one, last_one), (x_two, last_two))):
        tokens = jnp.concatenate(tokens_of(chunk, rows, own_ref, x_ref, core_ref, last_ref), axis=0)
        gain = gain_ref[0:1, chunk * KV : (chunk + 1) * KV].astype(F32)
        halves.append((tokens.astype(F32) * gain).astype(BF16))
    product = jnp.dot(halves[0], weight_ref[0:KV], preferred_element_type=F32)
    product = product + jnp.dot(halves[1], weight_ref[KV:], preferred_element_type=F32)
    keep[...] = product[0 : 2 * rows]
    send[...] = product[2 * rows :].astype(BF16)


def finish_keys(mine_ref, got_ref, inv_ref, cos_ref, sin_ref, keys):
    projected = mine_ref[...] + got_ref[...].astype(F32)
    projected = jnp.concatenate(
        [projected[:, h * HD : (h + 1) * HD] * inv_ref[...] for h in range(KH)], axis=1
    )
    keys[...] = rotate(projected, cos_ref[...], sin_ref[...], -1.0).astype(BF16)


def finish_weights(chunk, wide_size, grad_scale, gain_ref, weight_ref, *rest):
    mine, near, far, out, gain_out = rest[-5:]
    first, second = place(wide_size, 0), place(wide_size, 1)
    for a in range(2):
        for b in range(2):
            source = (near if b else mine)[...] if a == 0 else far[b * TILE : (b + 1) * TILE]
            terms = source.astype(F32) * grad_scale
            at = pl.multiple_of(((first ^ a) * 2 + (second ^ b)) * TILE, TILE)
            weight = weight_ref[pl.ds(at, TILE)].astype(F32)
            product = terms * weight
            folded = sum(product[:, h * TILE : (h + 1) * TILE] for h in range(KV // TILE))
            gain_out[pl.ds((first ^ a) * 2 + (second ^ b), 1)] = jnp.sum(folded.T, axis=0, keepdims=True)
            gain = gain_ref[0:1, pl.ds(pl.multiple_of(chunk * KV + at, TILE), TILE)].astype(F32)
            column = jnp.broadcast_to(gain, (TILE, TILE)).T
            for h in range(KV // TILE):
                out[pl.ds(at, TILE), h * TILE : (h + 1) * TILE] = terms[:, h * TILE : (h + 1) * TILE] * column


def write_weights(chunk, wide_size, grad_scale, gain_row, key_weight, mine, near, far, before):
    whole = pl.BlockSpec(memory_space=pltpu.VMEM)
    operands = [gain_row, key_weight]
    specs = [whole, pl.BlockSpec((KV, KV), lambda _: (chunk, 0))]
    aliases = {}
    if before is not None:
        aliases = {2: 0}
        operands.append(before)
        specs.append(pl.BlockSpec(memory_space=pl.ANY))
    return pl.pallas_call(
        functools.partial(finish_weights, chunk, wide_size, grad_scale),
        grid=(1,),
        out_shape=[
            jax.ShapeDtypeStruct(key_weight.shape, F32),
            jax.ShapeDtypeStruct((KV // TILE, TILE), F32),
        ],
        in_specs=specs + [whole] * 3,
        out_specs=[pl.BlockSpec((KV, KV), lambda _: (chunk, 0)), whole],
        input_output_aliases=aliases,
        compiler_params=pltpu.CompilerParams(vmem_limit_bytes=32 * 1024 * 1024),
    )(*operands, mine, near, far)


def sum_over_wide(keep, send, wide_size, narrow_size):
    swap = functools.partial(swap_wide, wide_size=wide_size, narrow_size=narrow_size)
    total = keep + swap(send, stage=0).astype(F32)
    total = total[:TILE] + swap(total[TILE:].astype(BF16), stage=1).astype(F32)
    for stage in range(2, wide_size.bit_length() - 1):
        rounded = total.astype(BF16)
        total = rounded.astype(F32) + swap(rounded, stage=stage).astype(F32)
    mine = total.astype(BF16)
    near = swap(mine, stage=1)
    far = swap(jnp.concatenate([mine, near], axis=0), stage=0)
    return mine, near, far


def by_permutes(tokens, norm_gain, key_weight, key_grad, cosine, sine, grad_scale):
    rows = tokens.shape[0]
    narrow_size, wide_size = lax.axis_size("narrow"), lax.axis_size("wide")
    own = key_weight.shape[0]
    core, over = 1, 2
    swap = functools.partial(swap_narrow, narrow_size=narrow_size)
    x_one, x_two, core_out, own_tokens, inv_rms = call(
        functools.partial(prepare, own),
        [
            ((3 * rows, KV), BF16),
            ((2 * rows, KV), BF16),
            ((3 * rows, KV), BF16),
            ((2 * rows, KV), BF16),
            ((rows, TILE), F32),
        ],
        tokens,
        key_grad,
        cosine,
        sine,
    )
    gain_row = norm_gain.reshape(1, own)
    x_one = swap(x_one, mask=over)
    x_two = swap(x_two, mask=over)
    core_in = swap(core_out, mask=core)
    last_one = swap(x_one[rows:], mask=core)
    last_two = swap(x_two[rows:], mask=core)
    half = [((2 * TILE, KV), F32), ((2 * TILE, KV), BF16)]
    keep_one, send_one = call(
        functools.partial(weight_terms, 0, rows, wide_size),
        half, own_tokens, core_out, x_one, core_in, last_one,
    )
    keep_two, send_two = call(
        functools.partial(weight_terms, 1, rows, wide_size),
        half, own_tokens, core_out, x_two, core_in, last_two, x_one, last_one,
    )
    first_parts = sum_over_wide(keep_one, send_one, wide_size, narrow_size)
    second_parts = sum_over_wide(keep_two, send_two, wide_size, narrow_size)
    keep, send = call(
        functools.partial(projections, rows),
        [((2 * rows, KV), F32), ((2 * rows, KV), BF16)],
        gain_row, key_weight, own_tokens, x_one, x_two, core_in, last_one, last_two,
    )
    pair = keep + swap(send, mask=core).astype(F32)
    got = swap(pair[rows:].astype(BF16), mask=over)
    (keys,) = call(finish_keys, [((rows, KV), BF16)], pair[:rows], got, inv_rms, cosine, sine)
    weight_grad, gain_one = write_weights(0, wide_size, grad_scale, gain_row, key_weight, *first_parts, None)
    weight_grad, gain_two = write_weights(1, wide_size, grad_scale, gain_row, key_weight, *second_parts, weight_grad)
    return keys, weight_grad, jnp.concatenate([gain_one, gain_two], axis=0).reshape(own)


def by_groups(tokens, norm_gain, key_weight, key_grad, cosine, sine, grad_scale):
    widened = tokens.astype(F32)
    inv_rms = lax.rsqrt(jnp.mean(widened * widened, axis=1, keepdims=True) + norm_eps)
    scaled = (rotate(key_grad.astype(F32), cosine, sine, 1.0) * inv_rms).astype(BF16)
    features = lax.all_to_all(tokens, "narrow", split_axis=1, concat_axis=0, tiled=True)
    upstream = lax.all_gather(scaled, "narrow", axis=0, tiled=True)
    gain = norm_gain.astype(F32)
    terms = lax.dot_general(features, upstream, (((0,), (0,)), ((), ())), preferred_element_type=F32)
    terms = lax.psum(terms, "wide") * grad_scale
    gained = (features.astype(F32) * gain[None, :]).astype(BF16)
    product = jnp.dot(gained, key_weight, preferred_element_type=F32)
    projected = lax.psum_scatter(product, "narrow", scatter_dimension=0, tiled=True)
    keys = rotate(projected * inv_rms, cosine, sine, -1.0).astype(BF16)
    return keys, terms * gain[:, None], jnp.sum(terms * key_weight.astype(F32), axis=1)


def local(tokens, norm_gain, key_weight, key_grad):
    row_count = tokens.shape[0]
    narrow_size = lax.axis_size("narrow")
    wide_size = lax.axis_size("wide")
    first_row = (lax.axis_index("wide") * narrow_size + lax.axis_index("narrow")) * row_count
    grad_scale = 1.0 / math.sqrt(row_count * narrow_size * wide_size)
    cosine, sine = rope_tables(first_row, row_count)
    fits = narrow_size == 4 and key_weight.shape[0] == 2 * KV and row_count == TILE
    fits = fits and wide_size >= 4 and wide_size & (wide_size - 1) == 0
    way = by_permutes if fits else by_groups
    return way(tokens, norm_gain, key_weight, key_grad, cosine, sine, grad_scale)


def solution(mesh):
    return jax.shard_map(
        local,
        mesh=mesh,
        in_specs=(
            P(("wide", "narrow"), None),
            P("narrow"),
            P("narrow", None),
            P(("wide", "narrow"), None),
        ),
        out_specs=(P(("wide", "narrow"), None), P("narrow", None), P("narrow")),
        check_vma=False,
    )
```

time: 227 us -> 68.3 us (0.30)
  waiting for transfers between devices: 118 us -> 35.1 us
  blocking collectives: 68.8 us -> 0 us
  starting transfers between devices: 3.69 us -> 22.7 us
  between operations: 14.8 us -> 0.84 us
  matrix products: 8.02 us -> 0 us
  local copies, waits for them, and re-layouts: 7.64 us -> 2.24 us
  Pallas kernels: 0 us -> 5.31 us
  other arithmetic: 5.37 us -> 2.03 us
    psum x1 -> x0, waiting for transfers between devices: 62.4 us -> none  [local(): weight_grad, gain_grad = lax.psum((weight_rows, gain_rows), 'wide')]
    ppermute x0 -> x17, waiting for transfers between devices: none -> 35.1 us  [the longest x7 19.4 us: swap_narrow(): lax.ppermute(value, 'narrow', [(i, i ^ mask) for i in range(narrow_size)])]
    all_gather x1 -> x0, waiting for transfers between devices: 30.9 us -> none  [local(): lax.all_gather(key_weight, 'narrow', axis=0, tiled=True)]
    all_to_all x1 -> x0, blocking collectives: 28.9 us -> none  [local(): lax.all_to_all(back_part, 'narrow', split_axis=0, concat_axis=0, tiled=True)]
    all_to_all x1 -> x0, waiting for transfers between devices: 23.6 us -> none  [local(): lax.all_to_all(front_part, 'narrow', split_axis=0, concat_axis=0, tiled=T...]
    psum x1 -> x0, blocking collectives: 22.7 us -> none  [local(): weight_grad, gain_grad = lax.psum((weight_rows, gain_rows), 'wide')]
    ppermute x0 -> x17, starting transfers between devices: none -> 22.7 us  [the longest x10 17.9 us: swap_wide(): return lax.ppermute(value, BOTH, pairs)]
    unnamed x1 -> x0, blocking collectives: 10.9 us -> none
  transfers between devices with their start and end apart: 3 -> 17, of which waited for: 3 -> 11; matrix products, arithmetic and copies ran while one was open for 4% -> 1% of each run, Pallas kernels for 0% -> 5%
where the time goes in v1:
time: 68.3 us; the launch traced here: 68.2 us
  waiting for transfers between devices  35.1 us (51%)
  starting transfers between devices  22.7 us (33%)
  Pallas kernels  5.31 us (8%)
  local copies, waits for them, and re-layouts  2.24 us (3%)
  other arithmetic  2.03 us (3%)
  between operations  0.84 us (1%)
    ppermute x7, waiting for transfers between devices, swap_narrow(): lax.ppermute(value, 'narrow', [(i, i ^ mask) for i in range(narrow_size)])  19.4 us
    ppermute x10, starting transfers between devices, swap_wide(): return lax.ppermute(value, BOTH, pairs)  17.9 us
    ppermute x10, waiting for transfers between devices, swap_wide(): return lax.ppermute(value, BOTH, pairs)  15.7 us
    ppermute x7, starting transfers between devices, swap_narrow(): lax.ppermute(value, 'narrow', [(i, i ^ mask) for i in range(narrow_size)])  4.77 us
    pallas_call x5, Pallas kernels, call(): pl.pallas_call(body, out_shape=[jax.ShapeDtypeStruct(shape, kind) for sha...  2.85 us
    pallas_call x2, Pallas kernels, write_weights(): pl.pallas_call(functools.partial(finish_weights, chunk, wide_size, grad_s...  2.46 us
    unnamed x8, local copies, waits for them, and re-layouts  2.14 us
  transfers between devices with their start and end apart: 17, of which 11 were waited for; matrix products, arithmetic and copies ran while one was open for 1% of the time, Pallas kernels for 5%

profile of v1, /device:TPU:0, one launch (start us, length us, event | category | flops | bytes accessed | tf_op | source)
XLA Modules:
  0.0 68.2 jit_solution(15539206736523247259)
XLA Ops:
  0.7 1.0 %fusion.2 = (f32[128,128]{1,0:T(8,128)S(1)}, f32[128,128]{1,0:T(8,128)S(1)}) fusion(f32[128]{0:T(128)} %constant.37.clone.1, f32[128]{0:T(128)S(1)} %pad_maximum_fusion.2, f32[128]{0:T(128)S(1)} %fusion.3), kind=kLoop, calls=%fused_computation.16 | loop fusion | flops 32768 | bytes 132608 | tf_op jit(solution)/shard_map/mul | solution.py:31
  1.7 1.2 %copy-done.1 = bf16[128,4096]{1,0:T(8,128)(2,1)S(1)} copy-done((bf16[128,4096]{1,0:T(8,128)(2,1)S(1)}, bf16[128,4096]{1,0:T(8,128)(2,1)}, u32[]{:S(2)}) %copy-start.1) | copy-done | bytes 1048600
  2.9 0.9 %copy-done.2 = bf16[128,512]{1,0:T(8,128)(2,1)S(1)} copy-done((bf16[128,512]{1,0:T(8,128)(2,1)S(1)}, bf16[128,512]{1,0:T(8,128)(2,1)}, u32[]{:S(2)}) %copy-start.2) | copy-done | bytes 131096
  3.8 0.4 shard_map.67
  4.2 3.0 %collective-permute-start = (bf16[384,512]{1,0:T(8,128)(2,1)S(1)}, bf16[384,512]{1,0:T(8,128)(2,1)S(1)}, u32[]{:S(2)}, u32[]{:S(2)}) collective-permute-start(bf16[384,512]{1,0:T(8,128)(2,1)S(1)} %get-tuple-element.19), channel_id=1, source_target_pairs={{0,2},{1,3},{2,0},{3,1},{4,6},{5,7},{6,4},{7,5},{8,10},{9,11},{10,... | collective-permute-start | bytes 1179656 | tf_op jit(solution)/shard_map/ppermute | solution.py:69
  7.3 9.9 %collective-permute-done.x_one.x_ref.rest_0_ = bf16[384,512]{1,0:T(8,128)(2,1)S(1)} collective-permute-done((bf16[384,512]{1,0:T(8,128)(2,1)S(1)}, bf16[384,512]{1,0:T(8,128)(2,1)S(1)}, u32[]{:S(2)}, u32[]{:S(2)}) %collective-permute-start) | collective-permute-done | bytes 393248 | tf_op jit(solution)/shard_map/ppermute | solution.py:69
  17.3 4.7 %collective-permute-done.1.x_two.x_ref = bf16[256,512]{1,0:T(8,128)(2,1)S(1)} collective-permute-done((bf16[256,512]{1,0:T(8,128)(2,1)S(1)}, bf16[256,512]{1,0:T(8,128)(2,1)S(1)}, u32[]{:S(2)}, u32[]{:S(2)}) %collective-permute-start.1) | collective-permute-done | bytes 262176 | tf_op jit(solution)/shard_map/ppermute | solution.py:69
  22.0 1.3 %collective-permute-done.4.last_two.last_ref = bf16[128,512]{1,0:T(8,128)(2,1)S(1)} collective-permute-done((bf16[128,512]{1,0:T(8,128)(2,1)S(1)}, bf16[128,512]{1,0:T(8,128)(2,1)S(1)}, u32[]{:S(2)}, u32[]{:S(2)}) %collective-permute-start.4) | collective-permute-done | bytes 131104 | tf_op jit(solution)/shard_map/ppermute | solution.py:69
  23.4 0.5 shard_map.72
  23.9 1.8 %collective-permute-start.12 = (bf16[256,512]{1,0:T(8,128)(2,1)S(1)}, bf16[256,512]{1,0:T(8,128)(2,1)S(1)}, u32[]{:S(2)}, u32[]{:S(2)}) collective-permute-start(bf16[256,512]{1,0:T(8,128)(2,1)S(1)} %get-tuple-element.29), channel_id=1, source_target_pairs={{0,4},{1,9},{2,6},{3,11},{4,0},{5,13},{6,2},{7,15},{8,12},{9,1},{1... | collective-permute-start | bytes 786440 | tf_op jit(solution)/shard_map/ppermute | solution.py:65
  25.7 0.5 shard_map.70
  26.5 0.7 %shard_map.68 = (f32[256,512]{1,0:T(8,128)S(1)}, bf16[256,512]{1,0:T(8,128)(2,1)S(1)}) custom-call(bf16[1,1024]{1,0:T(2,128)(2,1)S(1)} %reshape.29.gain_ref, bf16[1024,512]{1,0:T(8,128)(2,1)S(1)} %copy-done, bf16[256,512]{1,0:T(8,128)(2,1)S(1)} %get-tuple-element.18.own_ref, bf16[384,512]{1,0:T(8,128)(2,1)S(1)} %collective-permute-done.x_one.x_ref.rest_0_, ...), custom_call_target="tpu_custom_call" | custom-call | tf_op jit(solution)/shard_map/pallas_call | solution.py:74
  27.3 3.0 %collective-permute-done.12 = bf16[256,512]{1,0:T(8,128)(2,1)S(1)} collective-permute-done((bf16[256,512]{1,0:T(8,128)(2,1)S(1)}, bf16[256,512]{1,0:T(8,128)(2,1)S(1)}, u32[]{:S(2)}, u32[]{:S(2)}) %collective-permute-start.12) | collective-permute-done | bytes 262176 | tf_op jit(solution)/shard_map/ppermute | solution.py:65
  30.4 1.9 %collective-permute-start.13 = (bf16[128,512]{1,0:T(8,128)(2,1)S(1)}, bf16[128,512]{1,0:T(8,128)(2,1)S(1)}, u32[]{:S(2)}, u32[]{:S(2)}) collective-permute-start(bf16[128,512]{1,0:T(8,128)(2,1)S(1)} %slice.52), channel_id=1, source_target_pairs={{0,8},{1,5},{2,10},{3,7},{4,12},{5,1},{6,14},{7,3},{8,0},{9,13},{1... | collective-permute-start | bytes 393224 | tf_op jit(solution)/shard_map/ppermute | solution.py:65
  32.3 1.4 %collective-permute-done.7 = bf16[256,512]{1,0:T(8,128)(2,1)S(1)} collective-permute-done((bf16[256,512]{1,0:T(8,128)(2,1)S(1)}, bf16[256,512]{1,0:T(8,128)(2,1)S(1)}, u32[]{:S(2)}, u32[]{:S(2)}) %collective-permute-start.7) | collective-permute-done | bytes 262176 | tf_op jit(solution)/shard_map/ppermute | solution.py:65
  33.8 2.0 %collective-permute-start.8 = (bf16[128,512]{1,0:T(8,128)(2,1)S(1)}, bf16[128,512]{1,0:T(8,128)(2,1)S(1)}, u32[]{:S(2)}, u32[]{:S(2)}) collective-permute-start(bf16[128,512]{1,0:T(8,128)(2,1)S(1)} %slice.53), channel_id=1, source_target_pairs={{0,8},{1,5},{2,10},{3,7},{4,12},{5,1},{6,14},{7,3},{8,0},{9,13},{1... | collective-permute-start | bytes 393224 | tf_op jit(solution)/shard_map/ppermute | solution.py:65
  35.9 2.7 %collective-permute-start.14 = (bf16[128,512]{1,0:T(8,128)(2,1)S(1)}, bf16[128,512]{1,0:T(8,128)(2,1)S(1)}, u32[]{:S(2)}, u32[]{:S(2)}) collective-permute-start(bf16[128,512]{1,0:T(8,128)(2,1)S(1)} %fusion), channel_id=1, source_target_pairs={{0,16},{1,17},{2,18},{3,19},{4,20},{5,21},{6,22},{7,23},{8,24},{9,... | collective-permute-start | bytes 393224 | tf_op jit(solution)/shard_map/ppermute | solution.py:65
  38.5 1.5 %collective-permute-done.8 = bf16[128,512]{1,0:T(8,128)(2,1)S(1)} collective-permute-done((bf16[128,512]{1,0:T(8,128)(2,1)S(1)}, bf16[128,512]{1,0:T(8,128)(2,1)S(1)}, u32[]{:S(2)}, u32[]{:S(2)}) %collective-permute-start.8) | collective-permute-done | bytes 131104 | tf_op jit(solution)/shard_map/ppermute | solution.py:65
  40.0 3.3 %collective-permute-start.9 = (bf16[128,512]{1,0:T(8,128)(2,1)S(1)}, bf16[128,512]{1,0:T(8,128)(2,1)S(1)}, u32[]{:S(2)}, u32[]{:S(2)}) collective-permute-start(bf16[128,512]{1,0:T(8,128)(2,1)S(1)} %fusion.1), channel_id=1, source_target_pairs={{0,16},{1,17},{2,18},{3,19},{4,20},{5,21},{6,22},{7,23},{8,24},{9,... | collective-permute-start | bytes 393224 | tf_op jit(solution)/shard_map/ppermute | solution.py:65
  43.3 4.9 %collective-permute-done.14 = bf16[128,512]{1,0:T(8,128)(2,1)S(1)} collective-permute-done((bf16[128,512]{1,0:T(8,128)(2,1)S(1)}, bf16[128,512]{1,0:T(8,128)(2,1)S(1)}, u32[]{:S(2)}, u32[]{:S(2)}) %collective-permute-start.14) | collective-permute-done | bytes 131104 | tf_op jit(solution)/shard_map/ppermute | solution.py:65
  48.5 1.3 %collective-permute-done.9 = bf16[128,512]{1,0:T(8,128)(2,1)S(1)} collective-permute-done((bf16[128,512]{1,0:T(8,128)(2,1)S(1)}, bf16[128,512]{1,0:T(8,128)(2,1)S(1)}, u32[]{:S(2)}, u32[]{:S(2)}) %collective-permute-start.9) | collective-permute-done | bytes 131104 | tf_op jit(solution)/shard_map/ppermute | solution.py:65
  49.8 0.8 %collective-permute-start.10 = (bf16[128,512]{1,0:T(8,128)(2,1)S(1)}, bf16[128,512]{1,0:T(8,128)(2,1)S(1)}, u32[]{:S(2)}, u32[]{:S(2)}) collective-permute-start(bf16[128,512]{1,0:T(8,128)(2,1)S(1)} %add_convert_fusion.1.rest_0_), channel_id=1, source_target_pairs={{0,8},{1,5},{2,10},{3,7},{4,12},{5,1},{6,14},{7,3},{8,0},{9,13},{1... | collective-permute-start | bytes 393224 | tf_op jit(solution)/shard_map/ppermute | solution.py:65
  50.5 3.3 %collective-permute-done.15.rest_2_ = bf16[128,512]{1,0:T(8,128)(2,1)S(1)} collective-permute-done((bf16[128,512]{1,0:T(8,128)(2,1)S(1)}, bf16[128,512]{1,0:T(8,128)(2,1)S(1)}, u32[]{:S(2)}, u32[]{:S(2)}) %collective-permute-start.15) | collective-permute-done | bytes 131104 | tf_op jit(solution)/shard_map/ppermute | solution.py:65
  53.9 2.5 %collective-permute-start.16 = (bf16[256,512]{1,0:T(8,128)(2,1)S(1)}, bf16[256,512]{1,0:T(8,128)(2,1)S(1)}, u32[]{:S(2)}, u32[]{:S(2)}) collective-permute-start(bf16[256,512]{1,0:T(8,128)(2,1)S(1)} %pad_maximum_fusion.1), channel_id=1, source_target_pairs={{0,4},{1,9},{2,6},{3,11},{4,0},{5,13},{6,2},{7,15},{8,12},{9,1},{1... | collective-permute-start | bytes 786440 | tf_op jit(solution)/shard_map/ppermute | solution.py:65
  56.3 0.3 collective-permute-done.10.rest_1_
  56.7 2.5 %collective-permute-start.11 = (bf16[256,512]{1,0:T(8,128)(2,1)S(1)}, bf16[256,512]{1,0:T(8,128)(2,1)S(1)}, u32[]{:S(2)}, u32[]{:S(2)}) collective-permute-start(bf16[256,512]{1,0:T(8,128)(2,1)S(1)} %pad_maximum_fusion), channel_id=1, source_target_pairs={{0,4},{1,9},{2,6},{3,11},{4,0},{5,13},{6,2},{7,15},{8,12},{9,1},{1... | collective-permute-start | bytes 786440 | tf_op jit(solution)/shard_map/ppermute | solution.py:65
  59.3 1.5 %collective-permute-start.6 = (bf16[128,512]{1,0:T(8,128)(2,1)S(1)}, bf16[128,512]{1,0:T(8,128)(2,1)S(1)}, u32[]{:S(2)}, u32[]{:S(2)}) collective-permute-start(bf16[128,512]{1,0:T(8,128)(2,1)S(1)} %slice.54), channel_id=1, source_target_pairs={{0,2},{1,3},{2,0},{3,1},{4,6},{5,7},{6,4},{7,5},{8,10},{9,11},{10,... | collective-permute-start | bytes 393224 | tf_op jit(solution)/shard_map/ppermute | solution.py:69
  60.8 3.5 %collective-permute-done.6.got_ref = bf16[128,512]{1,0:T(8,128)(2,1)S(1)} collective-permute-done((bf16[128,512]{1,0:T(8,128)(2,1)S(1)}, bf16[128,512]{1,0:T(8,128)(2,1)S(1)}, u32[]{:S(2)}, u32[]{:S(2)}) %collective-permute-start.6) | collective-permute-done | bytes 131104 | tf_op jit(solution)/shard_map/ppermute | solution.py:69
  64.3 0.8 %shard_map.69 = bf16[128,512]{1,0:T(8,128)(2,1)} custom-call(f32[128,512]{1,0:T(8,128)S(1)} %slice.37.mine_ref, bf16[128,512]{1,0:T(8,128)(2,1)S(1)} %collective-permute-done.6.got_ref, f32[128,128]{1,0:T(8,128)S(1)} %get-tuple-element.24.inv_ref, f32[128,128]{1,0:T(8,128)S(1)} %get-tuple-element.34.cos_ref, f32[128,128]{1,0:T(8,128)S(1)} %get-tuple-element.33.sin_ref), custom_call_target="tpu_custom_call" | custom-call | tf_op jit(solution)/shard_map/pallas_call | solution.py:74
  65.1 1.2 %shard_map.71 = (f32[1024,512]{1,0:T(8,128)}, f32[4,128]{1,0:T(4,128)S(1)}) custom-call(bf16[1,1024]{1,0:T(2,128)(2,1)S(1)} %reshape.29.gain_ref, bf16[1024,512]{1,0:T(8,128)(2,1)S(1)} %copy-done, bf16[128,512]{1,0:T(8,128)(2,1)S(1)} %add_convert_fusion.1.rest_0_, bf16[128,512]{1,0:T(8,128)(2,1)S(1)} %collective-permute-done.10.rest_1_, ...), custom_call_target="tpu_custom_call" | custom-call | tf_op jit(solution)/shard_map/pallas_call | solution.py:197
  66.3 1.2 %shard_map.73 = (f32[1024,512]{1,0:T(8,128)}, f32[4,128]{1,0:T(4,128)S(1)}) custom-call(bf16[1,1024]{1,0:T(2,128)(2,1)S(1)} %reshape.29.gain_ref, bf16[1024,512]{1,0:T(8,128)(2,1)S(1)} %copy-done, f32[1024,512]{1,0:T(8,128)} %get-tuple-element.27.rest_0_, bf16[128,512]{1,0:T(8,128)(2,1)S(1)} %add_convert_fusion.rest_1_, ...), custom_call_target="tpu_custom_call", output_to_operand_aliasing={{0}: (2, {})} | custom-call | tf_op jit(solution)/shard_map/pallas_call | solution.py:197
  67.6 0.6 maximum_bitcast_fusion
  (38 shorter events, 1.5 us)
Async XLA Ops:
  1.7 1.2 %copy-start.1 = (bf16[128,4096]{1,0:T(8,128)(2,1)S(1)}, bf16[128,4096]{1,0:T(8,128)(2,1)}, u32[]{:S(2)}) copy-start(bf16[128,4096]{1,0:T(8,128)(2,1)} %tok_ref.1) | copy-start | bytes 3145732
  2.9 0.9 %copy-start.2 = (bf16[128,512]{1,0:T(8,128)(2,1)S(1)}, bf16[128,512]{1,0:T(8,128)(2,1)}, u32[]{:S(2)}) copy-start(bf16[128,512]{1,0:T(8,128)(2,1)} %grad_ref.1) | copy-start | bytes 393220
  4.2 12.9 %collective-permute-start = (bf16[384,512]{1,0:T(8,128)(2,1)S(1)}, bf16[384,512]{1,0:T(8,128)(2,1)S(1)}, u32[]{:S(2)}, u32[]{:S(2)}) collective-permute-start(bf16[384,512]{1,0:T(8,128)(2,1)S(1)} %get-tuple-element.19), channel_id=1, source_target_pairs={{0,2},{1,3},{2,0},{3,1},{4,6},{5,7},{6,4},{7,5},{8,10},{9,11},{10,... | collective-permute-start | bytes 1179656 | tf_op jit(solution)/shard_map/ppermute | solution.py:69
  7.2 14.7 %collective-permute-start.1 = (bf16[256,512]{1,0:T(8,128)(2,1)S(1)}, bf16[256,512]{1,0:T(8,128)(2,1)S(1)}, u32[]{:S(2)}, u32[]{:S(2)}) collective-permute-start(bf16[256,512]{1,0:T(8,128)(2,1)S(1)} %get-tuple-element.20), channel_id=1, source_target_pairs={{0,2},{1,3},{2,0},{3,1},{4,6},{5,7},{6,4},{7,5},{8,10},{9,11},{10,... | collective-permute-start | bytes 786440 | tf_op jit(solution)/shard_map/ppermute | solution.py:69
  7.3 16.1 %collective-permute-start.2 = (bf16[384,512]{1,0:T(8,128)(2,1)S(1)}, bf16[384,512]{1,0:T(8,128)(2,1)S(1)}, u32[]{:S(2)}, u32[]{:S(2)}) collective-permute-start(bf16[384,512]{1,0:T(8,128)(2,1)S(1)} %get-tuple-element.21.sent_ref), channel_id=1, source_target_pairs={{0,1},{1,0},{2,3},{3,2},{4,5},{5,4},{6,7},{7,6},{8,9},{9,8},{10,11... | collective-permute-start | bytes 1179656 | tf_op jit(solution)/shard_map/ppermute | solution.py:69
  17.2 9.4 %copy-start.3 = (bf16[1024]{0:T(1024)(128)(2,1)S(1)}, bf16[1024]{0:T(1024)(128)(2,1)}, u32[]{:S(2)}) copy-start(bf16[1024]{0:T(1024)(128)(2,1)} %param.5) | copy-start | bytes 6148
  17.2 9.3 %copy-start = (bf16[1024,512]{1,0:T(8,128)(2,1)S(1)}, bf16[1024,512]{1,0:T(8,128)(2,1)}, u32[]{:S(2)}) copy-start(bf16[1024,512]{1,0:T(8,128)(2,1)} %weight_ref.5) | copy-start | bytes 3145732
  17.2 6.2 %collective-permute-start.3 = (bf16[256,512]{1,0:T(8,128)(2,1)S(1)}, bf16[256,512]{1,0:T(8,128)(2,1)S(1)}, u32[]{:S(2)}, u32[]{:S(2)}) collective-permute-start(bf16[256,512]{1,0:T(8,128)(2,1)S(1)} %slice.35), channel_id=1, source_target_pairs={{0,1},{1,0},{2,3},{3,2},{4,5},{5,4},{6,7},{7,6},{8,9},{9,8},{10,11... | collective-permute-start | bytes 786440 | tf_op jit(solution)/shard_map/ppermute | solution.py:69
  22.0 1.4 %collective-permute-start.4 = (bf16[128,512]{1,0:T(8,128)(2,1)S(1)}, bf16[128,512]{1,0:T(8,128)(2,1)S(1)}, u32[]{:S(2)}, u32[]{:S(2)}) collective-permute-start(bf16[128,512]{1,0:T(8,128)(2,1)S(1)} %slice.36), channel_id=1, source_target_pairs={{0,1},{1,0},{2,3},{3,2},{4,5},{5,4},{6,7},{7,6},{8,9},{9,8},{10,11... | collective-permute-start | bytes 393224 | tf_op jit(solution)/shard_map/ppermute | solution.py:69
  23.9 6.4 %collective-permute-start.12 = (bf16[256,512]{1,0:T(8,128)(2,1)S(1)}, bf16[256,512]{1,0:T(8,128)(2,1)S(1)}, u32[]{:S(2)}, u32[]{:S(2)}) collective-permute-start(bf16[256,512]{1,0:T(8,128)(2,1)S(1)} %get-tuple-element.29), channel_id=1, source_target_pairs={{0,4},{1,9},{2,6},{3,11},{4,0},{5,13},{6,2},{7,15},{8,12},{9,1},{1... | collective-permute-start | bytes 786440 | tf_op jit(solution)/shard_map/ppermute | solution.py:65
  26.2 7.5 %collective-permute-start.7 = (bf16[256,512]{1,0:T(8,128)(2,1)S(1)}, bf16[256,512]{1,0:T(8,128)(2,1)S(1)}, u32[]{:S(2)}, u32[]{:S(2)}) collective-permute-start(bf16[256,512]{1,0:T(8,128)(2,1)S(1)} %get-tuple-element.26), channel_id=1, source_target_pairs={{0,4},{1,9},{2,6},{3,11},{4,0},{5,13},{6,2},{7,15},{8,12},{9,1},{1... | collective-permute-start | bytes 786440 | tf_op jit(solution)/shard_map/ppermute | solution.py:65
  27.3 31.9 %collective-permute-start.5 = (bf16[256,512]{1,0:T(8,128)(2,1)S(1)}, bf16[256,512]{1,0:T(8,128)(2,1)S(1)}, u32[]{:S(2)}, u32[]{:S(2)}) collective-permute-start(bf16[256,512]{1,0:T(8,128)(2,1)S(1)} %get-tuple-element.23), channel_id=1, source_target_pairs={{0,1},{1,0},{2,3},{3,2},{4,5},{5,4},{6,7},{7,6},{8,9},{9,8},{10,11... | collective-permute-start | bytes 786440 | tf_op jit(solution)/shard_map/ppermute | solution.py:69
  30.4 5.4 %collective-permute-start.13 = (bf16[128,512]{1,0:T(8,128)(2,1)S(1)}, bf16[128,512]{1,0:T(8,128)(2,1)S(1)}, u32[]{:S(2)}, u32[]{:S(2)}) collective-permute-start(bf16[128,512]{1,0:T(8,128)(2,1)S(1)} %slice.52), channel_id=1, source_target_pairs={{0,8},{1,5},{2,10},{3,7},{4,12},{5,1},{6,14},{7,3},{8,0},{9,13},{1... | collective-permute-start | bytes 393224 | tf_op jit(solution)/shard_map/ppermute | solution.py:65
  33.8 6.2 %collective-permute-start.8 = (bf16[128,512]{1,0:T(8,128)(2,1)S(1)}, bf16[128,512]{1,0:T(8,128)(2,1)S(1)}, u32[]{:S(2)}, u32[]{:S(2)}) collective-permute-start(bf16[128,512]{1,0:T(8,128)(2,1)S(1)} %slice.53), channel_id=1, source_target_pairs={{0,8},{1,5},{2,10},{3,7},{4,12},{5,1},{6,14},{7,3},{8,0},{9,13},{1... | collective-permute-start | bytes 393224 | tf_op jit(solution)/shard_map/ppermute | solution.py:65
  35.9 12.3 %collective-permute-start.14 = (bf16[128,512]{1,0:T(8,128)(2,1)S(1)}, bf16[128,512]{1,0:T(8,128)(2,1)S(1)}, u32[]{:S(2)}, u32[]{:S(2)}) collective-permute-start(bf16[128,512]{1,0:T(8,128)(2,1)S(1)} %fusion), channel_id=1, source_target_pairs={{0,16},{1,17},{2,18},{3,19},{4,20},{5,21},{6,22},{7,23},{8,24},{9,... | collective-permute-start | bytes 393224 | tf_op jit(solution)/shard_map/ppermute | solution.py:65
  40.0 9.7 %collective-permute-start.9 = (bf16[128,512]{1,0:T(8,128)(2,1)S(1)}, bf16[128,512]{1,0:T(8,128)(2,1)S(1)}, u32[]{:S(2)}, u32[]{:S(2)}) collective-permute-start(bf16[128,512]{1,0:T(8,128)(2,1)S(1)} %fusion.1), channel_id=1, source_target_pairs={{0,16},{1,17},{2,18},{3,19},{4,20},{5,21},{6,22},{7,23},{8,24},{9,... | collective-permute-start | bytes 393224 | tf_op jit(solution)/shard_map/ppermute | solution.py:65
  48.2 5.7 %collective-permute-start.15 = (bf16[128,512]{1,0:T(8,128)(2,1)S(1)}, bf16[128,512]{1,0:T(8,128)(2,1)S(1)}, u32[]{:S(2)}, u32[]{:S(2)}) collective-permute-start(bf16[128,512]{1,0:T(8,128)(2,1)S(1)} %add_convert_fusion.rest_1_), channel_id=1, source_target_pairs={{0,8},{1,5},{2,10},{3,7},{4,12},{5,1},{6,14},{7,3},{8,0},{9,13},{1... | collective-permute-start | bytes 393224 | tf_op jit(solution)/shard_map/ppermute | solution.py:65
  49.8 6.9 %collective-permute-start.10 = (bf16[128,512]{1,0:T(8,128)(2,1)S(1)}, bf16[128,512]{1,0:T(8,128)(2,1)S(1)}, u32[]{:S(2)}, u32[]{:S(2)}) collective-permute-start(bf16[128,512]{1,0:T(8,128)(2,1)S(1)} %add_convert_fusion.1.rest_0_), channel_id=1, source_target_pairs={{0,8},{1,5},{2,10},{3,7},{4,12},{5,1},{6,14},{7,3},{8,0},{9,13},{1... | collective-permute-start | bytes 393224 | tf_op jit(solution)/shard_map/ppermute | solution.py:65
  53.9 12.4 %collective-permute-start.16 = (bf16[256,512]{1,0:T(8,128)(2,1)S(1)}, bf16[256,512]{1,0:T(8,128)(2,1)S(1)}, u32[]{:S(2)}, u32[]{:S(2)}) collective-permute-start(bf16[256,512]{1,0:T(8,128)(2,1)S(1)} %pad_maximum_fusion.1), channel_id=1, source_target_pairs={{0,4},{1,9},{2,6},{3,11},{4,0},{5,13},{6,2},{7,15},{8,12},{9,1},{1... | collective-permute-start | bytes 786440 | tf_op jit(solution)/shard_map/ppermute | solution.py:65
  56.7 8.4 %collective-permute-start.11 = (bf16[256,512]{1,0:T(8,128)(2,1)S(1)}, bf16[256,512]{1,0:T(8,128)(2,1)S(1)}, u32[]{:S(2)}, u32[]{:S(2)}) collective-permute-start(bf16[256,512]{1,0:T(8,128)(2,1)S(1)} %pad_maximum_fusion), channel_id=1, source_target_pairs={{0,4},{1,9},{2,6},{3,11},{4,0},{5,13},{6,2},{7,15},{8,12},{9,1},{1... | collective-permute-start | bytes 786440 | tf_op jit(solution)/shard_map/ppermute | solution.py:65
  59.3 5.0 %collective-permute-start.6 = (bf16[128,512]{1,0:T(8,128)(2,1)S(1)}, bf16[128,512]{1,0:T(8,128)(2,1)S(1)}, u32[]{:S(2)}, u32[]{:S(2)}) collective-permute-start(bf16[128,512]{1,0:T(8,128)(2,1)S(1)} %slice.54), channel_id=1, source_target_pairs={{0,2},{1,3},{2,0},{3,1},{4,6},{5,7},{6,4},{7,5},{8,10},{9,11},{10,... | collective-permute-start | bytes 393224 | tf_op jit(solution)/shard_map/ppermute | solution.py:69

commit v2 on v1

v2 whole, which is shorter than its diff:
```python
import functools
import math

import jax
import jax.numpy as jnp
from jax import lax
from jax.experimental import pallas as pl
from jax.experimental.pallas import tpu as pltpu
from jax.sharding import PartitionSpec as P

KH = 4
HD = 128
KV = 512
SEQ = 4096
TILE = 128


rope_base = 500000.0
norm_eps = 1e-05
BF16 = jnp.bfloat16
F32 = jnp.float32
BOTH = ("wide", "narrow")
CHUNKS = (4, 4)


def rope_tables(first_row, row_count):
    position = ((first_row + jnp.arange(row_count, dtype=jnp.int32)) % SEQ).astype(F32)
    halves = jnp.arange(HD // 2, dtype=F32)
    frequency = rope_base ** (-2.0 * halves / HD)
    angle = position[:, None] * frequency[None, :]
    cosine, sine = jnp.cos(angle), jnp.sin(angle)
    return jnp.concatenate([cosine, cosine], axis=1), jnp.concatenate([sine, -sine], axis=1)


def swap_halves(head):
    return jnp.concatenate([head[:, HD // 2 :], head[:, : HD // 2]], axis=1)


def rotate(columns, cosine, sine, direction):
    heads = [columns[:, h * HD : (h + 1) * HD] for h in range(KH)]
    return jnp.concatenate(
        [head * cosine + direction * swap_halves(head) * sine for head in heads], axis=1
    )


def stage_bits(wide_size):
    bits = wide_size.bit_length() - 1
    first = list(range(bits))
    second = first[1:] + first[:1]
    return first, second


def place(wide_size, stage):
    first, second = stage_bits(wide_size)
    wide, core = lax.axis_index("wide"), lax.axis_index("narrow") & 1
    return lax.select(core == 0, (wide >> first[stage]) & 1, (wide >> second[stage]) & 1)


def swap_wide(value, wide_size, narrow_size, stage):
    first, second = stage_bits(wide_size)
    pairs = []
    for wide in range(wide_size):
        for narrow in range(narrow_size):
            bit = (second if narrow & 1 else first)[stage]
            pairs.append((wide * narrow_size + narrow, (wide ^ (1 << bit)) * narrow_size + narrow))
    return lax.ppermute(value, BOTH, pairs)


def swap_narrow(value, narrow_size, mask):
    return lax.ppermute(value, "narrow", [(i, i ^ mask) for i in range(narrow_size)])


def after(value, *others):
    return lax.optimization_barrier((value, *others))[0]


def call(body, outs, *operands, scratch=(), anywhere=(), **more):
    whole = pl.BlockSpec(memory_space=pltpu.VMEM)
    far = pl.BlockSpec(memory_space=pl.ANY)
    return pl.pallas_call(
        body,
        out_shape=[jax.ShapeDtypeStruct(shape, kind) for shape, kind, *_ in outs],
        in_specs=[far if i in anywhere else whole for i in range(len(operands))],
        out_specs=[far if len(out) > 2 else whole for out in outs],
        scratch_shapes=scratch,
        compiler_params=pltpu.CompilerParams(vmem_limit_bytes=32 * 1024 * 1024),
        **more,
    )(*operands)


def features_at(own, mask, start):
    return pl.multiple_of((lax.axis_index("narrow") ^ mask) * own + start, TILE)


def first_tokens(own, size, tok_ref, x_out, arrived):
    copies = [
        pltpu.make_async_copy(
            tok_ref.at[:, pl.ds(features_at(own, mask, 0), size)],
            x_out.at[:, pl.ds(at * size, size)],
            arrived.at[at],
        )
        for at, mask in enumerate((2, 3))
    ]
    for copy in copies:
        copy.start()
    for copy in copies:
        copy.wait()


def prepare(own, chunks, tok_ref, grad_ref, cos_ref, sin_ref, scaled_out, core_out, own_out, inv_out, *x_outs):
    rows = tok_ref.shape[0]
    total = jnp.zeros((rows, TILE), F32)
    for at in range(0, tok_ref.shape[1], TILE):
        part = tok_ref[:, at : at + TILE].astype(F32)
        total = total + part * part
    mean = jnp.sum(total, axis=1, keepdims=True) * (1.0 / tok_ref.shape[1])
    inv = lax.rsqrt(mean + norm_eps)
    inv_out[...] = jnp.broadcast_to(inv, (rows, TILE))
    turned = rotate(grad_ref[...].astype(F32), cos_ref[...], sin_ref[...], 1.0)
    scaled = (turned * inv).astype(BF16)
    scaled_out[...] = scaled
    core_out[:, :KV] = scaled
    core_out[:, KV:] = tok_ref[:, pl.ds(features_at(own, 1, 0), own)]
    own_out[...] = tok_ref[:, pl.ds(features_at(own, 0, 0), own)]
    for (start, size), x_out in zip(chunks[1:], x_outs, strict=True):
        x_out[:, :size] = tok_ref[:, pl.ds(features_at(own, 2, start), size)]
        x_out[:, size:] = tok_ref[:, pl.ds(features_at(own, 3, start), size)]


def tokens_of(start, size, own_ref, core_ref, x_ref, last_ref):
    return jnp.concatenate(
        [
            own_ref[:, start : start + size],
            x_ref[:, :size],
            core_ref[:, KV + start : KV + start + size],
            last_ref[...],
        ],
        axis=0,
    )


def quarters(wide_size):
    first, second = place(wide_size, 0), place(wide_size, 1)
    return [
        pl.multiple_of(((first ^ a) * 2 + (second ^ b)) * TILE, TILE) for a in (0, 1) for b in (0, 1)
    ]


def weight_terms(start, size, wide_size, own_ref, core_ref, x_ref, last_ref, scaled_ref, x_grad, last_grad, keep, send):
    tokens = tokens_of(start, size, own_ref, core_ref, x_ref, last_ref)
    columns = [
        jnp.concatenate([ref[:, pl.ds(at, TILE)] for at in quarters(wide_size)], axis=1)
        for ref in (scaled_ref, x_grad, core_ref, last_grad)
    ]
    terms = lax.dot_general(
        tokens, jnp.concatenate(columns, axis=0), (((0,), (0,)), ((), ())), preferred_element_type=F32
    )
    for b in range(2):
        keep[b] = terms[:, b * TILE : (b + 1) * TILE]
        send[b] = terms[:, (2 + b) * TILE : (3 + b) * TILE].astype(BF16)


def projections(rows, chunks, gain_ref, weight_ref, own_ref, core_ref, *rest):
    keep, send = rest[-2:]
    product = None
    for (start, size), x_ref, last_ref in zip(chunks, rest[: len(chunks)], rest[len(chunks) : -2], strict=True):
        tokens = tokens_of(start, size, own_ref, core_ref, x_ref, last_ref)
        gain = gain_ref[0:1, start : start + size].astype(F32)
        gained = (tokens.astype(F32) * gain).astype(BF16)
        term = jnp.dot(gained, weight_ref[start : start + size], preferred_element_type=F32)
        product = term if product is None else product + term
    keep[...] = product[0 : 2 * rows]
    send[...] = product[2 * rows :].astype(BF16)


def finish_keys(mine_ref, got_ref, inv_ref, cos_ref, sin_ref, keys):
    projected = mine_ref[...] + got_ref[...].astype(F32)
    projected = jnp.concatenate(
        [projected[:, h * HD : (h + 1) * HD] * inv_ref[...] for h in range(KH)], axis=1
    )
    keys[...] = rotate(projected, cos_ref[...], sin_ref[...], -1.0).astype(BF16)


def finish_weights(start, size, wide_size, grad_scale, gain_ref, weight_ref, mine, near, far, *rest):
    gain_before = rest[1] if len(rest) > 5 else None
    out, gain_out, held, sent = rest[-4:]
    if gain_before is not None:
        gain_out[...] = gain_before[...]
    copies = []
    for row in range(0, size, TILE):
        rows = slice(row, row + TILE)
        gain = gain_ref[0:1, start + row : start + row + TILE].astype(F32) * grad_scale
        column = jnp.broadcast_to(gain, (TILE, TILE)).T
        folded = jnp.zeros((TILE, TILE), F32)
        for part, at in enumerate(quarters(wide_size)):
            source = (mine[rows], near[rows], far[0, rows], far[1, rows])[part].astype(F32)
            weight = weight_ref[start + row : start + row + TILE, pl.ds(at, TILE)].astype(F32)
            folded = folded + source * weight
            held[rows, pl.ds(at, TILE)] = source * column
        copy = pltpu.make_async_copy(
            held.at[rows], out.at[start + row : start + row + TILE], sent.at[row // TILE]
        )
        copy.start()
        copies.append(copy)
        at = (start + row) // TILE
        gain_out[at : at + 1] = jnp.sum(folded.T, axis=0, keepdims=True) * grad_scale
    for copy in copies:
        copy.wait()


def write_weights(start, size, wide_size, grad_scale, gain_row, key_weight, parts, before):
    own = key_weight.shape[0]
    return call(
        functools.partial(finish_weights, start, size, wide_size, grad_scale),
        [((own, KV), F32, "far"), ((own // TILE, TILE), F32)],
        gain_row, key_weight, *parts, *before,
        anywhere=(5,),
        scratch=[pltpu.VMEM((size, KV), F32), pltpu.SemaphoreType.DMA((size // TILE,))],
        input_output_aliases={5: 0} if before else {},
    )


def by_permutes(tokens, norm_gain, key_weight, key_grad, cosine, sine, grad_scale):
    rows = tokens.shape[0]
    narrow_size, wide_size = lax.axis_size("narrow"), lax.axis_size("wide")
    own = key_weight.shape[0]
    core, over = 1, 2
    swap = functools.partial(swap_narrow, narrow_size=narrow_size)
    summed = functools.partial(swap_wide, wide_size=wide_size, narrow_size=narrow_size)
    chunks = []
    for eighths in CHUNKS:
        chunks.append((sum(size for _, size in chunks), own * eighths // 8))
    gain_row = norm_gain.reshape(1, own)

    (x_first,) = call(
        functools.partial(first_tokens, own, chunks[0][1]),
        [((rows, 2 * chunks[0][1]), BF16)],
        tokens,
        anywhere=(0,),
        scratch=[pltpu.SemaphoreType.DMA((2,))],
    )
    x_in = [swap(x_first, mask=over)]
    scaled, core_out, own_tokens, inv_rms, *x_outs = call(
        functools.partial(prepare, own, chunks),
        [
            ((rows, KV), BF16),
            ((rows, KV + own), BF16),
            ((rows, own), BF16),
            ((rows, TILE), F32),
            *[((rows, 2 * size), BF16) for _, size in chunks[1:]],
        ],
        after(tokens, x_first), key_grad, cosine, sine,
    )
    x_grad = swap(scaled, mask=over)
    core_in = swap(core_out, mask=core)
    x_in = x_in + [swap(x_out, mask=over) for x_out in x_outs]
    last_in = [swap(x_in[0][:, chunks[0][1] :], mask=core)]
    last_grad = swap(x_grad, mask=core)

    state = []
    for k, (start, size) in enumerate(chunks):
        if k:
            arrived = after(x_in[k], state[k - 1][1])
            x_in[k] = arrived
            last_in.append(swap(arrived[:, size:], mask=core))
        state.append(call(
            functools.partial(weight_terms, start, size, wide_size),
            [((2, size, TILE), F32), ((2, size, TILE), BF16)],
            own_tokens, core_in, x_in[k], last_in[k], scaled, x_grad, last_grad,
        ))
    latest = state[-1][1]
    keep, send = call(
        functools.partial(projections, rows, chunks),
        [((2 * rows, KV), F32), ((2 * rows, KV), BF16)],
        gain_row, after(key_weight, latest), own_tokens, core_in, *x_in, *last_in,
    )
    got_core = swap(send, mask=core)

    count = len(chunks)
    totals = []
    got = [summed(send_half, stage=0) for _, send_half in state]
    for k in range(count):
        totals.append(state[k][0] + after(got[k], latest).astype(F32))
        latest = totals[-1]
    pair = keep + after(got_core, latest).astype(F32)
    got_x = swap(pair[rows:].astype(BF16), mask=over)
    latest = pair
    got = [summed(total[1].astype(BF16), stage=1) for total in totals]
    for k in range(count):
        totals[k] = totals[k][0] + after(got[k], latest).astype(F32)
        latest = totals[k]
    (keys,) = call(
        finish_keys, [((rows, KV), BF16)], pair[:rows], after(got_x, latest), inv_rms, cosine, sine
    )
    latest = keys
    for stage in range(2, wide_size.bit_length() - 1):
        rounded = [total.astype(BF16) for total in totals]
        got = [summed(value, stage=stage) for value in rounded]
        for k in range(count):
            totals[k] = rounded[k].astype(F32) + after(got[k], latest).astype(F32)
            latest = totals[k]
    mine = [total.astype(BF16) for total in totals]
    near = [summed(value, stage=1) for value in mine]
    both = []
    for k in range(count):
        both.append(jnp.stack([mine[k], after(near[k], latest)]))
        latest = both[-1]
    far = [summed(value, stage=0) for value in both]
    before = ()
    for k, (start, size) in enumerate(chunks):
        before = write_weights(
            start, size, wide_size, grad_scale, gain_row, key_weight,
            (mine[k], near[k], after(far[k], latest)), before,
        )
        latest = before[0]
    weight_grad, gain_grad = before
    return keys, weight_grad, gain_grad.reshape(own)


def by_groups(tokens, norm_gain, key_weight, key_grad, cosine, sine, grad_scale):
    widened = tokens.astype(F32)
    inv_rms = lax.rsqrt(jnp.mean(widened * widened, axis=1, keepdims=True) + norm_eps)
    scaled = (rotate(key_grad.astype(F32), cosine, sine, 1.0) * inv_rms).astype(BF16)
    features = lax.all_to_all(tokens, "narrow", split_axis=1, concat_axis=0, tiled=True)
    upstream = lax.all_gather(scaled, "narrow", axis=0, tiled=True)
    gain = norm_gain.astype(F32)
    terms = lax.dot_general(features, upstream, (((0,), (0,)), ((), ())), preferred_element_type=F32)
    terms = lax.psum(terms, "wide") * grad_scale
    gained = (features.astype(F32) * gain[None, :]).astype(BF16)
    product = jnp.dot(gained, key_weight, preferred_element_type=F32)
    projected = lax.psum_scatter(product, "narrow", scatter_dimension=0, tiled=True)
    keys = rotate(projected * inv_rms, cosine, sine, -1.0).astype(BF16)
    return keys, terms * gain[:, None], jnp.sum(terms * key_weight.astype(F32), axis=1)


def local(tokens, norm_gain, key_weight, key_grad):
    row_count = tokens.shape[0]
    narrow_size = lax.axis_size("narrow")
    wide_size = lax.axis_size("wide")
    first_row = (lax.axis_index("wide") * narrow_size + lax.axis_index("narrow")) * row_count
    grad_scale = 1.0 / math.sqrt(row_count * narrow_size * wide_size)
    cosine, sine = rope_tables(first_row, row_count)
    fits = narrow_size == 4 and key_weight.shape[0] == 2 * KV and row_count == TILE
    fits = fits and wide_size >= 4 and wide_size & (wide_size - 1) == 0
    way = by_permutes if fits else by_groups
    return way(tokens, norm_gain, key_weight, key_grad, cosine, sine, grad_scale)


def solution(mesh):
    return jax.shard_map(
        local,
        mesh=mesh,
        in_specs=(
            P(("wide", "narrow"), None),
            P("narrow"),
            P("narrow", None),
            P(("wide", "narrow"), None),
        ),
        out_specs=(P(("wide", "narrow"), None), P("narrow", None), P("narrow")),
        check_vma=False,
    )
```

time: 68.3 us -> 59.9 us (0.88)
  waiting for transfers between devices: 35.1 us -> 22.2 us
  starting transfers between devices: 22.7 us -> 27.9 us
  other arithmetic: 2.03 us -> 0.8 us
    ppermute x7 -> x9, waiting for transfers between devices: 19.4 us -> 8.92 us  [swap_narrow(): lax.ppermute(value, 'narrow', [(i, i ^ mask) for i in range(narrow_size)])]
    pallas_call x5 -> x8, Pallas kernels: 2.85 us -> 5.76 us  [call(): pl.pallas_call(body, out_shape=[jax.ShapeDtypeStruct(shape, kind) for sha...]
    ppermute x10, starting transfers between devices: 17.9 us -> 20.6 us  [swap_wide(): return lax.ppermute(value, BOTH, pairs)]
    ppermute x7 -> x9, starting transfers between devices: 4.77 us -> 7.37 us  [swap_narrow(): lax.ppermute(value, 'narrow', [(i, i ^ mask) for i in range(narrow_size)])]
    pallas_call x2 -> x0, Pallas kernels: 2.46 us -> none  [write_weights(): pl.pallas_call(functools.partial(finish_weights, chunk, wide_size, grad_s...]
    ppermute x10, waiting for transfers between devices: 15.7 us -> 13.2 us  [swap_wide(): return lax.ppermute(value, BOTH, pairs)]
    mul x1 -> x0, other arithmetic: 0.96 us -> none  [rope_tables(): return (jnp.cos(angle), jnp.sin(angle) * sign[None, :])]
    unnamed x8 -> x10, local copies, waits for them, and re-layouts: 2.14 us -> 2.13 us
  transfers between devices with their start and end apart: 17 -> 19, of which waited for: 11 -> 10; matrix products, arithmetic and copies ran while one was open for 1% -> 1% of each run, Pallas kernels for 5% -> 7%
where the time goes in v2:
time: 59.9 us; the launch traced here: 59.8 us
  starting transfers between devices  27.9 us (47%)
  waiting for transfers between devices  22.2 us (37%)
  Pallas kernels  5.76 us (10%)
  local copies, waits for them, and re-layouts  2.23 us (4%)
  between operations  0.88 us (1%)
  other arithmetic  0.8 us (1%)
    ppermute x10, starting transfers between devices, swap_wide(): return lax.ppermute(value, BOTH, pairs)  20.6 us
    ppermute x10, waiting for transfers between devices, swap_wide(): return lax.ppermute(value, BOTH, pairs)  13.2 us
    ppermute x9, waiting for transfers between devices, swap_narrow(): lax.ppermute(value, 'narrow', [(i, i ^ mask) for i in range(narrow_size)])  8.92 us
    ppermute x9, starting transfers between devices, swap_narrow(): lax.ppermute(value, 'narrow', [(i, i ^ mask) for i in range(narrow_size)])  7.37 us
    pallas_call x8, Pallas kernels, call(): pl.pallas_call(body, out_shape=[jax.ShapeDtypeStruct(shape, kind) for sha...  5.76 us
    unnamed x10, local copies, waits for them, and re-layouts  2.13 us
  transfers between devices with their start and end apart: 19, of which 10 were waited for; matrix products, arithmetic and copies ran while one was open for 1% of the time, Pallas kernels for 7%

profile of v2, /device:TPU:0, one launch (start us, length us, event | category | flops | bytes accessed | tf_op | source)
XLA Modules:
  0.0 59.8 jit_solution(8070393424202813930)
XLA Ops:
  0.6 1.2 %copy-done.1 = bf16[128,4096]{1,0:T(8,128)(2,1)S(1)} copy-done((bf16[128,4096]{1,0:T(8,128)(2,1)S(1)}, bf16[128,4096]{1,0:T(8,128)(2,1)}, u32[]{:S(2)}) %copy-start.1) | copy-done | bytes 1048600
  1.9 3.0 %collective-permute-start.2 = (bf16[128,1024]{1,0:T(8,128)(2,1)S(1)}, bf16[128,1024]{1,0:T(8,128)(2,1)S(1)}, u32[]{:S(2)}, u32[]{:S(2)}) collective-permute-start(bf16[128,1024]{1,0:T(8,128)(2,1)S(1)} %shard_map.67), channel_id=1, source_target_pairs={{0,2},{1,3},{2,0},{3,1},{4,6},{5,7},{6,4},{7,5},{8,10},{9,11},{10,... | collective-permute-start | bytes 786440 | tf_op jit(solution)/shard_map/ppermute | solution.py:70
  5.4 0.9 %copy-done.3 = bf16[128,512]{1,0:T(8,128)(2,1)S(1)} copy-done((bf16[128,512]{1,0:T(8,128)(2,1)S(1)}, bf16[128,512]{1,0:T(8,128)(2,1)}, u32[]{:S(2)}) %copy-start.3) | copy-done | bytes 131096
  6.7 0.7 %collective-permute-start.4 = (bf16[128,512]{1,0:T(8,128)(2,1)S(1)}, bf16[128,512]{1,0:T(8,128)(2,1)S(1)}, u32[]{:S(2)}, u32[]{:S(2)}) collective-permute-start(bf16[128,512]{1,0:T(8,128)(2,1)S(1)} %get-tuple-element.37.scaled_ref), channel_id=1, source_target_pairs={{0,2},{1,3},{2,0},{3,1},{4,6},{5,7},{6,4},{7,5},{8,10},{9,11},{10,... | collective-permute-start | bytes 393224 | tf_op jit(solution)/shard_map/ppermute | solution.py:70
  7.4 1.4 %collective-permute-start.1 = (bf16[128,1024]{1,0:T(8,128)(2,1)S(1)}, bf16[128,1024]{1,0:T(8,128)(2,1)S(1)}, u32[]{:S(2)}, u32[]{:S(2)}) collective-permute-start(bf16[128,1024]{1,0:T(8,128)(2,1)S(1)} %get-tuple-element.36), channel_id=1, source_target_pairs={{0,2},{1,3},{2,0},{3,1},{4,6},{5,7},{6,4},{7,5},{8,10},{9,11},{10,... | collective-permute-start | bytes 786440 | tf_op jit(solution)/shard_map/ppermute | solution.py:70
  8.8 6.0 %collective-permute-done.4.x_grad = bf16[128,512]{1,0:T(8,128)(2,1)S(1)} collective-permute-done((bf16[128,512]{1,0:T(8,128)(2,1)S(1)}, bf16[128,512]{1,0:T(8,128)(2,1)S(1)}, u32[]{:S(2)}, u32[]{:S(2)}) %collective-permute-start.4) | collective-permute-done | bytes 131104 | tf_op jit(solution)/shard_map/ppermute | solution.py:70
  14.9 0.6 collective-permute-start.3
  15.5 0.8 %collective-permute-done.5.last_grad = bf16[128,512]{1,0:T(8,128)(2,1)S(1)} collective-permute-done((bf16[128,512]{1,0:T(8,128)(2,1)S(1)}, bf16[128,512]{1,0:T(8,128)(2,1)S(1)}, u32[]{:S(2)}, u32[]{:S(2)}) %collective-permute-start.5) | collective-permute-done | bytes 131104 | tf_op jit(solution)/shard_map/ppermute | solution.py:70
  16.5 0.5 shard_map.69
  17.0 2.2 %collective-permute-start.9 = (bf16[2,512,128]{2,1,0:T(8,128)(2,1)S(1)}, bf16[2,512,128]{2,1,0:T(8,128)(2,1)S(1)}, u32[]{:S(2)}, u32[]{:S(2)}) collective-permute-start(bf16[2,512,128]{2,1,0:T(8,128)(2,1)S(1)} %get-tuple-element.38), channel_id=1, source_target_pairs={{0,4},{1,9},{2,6},{3,11},{4,0},{5,13},{6,2},{7,15},{8,12},{9,1},{1... | collective-permute-start | bytes 786440 | tf_op jit(solution)/shard_map/ppermute | solution.py:66
  19.1 0.6 collective-permute-done.1.x_ref.rest_1_
  19.8 1.3 %collective-permute-done.6.last_ref.rest_3_ = bf16[128,512]{1,0:T(8,128)(2,1)S(1)} collective-permute-done((bf16[128,512]{1,0:T(8,128)(2,1)S(1)}, bf16[128,512]{1,0:T(8,128)(2,1)S(1)}, u32[]{:S(2)}, u32[]{:S(2)}) %collective-permute-start.6) | collective-permute-done | bytes 131104 | tf_op jit(solution)/shard_map/ppermute | solution.py:70
  21.1 0.5 shard_map.70
  21.6 1.8 %collective-permute-start.8 = (bf16[2,512,128]{2,1,0:T(8,128)(2,1)S(1)}, bf16[2,512,128]{2,1,0:T(8,128)(2,1)S(1)}, u32[]{:S(2)}, u32[]{:S(2)}) collective-permute-start(bf16[2,512,128]{2,1,0:T(8,128)(2,1)S(1)} %get-tuple-element.40), channel_id=1, source_target_pairs={{0,4},{1,9},{2,6},{3,11},{4,0},{5,13},{6,2},{7,15},{8,12},{9,1},{1... | collective-permute-start | bytes 786440 | tf_op jit(solution)/shard_map/ppermute | solution.py:66
  23.4 0.7 %shard_map.71 = (f32[256,512]{1,0:T(8,128)S(1)}, bf16[256,512]{1,0:T(8,128)(2,1)S(1)}) custom-call(bf16[1,1024]{1,0:T(2,128)(2,1)S(1)} %reshape.35.gain_ref, bf16[1024,512]{1,0:T(8,128)(2,1)S(1)} %copy-done, bf16[128,1024]{1,0:T(8,128)(2,1)S(1)} %get-tuple-element.34.own_ref, bf16[128,1536]{1,0:T(8,128)(2,1)S(1)} %collective-permute-done.core_ref, ...), custom_call_target="tpu_custom_call" | custom-call | tf_op jit(solution)/shard_map/pallas_call | solution.py:80
  24.3 1.6 %collective-permute-start.12 = (bf16[512,128]{1,0:T(8,128)(2,1)S(1)}, bf16[512,128]{1,0:T(8,128)(2,1)S(1)}, u32[]{:S(2)}, u32[]{:S(2)}) collective-permute-start(bf16[512,128]{1,0:T(8,128)(2,1)S(1)} %fusion.3), channel_id=1, source_target_pairs={{0,8},{1,17},{2,10},{3,19},{4,12},{5,21},{6,14},{7,23},{8,0},{9,25... | collective-permute-start | bytes 393224 | tf_op jit(solution)/shard_map/ppermute | solution.py:66
  26.0 2.1 %collective-permute-done.8 = bf16[2,512,128]{2,1,0:T(8,128)(2,1)S(1)} collective-permute-done((bf16[2,512,128]{2,1,0:T(8,128)(2,1)S(1)}, bf16[2,512,128]{2,1,0:T(8,128)(2,1)S(1)}, u32[]{:S(2)}, u32[]{:S(2)}) %collective-permute-start.8) | collective-permute-done | bytes 262176 | tf_op jit(solution)/shard_map/ppermute | solution.py:66
  28.2 1.9 %collective-permute-start.11 = (bf16[512,128]{1,0:T(8,128)(2,1)S(1)}, bf16[512,128]{1,0:T(8,128)(2,1)S(1)}, u32[]{:S(2)}, u32[]{:S(2)}) collective-permute-start(bf16[512,128]{1,0:T(8,128)(2,1)S(1)} %fusion.2), channel_id=1, source_target_pairs={{0,8},{1,17},{2,10},{3,19},{4,12},{5,21},{6,14},{7,23},{8,0},{9,25... | collective-permute-start | bytes 393224 | tf_op jit(solution)/shard_map/ppermute | solution.py:66
  30.1 1.5 %collective-permute-start.10 = (bf16[128,512]{1,0:T(8,128)(2,1)S(1)}, bf16[128,512]{1,0:T(8,128)(2,1)S(1)}, u32[]{:S(2)}, u32[]{:S(2)}) collective-permute-start(bf16[128,512]{1,0:T(8,128)(2,1)S(1)} %slice.55), channel_id=1, source_target_pairs={{0,2},{1,3},{2,0},{3,1},{4,6},{5,7},{6,4},{7,5},{8,10},{9,11},{10,... | collective-permute-start | bytes 393224 | tf_op jit(solution)/shard_map/ppermute | solution.py:70
  31.7 2.7 %collective-permute-start.14 = (bf16[512,128]{1,0:T(8,128)(2,1)S(1)}, bf16[512,128]{1,0:T(8,128)(2,1)S(1)}, u32[]{:S(2)}, u32[]{:S(2)}) collective-permute-start(bf16[512,128]{1,0:T(8,128)(2,1)S(1)} %fusion), channel_id=1, source_target_pairs={{0,16},{1,5},{2,18},{3,7},{4,20},{5,1},{6,22},{7,3},{8,24},{9,13},... | collective-permute-start | bytes 393224 | tf_op jit(solution)/shard_map/ppermute | solution.py:66
  34.4 2.2 %collective-permute-start.13 = (bf16[512,128]{1,0:T(8,128)(2,1)S(1)}, bf16[512,128]{1,0:T(8,128)(2,1)S(1)}, u32[]{:S(2)}, u32[]{:S(2)}) collective-permute-start(bf16[512,128]{1,0:T(8,128)(2,1)S(1)} %fusion.1), channel_id=1, source_target_pairs={{0,16},{1,5},{2,18},{3,7},{4,20},{5,1},{6,22},{7,3},{8,24},{9,13},... | collective-permute-start | bytes 393224 | tf_op jit(solution)/shard_map/ppermute | solution.py:66
  36.6 0.8 %shard_map.72 = bf16[128,512]{1,0:T(8,128)(2,1)} custom-call(f32[128,512]{1,0:T(8,128)S(1)} %slice.36.mine_ref, bf16[128,512]{1,0:T(8,128)(2,1)S(1)} %collective-permute-done.10.got_ref, f32[128,128]{1,0:T(8,128)S(1)} %get-tuple-element.52.inv_ref, f32[128,128]{1,0:T(8,128)S(1)} %get-tuple-element.66.cos_ref, f32[128,128]{1,0:T(8,128)S(1)} %get-tuple-element.67.sin_ref), custom_call_target="tpu_custom_call" | custom-call | tf_op jit(solution)/shard_map/pallas_call | solution.py:80
  37.4 1.5 %collective-permute-done.14 = bf16[512,128]{1,0:T(8,128)(2,1)S(1)} collective-permute-done((bf16[512,128]{1,0:T(8,128)(2,1)S(1)}, bf16[512,128]{1,0:T(8,128)(2,1)S(1)}, u32[]{:S(2)}, u32[]{:S(2)}) %collective-permute-start.14) | collective-permute-done | bytes 131104 | tf_op jit(solution)/shard_map/ppermute | solution.py:66
  38.9 1.0 %collective-permute-start.16 = (bf16[512,128]{1,0:T(8,128)(2,1)S(1)}, bf16[512,128]{1,0:T(8,128)(2,1)S(1)}, u32[]{:S(2)}, u32[]{:S(2)}) collective-permute-start(bf16[512,128]{1,0:T(8,128)(2,1)S(1)} %fusion.7.mine), channel_id=1, source_target_pairs={{0,8},{1,17},{2,10},{3,19},{4,12},{5,21},{6,14},{7,23},{8,0},{9,25... | collective-permute-start | bytes 393224 | tf_op jit(solution)/shard_map/ppermute | solution.py:66
  40.0 3.9 %collective-permute-done.13 = bf16[512,128]{1,0:T(8,128)(2,1)S(1)} collective-permute-done((bf16[512,128]{1,0:T(8,128)(2,1)S(1)}, bf16[512,128]{1,0:T(8,128)(2,1)S(1)}, u32[]{:S(2)}, u32[]{:S(2)}) %collective-permute-start.13) | collective-permute-done | bytes 131104 | tf_op jit(solution)/shard_map/ppermute | solution.py:66
  43.9 2.4 %collective-permute-start.15 = (bf16[512,128]{1,0:T(8,128)(2,1)S(1)}, bf16[512,128]{1,0:T(8,128)(2,1)S(1)}, u32[]{:S(2)}, u32[]{:S(2)}) collective-permute-start(bf16[512,128]{1,0:T(8,128)(2,1)S(1)} %fusion.8.mine), channel_id=1, source_target_pairs={{0,8},{1,17},{2,10},{3,19},{4,12},{5,21},{6,14},{7,23},{8,0},{9,25... | collective-permute-start | bytes 393224 | tf_op jit(solution)/shard_map/ppermute | solution.py:66
  46.3 1.2 %collective-permute-start.18 = (bf16[2,512,128]{2,1,0:T(8,128)(2,1)S(1)}, bf16[2,512,128]{2,1,0:T(8,128)(2,1)S(1)}, u32[]{:S(2)}, u32[]{:S(2)}) collective-permute-start(bf16[2,512,128]{2,1,0:T(8,128)(2,1)S(1)} %pad_maximum_fusion), channel_id=1, source_target_pairs={{0,4},{1,9},{2,6},{3,11},{4,0},{5,13},{6,2},{7,15},{8,12},{9,1},{1... | collective-permute-start | bytes 786440 | tf_op jit(solution)/shard_map/ppermute | solution.py:66
  47.5 2.6 %collective-permute-done.15.near = bf16[512,128]{1,0:T(8,128)(2,1)S(1)} collective-permute-done((bf16[512,128]{1,0:T(8,128)(2,1)S(1)}, bf16[512,128]{1,0:T(8,128)(2,1)S(1)}, u32[]{:S(2)}, u32[]{:S(2)}) %collective-permute-start.15) | collective-permute-done | bytes 131104 | tf_op jit(solution)/shard_map/ppermute | solution.py:66
  50.2 3.5 %collective-permute-start.17 = (bf16[2,512,128]{2,1,0:T(8,128)(2,1)S(1)}, bf16[2,512,128]{2,1,0:T(8,128)(2,1)S(1)}, u32[]{:S(2)}, u32[]{:S(2)}) collective-permute-start(bf16[2,512,128]{2,1,0:T(8,128)(2,1)S(1)} %pad_maximum_fusion.1), channel_id=1, source_target_pairs={{0,4},{1,9},{2,6},{3,11},{4,0},{5,13},{6,2},{7,15},{8,12},{9,1},{1... | collective-permute-start | bytes 786440 | tf_op jit(solution)/shard_map/ppermute | solution.py:66
  53.7 1.2 %shard_map.73 = (f32[1024,512]{1,0:T(8,128)}, f32[8,128]{1,0:T(8,128)S(1)}) custom-call(bf16[1,1024]{1,0:T(2,128)(2,1)S(1)} %reshape.35.gain_ref, bf16[1024,512]{1,0:T(8,128)(2,1)S(1)} %copy-done, bf16[512,128]{1,0:T(8,128)(2,1)S(1)} %fusion.7.mine, bf16[512,128]{1,0:T(8,128)(2,1)S(1)} %collective-permute-done.16.near, ...), custom_call_target="tpu_custom_call" | custom-call | tf_op jit(solution)/shard_map/pallas_call | solution.py:80
  54.8 3.2 %collective-permute-done.17.far = bf16[2,512,128]{2,1,0:T(8,128)(2,1)S(1)} collective-permute-done((bf16[2,512,128]{2,1,0:T(8,128)(2,1)S(1)}, bf16[2,512,128]{2,1,0:T(8,128)(2,1)S(1)}, u32[]{:S(2)}, u32[]{:S(2)}) %collective-permute-start.17) | collective-permute-done | bytes 262176 | tf_op jit(solution)/shard_map/ppermute | solution.py:66
  58.0 1.7 %shard_map.74 = (f32[1024,512]{1,0:T(8,128)}, f32[8,128]{1,0:T(8,128)}) custom-call(bf16[1,1024]{1,0:T(2,128)(2,1)S(1)} %reshape.35.gain_ref, bf16[1024,512]{1,0:T(8,128)(2,1)S(1)} %copy-done, bf16[512,128]{1,0:T(8,128)(2,1)S(1)} %fusion.8.mine, bf16[512,128]{1,0:T(8,128)(2,1)S(1)} %collective-permute-done.15.near, ...), custom_call_target="tpu_custom_call", output_to_operand_aliasing={{0}: (5, {})} | custom-call | tf_op jit(solution)/shard_map/pallas_call | solution.py:80
  (44 shorter events, 1.8 us)
Async XLA Ops:
  0.6 1.2 %copy-start.1 = (bf16[128,4096]{1,0:T(8,128)(2,1)S(1)}, bf16[128,4096]{1,0:T(8,128)(2,1)}, u32[]{:S(2)}) copy-start(bf16[128,4096]{1,0:T(8,128)(2,1)} %tok_ref.2) | copy-start | bytes 3145732
  1.9 3.5 %copy-start.2 = (bf16[128,4096]{1,0:T(8,128)(2,1)S(1)}, bf16[128,4096]{1,0:T(8,128)(2,1)}, u32[]{:S(2)}) copy-start(bf16[128,4096]{1,0:T(8,128)(2,1)} %tok_ref.2) | copy-start | bytes 3145732
  1.9 17.8 %copy-start.4 = (bf16[1024]{0:T(1024)(128)(2,1)S(1)}, bf16[1024]{0:T(1024)(128)(2,1)}, u32[]{:S(2)}) copy-start(bf16[1024]{0:T(1024)(128)(2,1)} %param.5) | copy-start | bytes 6148
  1.9 13.0 %collective-permute-start.2 = (bf16[128,1024]{1,0:T(8,128)(2,1)S(1)}, bf16[128,1024]{1,0:T(8,128)(2,1)S(1)}, u32[]{:S(2)}, u32[]{:S(2)}) collective-permute-start(bf16[128,1024]{1,0:T(8,128)(2,1)S(1)} %shard_map.67), channel_id=1, source_target_pairs={{0,2},{1,3},{2,0},{3,1},{4,6},{5,7},{6,4},{7,5},{8,10},{9,11},{10,... | collective-permute-start | bytes 786440 | tf_op jit(solution)/shard_map/ppermute | solution.py:70
  5.4 0.9 %copy-start.3 = (bf16[128,512]{1,0:T(8,128)(2,1)S(1)}, bf16[128,512]{1,0:T(8,128)(2,1)}, u32[]{:S(2)}) copy-start(bf16[128,512]{1,0:T(8,128)(2,1)} %grad_ref.1) | copy-start | bytes 393220
  6.3 17.1 %copy-start = (bf16[1024,512]{1,0:T(8,128)(2,1)S(1)}, bf16[1024,512]{1,0:T(8,128)(2,1)}, u32[]{:S(2)}) copy-start(bf16[1024,512]{1,0:T(8,128)(2,1)} %weight_ref.4) | copy-start | bytes 3145732
  6.7 9.8 %collective-permute-start = (bf16[128,1536]{1,0:T(8,128)(2,1)S(1)}, bf16[128,1536]{1,0:T(8,128)(2,1)S(1)}, u32[]{:S(2)}, u32[]{:S(2)}) collective-permute-start(bf16[128,1536]{1,0:T(8,128)(2,1)S(1)} %get-tuple-element.35), channel_id=1, source_target_pairs={{0,1},{1,0},{2,3},{3,2},{4,5},{5,4},{6,7},{7,6},{8,9},{9,8},{10,11... | collective-permute-start | bytes 1179656 | tf_op jit(solution)/shard_map/ppermute | solution.py:70
  6.7 8.1 %collective-permute-start.4 = (bf16[128,512]{1,0:T(8,128)(2,1)S(1)}, bf16[128,512]{1,0:T(8,128)(2,1)S(1)}, u32[]{:S(2)}, u32[]{:S(2)}) collective-permute-start(bf16[128,512]{1,0:T(8,128)(2,1)S(1)} %get-tuple-element.37.scaled_ref), channel_id=1, source_target_pairs={{0,2},{1,3},{2,0},{3,1},{4,6},{5,7},{6,4},{7,5},{8,10},{9,11},{10,... | collective-permute-start | bytes 393224 | tf_op jit(solution)/shard_map/ppermute | solution.py:70
  7.4 12.3 %collective-permute-start.1 = (bf16[128,1024]{1,0:T(8,128)(2,1)S(1)}, bf16[128,1024]{1,0:T(8,128)(2,1)S(1)}, u32[]{:S(2)}, u32[]{:S(2)}) collective-permute-start(bf16[128,1024]{1,0:T(8,128)(2,1)S(1)} %get-tuple-element.36), channel_id=1, source_target_pairs={{0,2},{1,3},{2,0},{3,1},{4,6},{5,7},{6,4},{7,5},{8,10},{9,11},{10,... | collective-permute-start | bytes 786440 | tf_op jit(solution)/shard_map/ppermute | solution.py:70
  14.9 1.3 %collective-permute-start.5 = (bf16[128,512]{1,0:T(8,128)(2,1)S(1)}, bf16[128,512]{1,0:T(8,128)(2,1)S(1)}, u32[]{:S(2)}, u32[]{:S(2)}) collective-permute-start(bf16[128,512]{1,0:T(8,128)(2,1)S(1)} %collective-permute-done.4.x_grad), channel_id=1, source_target_pairs={{0,1},{1,0},{2,3},{3,2},{4,5},{5,4},{6,7},{7,6},{8,9},{9,8},{10,11... | collective-permute-start | bytes 393224 | tf_op jit(solution)/shard_map/ppermute | solution.py:70
  14.9 1.6 %collective-permute-start.3 = (bf16[128,512]{1,0:T(8,128)(2,1)S(1)}, bf16[128,512]{1,0:T(8,128)(2,1)S(1)}, u32[]{:S(2)}, u32[]{:S(2)}) collective-permute-start(bf16[128,512]{1,0:T(8,128)(2,1)S(1)} %slice.35), channel_id=1, source_target_pairs={{0,1},{1,0},{2,3},{3,2},{4,5},{5,4},{6,7},{7,6},{8,9},{9,8},{10,11... | collective-permute-start | bytes 393224 | tf_op jit(solution)/shard_map/ppermute | solution.py:70
  17.0 7.3 %collective-permute-start.9 = (bf16[2,512,128]{2,1,0:T(8,128)(2,1)S(1)}, bf16[2,512,128]{2,1,0:T(8,128)(2,1)S(1)}, u32[]{:S(2)}, u32[]{:S(2)}) collective-permute-start(bf16[2,512,128]{2,1,0:T(8,128)(2,1)S(1)} %get-tuple-element.38), channel_id=1, source_target_pairs={{0,4},{1,9},{2,6},{3,11},{4,0},{5,13},{6,2},{7,15},{8,12},{9,1},{1... | collective-permute-start | bytes 786440 | tf_op jit(solution)/shard_map/ppermute | solution.py:66
  19.7 1.4 %collective-permute-start.6 = (bf16[128,512]{1,0:T(8,128)(2,1)S(1)}, bf16[128,512]{1,0:T(8,128)(2,1)S(1)}, u32[]{:S(2)}, u32[]{:S(2)}) collective-permute-start(bf16[128,512]{1,0:T(8,128)(2,1)S(1)} %slice.28), channel_id=1, source_target_pairs={{0,1},{1,0},{2,3},{3,2},{4,5},{5,4},{6,7},{7,6},{8,9},{9,8},{10,11... | collective-permute-start | bytes 393224 | tf_op jit(solution)/shard_map/ppermute | solution.py:70
  21.6 6.4 %collective-permute-start.8 = (bf16[2,512,128]{2,1,0:T(8,128)(2,1)S(1)}, bf16[2,512,128]{2,1,0:T(8,128)(2,1)S(1)}, u32[]{:S(2)}, u32[]{:S(2)}) collective-permute-start(bf16[2,512,128]{2,1,0:T(8,128)(2,1)S(1)} %get-tuple-element.40), channel_id=1, source_target_pairs={{0,4},{1,9},{2,6},{3,11},{4,0},{5,13},{6,2},{7,15},{8,12},{9,1},{1... | collective-permute-start | bytes 786440 | tf_op jit(solution)/shard_map/ppermute | solution.py:66
  24.1 3.9 %collective-permute-start.7 = (bf16[256,512]{1,0:T(8,128)(2,1)S(1)}, bf16[256,512]{1,0:T(8,128)(2,1)S(1)}, u32[]{:S(2)}, u32[]{:S(2)}) collective-permute-start(bf16[256,512]{1,0:T(8,128)(2,1)S(1)} %get-tuple-element.43), channel_id=1, source_target_pairs={{0,1},{1,0},{2,3},{3,2},{4,5},{5,4},{6,7},{7,6},{8,9},{9,8},{10,11... | collective-permute-start | bytes 786440 | tf_op jit(solution)/shard_map/ppermute | solution.py:70
  24.3 7.3 %collective-permute-start.12 = (bf16[512,128]{1,0:T(8,128)(2,1)S(1)}, bf16[512,128]{1,0:T(8,128)(2,1)S(1)}, u32[]{:S(2)}, u32[]{:S(2)}) collective-permute-start(bf16[512,128]{1,0:T(8,128)(2,1)S(1)} %fusion.3), channel_id=1, source_target_pairs={{0,8},{1,17},{2,10},{3,19},{4,12},{5,21},{6,14},{7,23},{8,0},{9,25... | collective-permute-start | bytes 393224 | tf_op jit(solution)/shard_map/ppermute | solution.py:66
  28.2 6.1 %collective-permute-start.11 = (bf16[512,128]{1,0:T(8,128)(2,1)S(1)}, bf16[512,128]{1,0:T(8,128)(2,1)S(1)}, u32[]{:S(2)}, u32[]{:S(2)}) collective-permute-start(bf16[512,128]{1,0:T(8,128)(2,1)S(1)} %fusion.2), channel_id=1, source_target_pairs={{0,8},{1,17},{2,10},{3,19},{4,12},{5,21},{6,14},{7,23},{8,0},{9,25... | collective-permute-start | bytes 393224 | tf_op jit(solution)/shard_map/ppermute | solution.py:66
  30.1 6.4 %collective-permute-start.10 = (bf16[128,512]{1,0:T(8,128)(2,1)S(1)}, bf16[128,512]{1,0:T(8,128)(2,1)S(1)}, u32[]{:S(2)}, u32[]{:S(2)}) collective-permute-start(bf16[128,512]{1,0:T(8,128)(2,1)S(1)} %slice.55), channel_id=1, source_target_pairs={{0,2},{1,3},{2,0},{3,1},{4,6},{5,7},{6,4},{7,5},{8,10},{9,11},{10,... | collective-permute-start | bytes 393224 | tf_op jit(solution)/shard_map/ppermute | solution.py:70
  31.7 7.2 %collective-permute-start.14 = (bf16[512,128]{1,0:T(8,128)(2,1)S(1)}, bf16[512,128]{1,0:T(8,128)(2,1)S(1)}, u32[]{:S(2)}, u32[]{:S(2)}) collective-permute-start(bf16[512,128]{1,0:T(8,128)(2,1)S(1)} %fusion), channel_id=1, source_target_pairs={{0,16},{1,5},{2,18},{3,7},{4,20},{5,1},{6,22},{7,3},{8,24},{9,13},... | collective-permute-start | bytes 393224 | tf_op jit(solution)/shard_map/ppermute | solution.py:66
  34.4 9.5 %collective-permute-start.13 = (bf16[512,128]{1,0:T(8,128)(2,1)S(1)}, bf16[512,128]{1,0:T(8,128)(2,1)S(1)}, u32[]{:S(2)}, u32[]{:S(2)}) collective-permute-start(bf16[512,128]{1,0:T(8,128)(2,1)S(1)} %fusion.1), channel_id=1, source_target_pairs={{0,16},{1,5},{2,18},{3,7},{4,20},{5,1},{6,22},{7,3},{8,24},{9,13},... | collective-permute-start | bytes 393224 | tf_op jit(solution)/shard_map/ppermute | solution.py:66
  38.9 7.3 %collective-permute-start.16 = (bf16[512,128]{1,0:T(8,128)(2,1)S(1)}, bf16[512,128]{1,0:T(8,128)(2,1)S(1)}, u32[]{:S(2)}, u32[]{:S(2)}) collective-permute-start(bf16[512,128]{1,0:T(8,128)(2,1)S(1)} %fusion.7.mine), channel_id=1, source_target_pairs={{0,8},{1,17},{2,10},{3,19},{4,12},{5,21},{6,14},{7,23},{8,0},{9,25... | collective-permute-start | bytes 393224 | tf_op jit(solution)/shard_map/ppermute | solution.py:66
  43.9 6.3 %collective-permute-start.15 = (bf16[512,128]{1,0:T(8,128)(2,1)S(1)}, bf16[512,128]{1,0:T(8,128)(2,1)S(1)}, u32[]{:S(2)}, u32[]{:S(2)}) collective-permute-start(bf16[512,128]{1,0:T(8,128)(2,1)S(1)} %fusion.8.mine), channel_id=1, source_target_pairs={{0,8},{1,17},{2,10},{3,19},{4,12},{5,21},{6,14},{7,23},{8,0},{9,25... | collective-permute-start | bytes 393224 | tf_op jit(solution)/shard_map/ppermute | solution.py:66
  46.3 7.4 %collective-permute-start.18 = (bf16[2,512,128]{2,1,0:T(8,128)(2,1)S(1)}, bf16[2,512,128]{2,1,0:T(8,128)(2,1)S(1)}, u32[]{:S(2)}, u32[]{:S(2)}) collective-permute-start(bf16[2,512,128]{2,1,0:T(8,128)(2,1)S(1)} %pad_maximum_fusion), channel_id=1, source_target_pairs={{0,4},{1,9},{2,6},{3,11},{4,0},{5,13},{6,2},{7,15},{8,12},{9,1},{1... | collective-permute-start | bytes 786440 | tf_op jit(solution)/shard_map/ppermute | solution.py:66
  50.2 7.9 %collective-permute-start.17 = (bf16[2,512,128]{2,1,0:T(8,128)(2,1)S(1)}, bf16[2,512,128]{2,1,0:T(8,128)(2,1)S(1)}, u32[]{:S(2)}, u32[]{:S(2)}) collective-permute-start(bf16[2,512,128]{2,1,0:T(8,128)(2,1)S(1)} %pad_maximum_fusion.1), channel_id=1, source_target_pairs={{0,4},{1,9},{2,6},{3,11},{4,0},{5,13},{6,2},{7,15},{8,12},{9,1},{1... | collective-permute-start | bytes 786440 | tf_op jit(solution)/shard_map/ppermute | solution.py:66

commit v3 on v2

--- a/solution.py
+++ b/solution.py
@@ -21,6 +21,7 @@
 F32 = jnp.float32
 BOTH = ("wide", "narrow")
 CHUNKS = (4, 4)
+ORDERS = (((1, 2, 0), (0, 1, 2)), ((0, 1, 2), (1, 0, 2)))
 
 
 def rope_tables(first_row, row_count):
@@ -43,25 +44,26 @@
     )
 
 
-def stage_bits(wide_size):
+def stage_bits(wide_size, chunk, core):
     bits = wide_size.bit_length() - 1
-    first = list(range(bits))
-    second = first[1:] + first[:1]
-    return first, second
-
-
-def place(wide_size, stage):
-    first, second = stage_bits(wide_size)
+    order = ORDERS[chunk][core]
+    return order if len(order) == bits else tuple(range(bits))
+
+
+def place(wide_size, chunk, stage):
     wide, core = lax.axis_index("wide"), lax.axis_index("narrow") & 1
-    return lax.select(core == 0, (wide >> first[stage]) & 1, (wide >> second[stage]) & 1)
-
-
-def swap_wide(value, wide_size, narrow_size, stage):
-    first, second = stage_bits(wide_size)
+    return lax.select(
+        core == 0,
+        (wide >> stage_bits(wide_size, chunk, 0)[stage]) & 1,
+        (wide >> stage_bits(wide_size, chunk, 1)[stage]) & 1,
+    )
+
+
+def swap_wide(value, wide_size, narrow_size, chunk, stage):
     pairs = []
     for wide in range(wide_size):
         for narrow in range(narrow_size):
-            bit = (second if narrow & 1 else first)[stage]
+            bit = stage_bits(wide_size, chunk, narrow & 1)[stage]
             pairs.append((wide * narrow_size + narrow, (wide ^ (1 << bit)) * narrow_size + narrow))
     return lax.ppermute(value, BOTH, pairs)
 
@@ -76,7 +78,7 @@
 
 def call(body, outs, *operands, scratch=(), anywhere=(), **more):
     whole = pl.BlockSpec(memory_space=pltpu.VMEM)
-    far = pl.BlockSpec(memory_space=pl.ANY)
+    far = pl.BlockSpec(memory_space=pltpu.HBM)
     return pl.pallas_call(
         body,
         out_shape=[jax.ShapeDtypeStruct(shape, kind) for shape, kind, *_ in outs],
@@ -139,17 +141,17 @@
     )
 
 
-def quarters(wide_size):
-    first, second = place(wide_size, 0), place(wide_size, 1)
+def quarters(wide_size, chunk):
+    first, second = place(wide_size, chunk, 0), place(wide_size, chunk, 1)
     return [
         pl.multiple_of(((first ^ a) * 2 + (second ^ b)) * TILE, TILE) for a in (0, 1) for b in (0, 1)
     ]
 
 
-def weight_terms(start, size, wide_size, own_ref, core_ref, x_ref, last_ref, scaled_ref, x_grad, last_grad, keep, send):
+def weight_terms(start, size, chunk, wide_size, own_ref, core_ref, x_ref, last_ref, scaled_ref, x_grad, last_grad, keep, send):
     tokens = tokens_of(start, size, own_ref, core_ref, x_ref, last_ref)
     columns = [
-        jnp.concatenate([ref[:, pl.ds(at, TILE)] for at in quarters(wide_size)], axis=1)
+        jnp.concatenate([ref[:, pl.ds(at, TILE)] for at in quarters(wide_size, chunk)], axis=1)
         for ref in (scaled_ref, x_grad, core_ref, last_grad)
     ]
     terms = lax.dot_general(
@@ -181,42 +183,55 @@
     keys[...] = rotate(projected, cos_ref[...], sin_ref[...], -1.0).astype(BF16)
 
 
-def finish_weights(start, size, wide_size, grad_scale, gain_ref, weight_ref, mine, near, far, *rest):
-    gain_before = rest[1] if len(rest) > 5 else None
-    out, gain_out, held, sent = rest[-4:]
-    if gain_before is not None:
-        gain_out[...] = gain_before[...]
+def finish_weights(start, size, chunk, wide_size, grad_scale, half, last, gain_ref, weight_ref, *rest):
+    out, gain_out, held, gains, sent = rest[-5:]
+    sources = [rest[0], rest[1]] if half == 0 else [rest[0].at[0], rest[0].at[1]]
+    before = rest[-6] if len(rest) > 5 + 2 - half else None
+    gains[...] = jnp.zeros_like(gains) if before is None else before[...]
+    places = quarters(wide_size, chunk)[2 * half : 2 * half + 2]
     copies = []
     for row in range(0, size, TILE):
-        rows = slice(row, row + TILE)
-        gain = gain_ref[0:1, start + row : start + row + TILE].astype(F32) * grad_scale
+        rows, here = slice(row, row + TILE), slice(start + row, start + row + TILE)
+        gain = gain_ref[0:1, here].astype(F32) * grad_scale
         column = jnp.broadcast_to(gain, (TILE, TILE)).T
         folded = jnp.zeros((TILE, TILE), F32)
-        for part, at in enumerate(quarters(wide_size)):
-            source = (mine[rows], near[rows], far[0, rows], far[1, rows])[part].astype(F32)
-            weight = weight_ref[start + row : start + row + TILE, pl.ds(at, TILE)].astype(F32)
-            folded = folded + source * weight
-            held[rows, pl.ds(at, TILE)] = source * column
-        copy = pltpu.make_async_copy(
-            held.at[rows], out.at[start + row : start + row + TILE], sent.at[row // TILE]
+        for part, (source, at) in enumerate(zip(sources, places, strict=True)):
+            terms = source[rows].astype(F32)
+            folded = folded + terms * weight_ref[here, pl.ds(at, TILE)].astype(F32)
+            held[part, rows] = terms * column
+        line = (start + row) // TILE
+        gains[line : line + 1] += jnp.sum(folded.T, axis=0, keepdims=True) * grad_scale
+    for part, at in enumerate(places):
+        copies.append(
+            pltpu.make_async_copy(
+                held.at[part], out.at[start : start + size, pl.ds(at, TILE)], sent.at[part]
+            )
         )
+    if last:
+        copies.append(pltpu.make_async_copy(gains, gain_out, sent.at[2]))
+    else:
+        gain_out[...] = gains[...]
+    for copy in copies:
         copy.start()
-        copies.append(copy)
-        at = (start + row) // TILE
-        gain_out[at : at + 1] = jnp.sum(folded.T, axis=0, keepdims=True) * grad_scale
     for copy in copies:
         copy.wait()
 
 
-def write_weights(start, size, wide_size, grad_scale, gain_row, key_weight, parts, before):
+def write_weights(start, size, chunk, wide_size, grad_scale, half, last, gain_row, key_weight, parts, before):
     own = key_weight.shape[0]
+    at = 2 + len(parts)
+    gain_kind = ((own // TILE, TILE), F32)
     return call(
-        functools.partial(finish_weights, start, size, wide_size, grad_scale),
-        [((own, KV), F32, "far"), ((own // TILE, TILE), F32)],
+        functools.partial(finish_weights, start, size, chunk, wide_size, grad_scale, half, last),
+        [((own, KV), F32, "far"), (*gain_kind, "far") if last else gain_kind],
         gain_row, key_weight, *parts, *before,
-        anywhere=(5,),
-        scratch=[pltpu.VMEM((size, KV), F32), pltpu.SemaphoreType.DMA((size // TILE,))],
-        input_output_aliases={5: 0} if before else {},
+        anywhere=(at,),
+        scratch=[
+            pltpu.VMEM((2, size, TILE), F32),
+            pltpu.VMEM(*gain_kind),
+            pltpu.SemaphoreType.DMA((3,)),
+        ],
+        input_output_aliases={at: 0} if before else {},
     )
 
 
@@ -264,7 +279,7 @@
             x_in[k] = arrived
             last_in.append(swap(arrived[:, size:], mask=core))
         state.append(call(
-            functools.partial(weight_terms, start, size, wide_size),
+            functools.partial(weight_terms, start, size, k, wide_size),
             [((2, size, TILE), F32), ((2, size, TILE), BF16)],
             own_tokens, core_in, x_in[k], last_in[k], scaled, x_grad, last_grad,
         ))
@@ -278,14 +293,14 @@
 
     count = len(chunks)
     totals = []
-    got = [summed(send_half, stage=0) for _, send_half in state]
+    got = [summed(send_half, chunk=k, stage=0) for k, (_, send_half) in enumerate(state)]
     for k in range(count):
         totals.append(state[k][0] + after(got[k], latest).astype(F32))
         latest = totals[-1]
     pair = keep + after(got_core, latest).astype(F32)
     got_x = swap(pair[rows:].astype(BF16), mask=over)
     latest = pair
-    got = [summed(total[1].astype(BF16), stage=1) for total in totals]
+    got = [summed(total[1].astype(BF16), chunk=k, stage=1) for k, total in enumerate(totals)]
     for k in range(count):
         totals[k] = totals[k][0] + after(got[k], latest).astype(F32)
         latest = totals[k]
@@ -295,24 +310,26 @@
     latest = keys
     for stage in range(2, wide_size.bit_length() - 1):
         rounded = [total.astype(BF16) for total in totals]
-        got = [summed(value, stage=stage) for value in rounded]
+        got = [summed(value, chunk=k, stage=stage) for k, value in enumerate(rounded)]
         for k in range(count):
             totals[k] = rounded[k].astype(F32) + after(got[k], latest).astype(F32)
             latest = totals[k]
     mine = [total.astype(BF16) for total in totals]
-    near = [summed(value, stage=1) for value in mine]
+    near = [summed(value, chunk=k, stage=1) for k, value in enumerate(mine)]
     both = []
     for k in range(count):
         both.append(jnp.stack([mine[k], after(near[k], latest)]))
         latest = both[-1]
-    far = [summed(value, stage=0) for value in both]
+    far = [summed(value, chunk=k, stage=0) for k, value in enumerate(both)]
     before = ()
-    for k, (start, size) in enumerate(chunks):
-        before = write_weights(
-            start, size, wide_size, grad_scale, gain_row, key_weight,
-            (mine[k], near[k], after(far[k], latest)), before,
-        )
-        latest = before[0]
+    for half in range(2):
+        for k, (start, size) in enumerate(chunks):
+            parts = (after(far[k], latest),) if half else (both[k][0], both[k][1])
+            before = write_weights(
+                start, size, k, wide_size, grad_scale, half, half == 1 and k == count - 1,
+                gain_row, key_weight, parts, before,
+            )
+            latest = before[1]
     weight_grad, gain_grad = before
     return keys, weight_grad, gain_grad.reshape(own)
 

time: 59.9 us -> 56.7 us (0.947)
  waiting for transfers between devices: 22.2 us -> 19.4 us
  starting transfers between devices: 27.9 us -> 26.2 us
  Pallas kernels: 5.76 us -> 7.05 us
    ppermute x10, waiting for transfers between devices: 13.2 us -> 10.5 us  [swap_wide(): return lax.ppermute(value, BOTH, pairs)]
    ppermute x10, starting transfers between devices: 20.6 us -> 18.8 us  [swap_wide(): return lax.ppermute(value, BOTH, pairs)]
    pallas_call x8 -> x10, Pallas kernels: 5.76 us -> 7.05 us  [call(): pl.pallas_call(body, out_shape=[jax.ShapeDtypeStruct(shape, kind) for sha...]
  transfers between devices with their start and end apart: 19 -> 19, of which waited for: 10 -> 10; matrix products, arithmetic and copies ran while one was open for 1% -> 2% of each run, Pallas kernels for 7% -> 11%
where the time goes in v3:
time: 56.7 us; the launch traced here: 56.5 us
  starting transfers between devices  26.2 us (46%)
  waiting for transfers between devices  19.4 us (34%)
  Pallas kernels  7.05 us (12%)
  local copies, waits for them, and re-layouts  2.23 us (4%)
  between operations  0.9 us (2%)
  other arithmetic  0.8 us (1%)
    ppermute x10, starting transfers between devices, swap_wide(): return lax.ppermute(value, BOTH, pairs)  18.8 us
    ppermute x10, waiting for transfers between devices, swap_wide(): return lax.ppermute(value, BOTH, pairs)  10.5 us
    ppermute x9, waiting for transfers between devices, swap_narrow(): lax.ppermute(value, 'narrow', [(i, i ^ mask) for i in range(narrow_size)])  8.87 us
    ppermute x9, starting transfers between devices, swap_narrow(): lax.ppermute(value, 'narrow', [(i, i ^ mask) for i in range(narrow_size)])  7.38 us
    pallas_call x10, Pallas kernels, call(): pl.pallas_call(body, out_shape=[jax.ShapeDtypeStruct(shape, kind) for sha...  7.05 us
    unnamed x10, local copies, waits for them, and re-layouts  2.13 us
  transfers between devices with their start and end apart: 19, of which 10 were waited for; matrix products, arithmetic and copies ran while one was open for 2% of the time, Pallas kernels for 11%

profile of v3, /device:TPU:0, one launch (start us, length us, event | category | flops | bytes accessed | tf_op | source)
XLA Modules:
  0.0 56.5 jit_solution(13783889853263311877)
XLA Ops:
  0.6 1.2 %copy-done.1 = bf16[128,4096]{1,0:T(8,128)(2,1)S(1)} copy-done((bf16[128,4096]{1,0:T(8,128)(2,1)S(1)}, bf16[128,4096]{1,0:T(8,128)(2,1)}, u32[]{:S(2)}) %copy-start.1) | copy-done | bytes 1048600
  1.9 3.0 %collective-permute-start.2 = (bf16[128,1024]{1,0:T(8,128)(2,1)S(1)}, bf16[128,1024]{1,0:T(8,128)(2,1)S(1)}, u32[]{:S(2)}, u32[]{:S(2)}) collective-permute-start(bf16[128,1024]{1,0:T(8,128)(2,1)S(1)} %shard_map.67), channel_id=1, source_target_pairs={{0,2},{1,3},{2,0},{3,1},{4,6},{5,7},{6,4},{7,5},{8,10},{9,11},{10,... | collective-permute-start | bytes 786440 | tf_op jit(solution)/shard_map/ppermute | solution.py:72
  5.4 0.9 %copy-done.3 = bf16[128,512]{1,0:T(8,128)(2,1)S(1)} copy-done((bf16[128,512]{1,0:T(8,128)(2,1)S(1)}, bf16[128,512]{1,0:T(8,128)(2,1)}, u32[]{:S(2)}) %copy-start.3) | copy-done | bytes 131096
  6.7 0.7 %collective-permute-start.4 = (bf16[128,512]{1,0:T(8,128)(2,1)S(1)}, bf16[128,512]{1,0:T(8,128)(2,1)S(1)}, u32[]{:S(2)}, u32[]{:S(2)}) collective-permute-start(bf16[128,512]{1,0:T(8,128)(2,1)S(1)} %get-tuple-element.41.scaled_ref), channel_id=1, source_target_pairs={{0,2},{1,3},{2,0},{3,1},{4,6},{5,7},{6,4},{7,5},{8,10},{9,11},{10,... | collective-permute-start | bytes 393224 | tf_op jit(solution)/shard_map/ppermute | solution.py:72
  7.4 1.4 %collective-permute-start.1 = (bf16[128,1024]{1,0:T(8,128)(2,1)S(1)}, bf16[128,1024]{1,0:T(8,128)(2,1)S(1)}, u32[]{:S(2)}, u32[]{:S(2)}) collective-permute-start(bf16[128,1024]{1,0:T(8,128)(2,1)S(1)} %get-tuple-element.40), channel_id=1, source_target_pairs={{0,2},{1,3},{2,0},{3,1},{4,6},{5,7},{6,4},{7,5},{8,10},{9,11},{10,... | collective-permute-start | bytes 786440 | tf_op jit(solution)/shard_map/ppermute | solution.py:72
  8.8 6.0 %collective-permute-done.4.x_grad = bf16[128,512]{1,0:T(8,128)(2,1)S(1)} collective-permute-done((bf16[128,512]{1,0:T(8,128)(2,1)S(1)}, bf16[128,512]{1,0:T(8,128)(2,1)S(1)}, u32[]{:S(2)}, u32[]{:S(2)}) %collective-permute-start.4) | collective-permute-done | bytes 131104 | tf_op jit(solution)/shard_map/ppermute | solution.py:72
  14.9 0.6 %collective-permute-start.3 = (bf16[128,512]{1,0:T(8,128)(2,1)S(1)}, bf16[128,512]{1,0:T(8,128)(2,1)S(1)}, u32[]{:S(2)}, u32[]{:S(2)}) collective-permute-start(bf16[128,512]{1,0:T(8,128)(2,1)S(1)} %slice.35), channel_id=1, source_target_pairs={{0,1},{1,0},{2,3},{3,2},{4,5},{5,4},{6,7},{7,6},{8,9},{9,8},{10,11... | collective-permute-start | bytes 393224 | tf_op jit(solution)/shard_map/ppermute | solution.py:72
  15.5 0.8 %collective-permute-done.5.last_grad = bf16[128,512]{1,0:T(8,128)(2,1)S(1)} collective-permute-done((bf16[128,512]{1,0:T(8,128)(2,1)S(1)}, bf16[128,512]{1,0:T(8,128)(2,1)S(1)}, u32[]{:S(2)}, u32[]{:S(2)}) %collective-permute-start.5) | collective-permute-done | bytes 131104 | tf_op jit(solution)/shard_map/ppermute | solution.py:72
  17.0 2.2 %collective-permute-start.9 = (bf16[2,512,128]{2,1,0:T(8,128)(2,1)S(1)}, bf16[2,512,128]{2,1,0:T(8,128)(2,1)S(1)}, u32[]{:S(2)}, u32[]{:S(2)}) collective-permute-start(bf16[2,512,128]{2,1,0:T(8,128)(2,1)S(1)} %get-tuple-element.42), channel_id=1, source_target_pairs={{0,8},{1,5},{2,10},{3,7},{4,12},{5,1},{6,14},{7,3},{8,0},{9,13},{1... | collective-permute-start | bytes 786440 | tf_op jit(solution)/shard_map/ppermute | solution.py:68
  19.2 0.5 collective-permute-done.1.x_ref.rest_1_
  19.8 1.3 %collective-permute-done.6.last_ref.rest_3_ = bf16[128,512]{1,0:T(8,128)(2,1)S(1)} collective-permute-done((bf16[128,512]{1,0:T(8,128)(2,1)S(1)}, bf16[128,512]{1,0:T(8,128)(2,1)S(1)}, u32[]{:S(2)}, u32[]{:S(2)}) %collective-permute-start.6) | collective-permute-done | bytes 131104 | tf_op jit(solution)/shard_map/ppermute | solution.py:72
  21.6 1.8 %collective-permute-start.8 = (bf16[2,512,128]{2,1,0:T(8,128)(2,1)S(1)}, bf16[2,512,128]{2,1,0:T(8,128)(2,1)S(1)}, u32[]{:S(2)}, u32[]{:S(2)}) collective-permute-start(bf16[2,512,128]{2,1,0:T(8,128)(2,1)S(1)} %get-tuple-element.44), channel_id=1, source_target_pairs={{0,4},{1,9},{2,6},{3,11},{4,0},{5,13},{6,2},{7,15},{8,12},{9,1},{1... | collective-permute-start | bytes 786440 | tf_op jit(solution)/shard_map/ppermute | solution.py:68
  23.4 0.7 %shard_map.71 = (f32[256,512]{1,0:T(8,128)S(1)}, bf16[256,512]{1,0:T(8,128)(2,1)S(1)}) custom-call(bf16[1,1024]{1,0:T(2,128)(2,1)S(1)} %reshape.35.gain_ref, bf16[1024,512]{1,0:T(8,128)(2,1)S(1)} %copy-done, bf16[128,1024]{1,0:T(8,128)(2,1)S(1)} %get-tuple-element.38.own_ref, bf16[128,1536]{1,0:T(8,128)(2,1)S(1)} %collective-permute-done.core_ref, ...), custom_call_target="tpu_custom_call" | custom-call | tf_op jit(solution)/shard_map/pallas_call | solution.py:82
  24.3 2.7 %collective-permute-start.12 = (bf16[512,128]{1,0:T(8,128)(2,1)S(1)}, bf16[512,128]{1,0:T(8,128)(2,1)S(1)}, u32[]{:S(2)}, u32[]{:S(2)}) collective-permute-start(bf16[512,128]{1,0:T(8,128)(2,1)S(1)} %fusion.3), channel_id=1, source_target_pairs={{0,16},{1,9},{2,18},{3,11},{4,20},{5,13},{6,22},{7,15},{8,24},{9,1... | collective-permute-start | bytes 393224 | tf_op jit(solution)/shard_map/ppermute | solution.py:68
  27.0 1.0 %collective-permute-done.8 = bf16[2,512,128]{2,1,0:T(8,128)(2,1)S(1)} collective-permute-done((bf16[2,512,128]{2,1,0:T(8,128)(2,1)S(1)}, bf16[2,512,128]{2,1,0:T(8,128)(2,1)S(1)}, u32[]{:S(2)}, u32[]{:S(2)}) %collective-permute-start.8) | collective-permute-done | bytes 262176 | tf_op jit(solution)/shard_map/ppermute | solution.py:68
  28.2 1.9 %collective-permute-start.11 = (bf16[512,128]{1,0:T(8,128)(2,1)S(1)}, bf16[512,128]{1,0:T(8,128)(2,1)S(1)}, u32[]{:S(2)}, u32[]{:S(2)}) collective-permute-start(bf16[512,128]{1,0:T(8,128)(2,1)S(1)} %fusion.2), channel_id=1, source_target_pairs={{0,8},{1,5},{2,10},{3,7},{4,12},{5,1},{6,14},{7,3},{8,0},{9,13},{1... | collective-permute-start | bytes 393224 | tf_op jit(solution)/shard_map/ppermute | solution.py:68
  30.1 1.5 %collective-permute-start.10 = (bf16[128,512]{1,0:T(8,128)(2,1)S(1)}, bf16[128,512]{1,0:T(8,128)(2,1)S(1)}, u32[]{:S(2)}, u32[]{:S(2)}) collective-permute-start(bf16[128,512]{1,0:T(8,128)(2,1)S(1)} %slice.55), channel_id=1, source_target_pairs={{0,2},{1,3},{2,0},{3,1},{4,6},{5,7},{6,4},{7,5},{8,10},{9,11},{10,... | collective-permute-start | bytes 393224 | tf_op jit(solution)/shard_map/ppermute | solution.py:72
  31.7 1.6 %collective-permute-start.14 = (bf16[512,128]{1,0:T(8,128)(2,1)S(1)}, bf16[512,128]{1,0:T(8,128)(2,1)S(1)}, u32[]{:S(2)}, u32[]{:S(2)}) collective-permute-start(bf16[512,128]{1,0:T(8,128)(2,1)S(1)} %fusion), channel_id=1, source_target_pairs={{0,4},{1,17},{2,6},{3,19},{4,0},{5,21},{6,2},{7,23},{8,12},{9,25},... | collective-permute-start | bytes 393224 | tf_op jit(solution)/shard_map/ppermute | solution.py:68
  33.3 3.6 %collective-permute-start.13 = (bf16[512,128]{1,0:T(8,128)(2,1)S(1)}, bf16[512,128]{1,0:T(8,128)(2,1)S(1)}, u32[]{:S(2)}, u32[]{:S(2)}) collective-permute-start(bf16[512,128]{1,0:T(8,128)(2,1)S(1)} %fusion.1), channel_id=1, source_target_pairs={{0,16},{1,17},{2,18},{3,19},{4,20},{5,21},{6,22},{7,23},{8,24},{9,... | collective-permute-start | bytes 393224 | tf_op jit(solution)/shard_map/ppermute | solution.py:68
  36.9 0.8 %shard_map.72 = bf16[128,512]{1,0:T(8,128)(2,1)} custom-call(f32[128,512]{1,0:T(8,128)S(1)} %slice.36.mine_ref, bf16[128,512]{1,0:T(8,128)(2,1)S(1)} %collective-permute-done.10.got_ref, f32[128,128]{1,0:T(8,128)S(1)} %get-tuple-element.56.inv_ref, f32[128,128]{1,0:T(8,128)S(1)} %get-tuple-element.74.cos_ref, f32[128,128]{1,0:T(8,128)S(1)} %get-tuple-element.75.sin_ref), custom_call_target="tpu_custom_call" | custom-call | tf_op jit(solution)/shard_map/pallas_call | solution.py:82
  37.8 1.6 %collective-permute-start.16 = (bf16[512,128]{1,0:T(8,128)(2,1)S(1)}, bf16[512,128]{1,0:T(8,128)(2,1)S(1)}, u32[]{:S(2)}, u32[]{:S(2)}) collective-permute-start(bf16[512,128]{1,0:T(8,128)(2,1)S(1)} %fusion.7.rest_0_), channel_id=1, source_target_pairs={{0,16},{1,9},{2,18},{3,11},{4,20},{5,13},{6,22},{7,15},{8,24},{9,1... | collective-permute-start | bytes 393224 | tf_op jit(solution)/shard_map/ppermute | solution.py:68
  39.4 3.3 %collective-permute-done.13 = bf16[512,128]{1,0:T(8,128)(2,1)S(1)} collective-permute-done((bf16[512,128]{1,0:T(8,128)(2,1)S(1)}, bf16[512,128]{1,0:T(8,128)(2,1)S(1)}, u32[]{:S(2)}, u32[]{:S(2)}) %collective-permute-start.13) | collective-permute-done | bytes 131104 | tf_op jit(solution)/shard_map/ppermute | solution.py:68
  42.7 1.8 %collective-permute-start.15 = (bf16[512,128]{1,0:T(8,128)(2,1)S(1)}, bf16[512,128]{1,0:T(8,128)(2,1)S(1)}, u32[]{:S(2)}, u32[]{:S(2)}) collective-permute-start(bf16[512,128]{1,0:T(8,128)(2,1)S(1)} %fusion.8.rest_0_), channel_id=1, source_target_pairs={{0,8},{1,5},{2,10},{3,7},{4,12},{5,1},{6,14},{7,3},{8,0},{9,13},{1... | collective-permute-start | bytes 393224 | tf_op jit(solution)/shard_map/ppermute | solution.py:68
  44.5 0.9 %collective-permute-done.16.rest_1_ = bf16[512,128]{1,0:T(8,128)(2,1)S(1)} collective-permute-done((bf16[512,128]{1,0:T(8,128)(2,1)S(1)}, bf16[512,128]{1,0:T(8,128)(2,1)S(1)}, u32[]{:S(2)}, u32[]{:S(2)}) %collective-permute-start.16) | collective-permute-done | bytes 131104 | tf_op jit(solution)/shard_map/ppermute | solution.py:68
  45.5 0.5 collective-permute-start.18
  46.0 1.8 %collective-permute-done.15.rest_1_ = bf16[512,128]{1,0:T(8,128)(2,1)S(1)} collective-permute-done((bf16[512,128]{1,0:T(8,128)(2,1)S(1)}, bf16[512,128]{1,0:T(8,128)(2,1)S(1)}, u32[]{:S(2)}, u32[]{:S(2)}) %collective-permute-start.15) | collective-permute-done | bytes 131104 | tf_op jit(solution)/shard_map/ppermute | solution.py:68
  47.8 1.1 %collective-permute-start.17 = (bf16[2,512,128]{2,1,0:T(8,128)(2,1)S(1)}, bf16[2,512,128]{2,1,0:T(8,128)(2,1)S(1)}, u32[]{:S(2)}, u32[]{:S(2)}) collective-permute-start(bf16[2,512,128]{2,1,0:T(8,128)(2,1)S(1)} %pad_maximum_fusion.1), channel_id=1, source_target_pairs={{0,4},{1,9},{2,6},{3,11},{4,0},{5,13},{6,2},{7,15},{8,12},{9,1},{1... | collective-permute-start | bytes 786440 | tf_op jit(solution)/shard_map/ppermute | solution.py:68
  48.9 1.0 %shard_map.73 = (f32[1024,512]{1,0:T(8,128)}, f32[8,128]{1,0:T(8,128)S(1)}) custom-call(bf16[1,1024]{1,0:T(2,128)(2,1)S(1)} %reshape.35.gain_ref, bf16[1024,512]{1,0:T(8,128)(2,1)S(1)} %copy-done, bf16[512,128]{1,0:T(8,128)(2,1)S(1)} %fusion.7.rest_0_, bf16[512,128]{1,0:T(8,128)(2,1)S(1)} %collective-permute-done.16.rest_1_), custom_call_target="tpu_custom_call" | custom-call | tf_op jit(solution)/shard_map/pallas_call | solution.py:82
  49.9 1.0 %shard_map.74 = (f32[1024,512]{1,0:T(8,128)}, f32[8,128]{1,0:T(8,128)S(1)}) custom-call(bf16[1,1024]{1,0:T(2,128)(2,1)S(1)} %reshape.35.gain_ref, bf16[1024,512]{1,0:T(8,128)(2,1)S(1)} %copy-done, bf16[512,128]{1,0:T(8,128)(2,1)S(1)} %fusion.8.rest_0_, bf16[512,128]{1,0:T(8,128)(2,1)S(1)} %collective-permute-done.15.rest_1_, ...), custom_call_target="tpu_custom_call", output_to_operand_aliasing={{0}: (4, {})} | custom-call | tf_op jit(solution)/shard_map/pallas_call | solution.py:82
  51.0 3.5 %collective-permute-done.18.rest_0_ = bf16[2,512,128]{2,1,0:T(8,128)(2,1)S(1)} collective-permute-done((bf16[2,512,128]{2,1,0:T(8,128)(2,1)S(1)}, bf16[2,512,128]{2,1,0:T(8,128)(2,1)S(1)}, u32[]{:S(2)}, u32[]{:S(2)}) %collective-permute-start.18) | collective-permute-done | bytes 262176 | tf_op jit(solution)/shard_map/ppermute | solution.py:68
  54.4 1.0 %shard_map.75 = (f32[1024,512]{1,0:T(8,128)}, f32[8,128]{1,0:T(8,128)S(1)}) custom-call(bf16[1,1024]{1,0:T(2,128)(2,1)S(1)} %reshape.35.gain_ref, bf16[1024,512]{1,0:T(8,128)(2,1)S(1)} %copy-done, bf16[2,512,128]{2,1,0:T(8,128)(2,1)S(1)} %collective-permute-done.18.rest_0_, f32[1024,512]{1,0:T(8,128)} %get-tuple-element.65.rest_1_, ...), custom_call_target="tpu_custom_call", output_to_operand_aliasing={{0}: (3, {})} | custom-call | tf_op jit(solution)/shard_map/pallas_call | solution.py:82
  55.5 1.0 %shard_map.76 = (f32[1024,512]{1,0:T(8,128)}, f32[8,128]{1,0:T(8,128)}) custom-call(bf16[1,1024]{1,0:T(2,128)(2,1)S(1)} %reshape.35.gain_ref, bf16[1024,512]{1,0:T(8,128)(2,1)S(1)} %copy-done, bf16[2,512,128]{2,1,0:T(8,128)(2,1)S(1)} %collective-permute-done.17.rest_0_, f32[1024,512]{1,0:T(8,128)} %get-tuple-element.68.rest_1_, ...), custom_call_target="tpu_custom_call", output_to_operand_aliasing={{0}: (3, {})} | custom-call | tf_op jit(solution)/shard_map/pallas_call | solution.py:82
  (46 shorter events, 2.8 us)
Async XLA Ops:
  0.6 1.2 %copy-start.1 = (bf16[128,4096]{1,0:T(8,128)(2,1)S(1)}, bf16[128,4096]{1,0:T(8,128)(2,1)}, u32[]{:S(2)}) copy-start(bf16[128,4096]{1,0:T(8,128)(2,1)} %tok_ref.2) | copy-start | bytes 3145732
  1.9 3.5 %copy-start.2 = (bf16[128,4096]{1,0:T(8,128)(2,1)S(1)}, bf16[128,4096]{1,0:T(8,128)(2,1)}, u32[]{:S(2)}) copy-start(bf16[128,4096]{1,0:T(8,128)(2,1)} %tok_ref.2) | copy-start | bytes 3145732
  1.9 17.8 %copy-start.4 = (bf16[1024]{0:T(1024)(128)(2,1)S(1)}, bf16[1024]{0:T(1024)(128)(2,1)}, u32[]{:S(2)}) copy-start(bf16[1024]{0:T(1024)(128)(2,1)} %param.5) | copy-start | bytes 6148
  1.9 13.0 %collective-permute-start.2 = (bf16[128,1024]{1,0:T(8,128)(2,1)S(1)}, bf16[128,1024]{1,0:T(8,128)(2,1)S(1)}, u32[]{:S(2)}, u32[]{:S(2)}) collective-permute-start(bf16[128,1024]{1,0:T(8,128)(2,1)S(1)} %shard_map.67), channel_id=1, source_target_pairs={{0,2},{1,3},{2,0},{3,1},{4,6},{5,7},{6,4},{7,5},{8,10},{9,11},{10,... | collective-permute-start | bytes 786440 | tf_op jit(solution)/shard_map/ppermute | solution.py:72
  5.4 0.9 %copy-start.3 = (bf16[128,512]{1,0:T(8,128)(2,1)S(1)}, bf16[128,512]{1,0:T(8,128)(2,1)}, u32[]{:S(2)}) copy-start(bf16[128,512]{1,0:T(8,128)(2,1)} %grad_ref.1) | copy-start | bytes 393220
  6.3 17.1 %copy-start = (bf16[1024,512]{1,0:T(8,128)(2,1)S(1)}, bf16[1024,512]{1,0:T(8,128)(2,1)}, u32[]{:S(2)}) copy-start(bf16[1024,512]{1,0:T(8,128)(2,1)} %weight_ref.8) | copy-start | bytes 3145732
  6.7 9.8 %collective-permute-start = (bf16[128,1536]{1,0:T(8,128)(2,1)S(1)}, bf16[128,1536]{1,0:T(8,128)(2,1)S(1)}, u32[]{:S(2)}, u32[]{:S(2)}) collective-permute-start(bf16[128,1536]{1,0:T(8,128)(2,1)S(1)} %get-tuple-element.39), channel_id=1, source_target_pairs={{0,1},{1,0},{2,3},{3,2},{4,5},{5,4},{6,7},{7,6},{8,9},{9,8},{10,11... | collective-permute-start | bytes 1179656 | tf_op jit(solution)/shard_map/ppermute | solution.py:72
  6.7 8.1 %collective-permute-start.4 = (bf16[128,512]{1,0:T(8,128)(2,1)S(1)}, bf16[128,512]{1,0:T(8,128)(2,1)S(1)}, u32[]{:S(2)}, u32[]{:S(2)}) collective-permute-start(bf16[128,512]{1,0:T(8,128)(2,1)S(1)} %get-tuple-element.41.scaled_ref), channel_id=1, source_target_pairs={{0,2},{1,3},{2,0},{3,1},{4,6},{5,7},{6,4},{7,5},{8,10},{9,11},{10,... | collective-permute-start | bytes 393224 | tf_op jit(solution)/shard_map/ppermute | solution.py:72
  7.4 12.3 %collective-permute-start.1 = (bf16[128,1024]{1,0:T(8,128)(2,1)S(1)}, bf16[128,1024]{1,0:T(8,128)(2,1)S(1)}, u32[]{:S(2)}, u32[]{:S(2)}) collective-permute-start(bf16[128,1024]{1,0:T(8,128)(2,1)S(1)} %get-tuple-element.40), channel_id=1, source_target_pairs={{0,2},{1,3},{2,0},{3,1},{4,6},{5,7},{6,4},{7,5},{8,10},{9,11},{10,... | collective-permute-start | bytes 786440 | tf_op jit(solution)/shard_map/ppermute | solution.py:72
  14.9 1.3 %collective-permute-start.5 = (bf16[128,512]{1,0:T(8,128)(2,1)S(1)}, bf16[128,512]{1,0:T(8,128)(2,1)S(1)}, u32[]{:S(2)}, u32[]{:S(2)}) collective-permute-start(bf16[128,512]{1,0:T(8,128)(2,1)S(1)} %collective-permute-done.4.x_grad), channel_id=1, source_target_pairs={{0,1},{1,0},{2,3},{3,2},{4,5},{5,4},{6,7},{7,6},{8,9},{9,8},{10,11... | collective-permute-start | bytes 393224 | tf_op jit(solution)/shard_map/ppermute | solution.py:72
  14.9 1.6 %collective-permute-start.3 = (bf16[128,512]{1,0:T(8,128)(2,1)S(1)}, bf16[128,512]{1,0:T(8,128)(2,1)S(1)}, u32[]{:S(2)}, u32[]{:S(2)}) collective-permute-start(bf16[128,512]{1,0:T(8,128)(2,1)S(1)} %slice.35), channel_id=1, source_target_pairs={{0,1},{1,0},{2,3},{3,2},{4,5},{5,4},{6,7},{7,6},{8,9},{9,8},{10,11... | collective-permute-start | bytes 393224 | tf_op jit(solution)/shard_map/ppermute | solution.py:72
  17.0 7.3 %collective-permute-start.9 = (bf16[2,512,128]{2,1,0:T(8,128)(2,1)S(1)}, bf16[2,512,128]{2,1,0:T(8,128)(2,1)S(1)}, u32[]{:S(2)}, u32[]{:S(2)}) collective-permute-start(bf16[2,512,128]{2,1,0:T(8,128)(2,1)S(1)} %get-tuple-element.42), channel_id=1, source_target_pairs={{0,8},{1,5},{2,10},{3,7},{4,12},{5,1},{6,14},{7,3},{8,0},{9,13},{1... | collective-permute-start | bytes 786440 | tf_op jit(solution)/shard_map/ppermute | solution.py:68
  19.7 1.4 %collective-permute-start.6 = (bf16[128,512]{1,0:T(8,128)(2,1)S(1)}, bf16[128,512]{1,0:T(8,128)(2,1)S(1)}, u32[]{:S(2)}, u32[]{:S(2)}) collective-permute-start(bf16[128,512]{1,0:T(8,128)(2,1)S(1)} %slice.28), channel_id=1, source_target_pairs={{0,1},{1,0},{2,3},{3,2},{4,5},{5,4},{6,7},{7,6},{8,9},{9,8},{10,11... | collective-permute-start | bytes 393224 | tf_op jit(solution)/shard_map/ppermute | solution.py:72
  21.6 6.4 %collective-permute-start.8 = (bf16[2,512,128]{2,1,0:T(8,128)(2,1)S(1)}, bf16[2,512,128]{2,1,0:T(8,128)(2,1)S(1)}, u32[]{:S(2)}, u32[]{:S(2)}) collective-permute-start(bf16[2,512,128]{2,1,0:T(8,128)(2,1)S(1)} %get-tuple-element.44), channel_id=1, source_target_pairs={{0,4},{1,9},{2,6},{3,11},{4,0},{5,13},{6,2},{7,15},{8,12},{9,1},{1... | collective-permute-start | bytes 786440 | tf_op jit(solution)/shard_map/ppermute | solution.py:68
  24.1 3.9 %collective-permute-start.7 = (bf16[256,512]{1,0:T(8,128)(2,1)S(1)}, bf16[256,512]{1,0:T(8,128)(2,1)S(1)}, u32[]{:S(2)}, u32[]{:S(2)}) collective-permute-start(bf16[256,512]{1,0:T(8,128)(2,1)S(1)} %get-tuple-element.47), channel_id=1, source_target_pairs={{0,1},{1,0},{2,3},{3,2},{4,5},{5,4},{6,7},{7,6},{8,9},{9,8},{10,11... | collective-permute-start | bytes 786440 | tf_op jit(solution)/shard_map/ppermute | solution.py:72
  24.3 7.3 %collective-permute-start.12 = (bf16[512,128]{1,0:T(8,128)(2,1)S(1)}, bf16[512,128]{1,0:T(8,128)(2,1)S(1)}, u32[]{:S(2)}, u32[]{:S(2)}) collective-permute-start(bf16[512,128]{1,0:T(8,128)(2,1)S(1)} %fusion.3), channel_id=1, source_target_pairs={{0,16},{1,9},{2,18},{3,11},{4,20},{5,13},{6,22},{7,15},{8,24},{9,1... | collective-permute-start | bytes 393224 | tf_op jit(solution)/shard_map/ppermute | solution.py:68
  28.2 5.0 %collective-permute-start.11 = (bf16[512,128]{1,0:T(8,128)(2,1)S(1)}, bf16[512,128]{1,0:T(8,128)(2,1)S(1)}, u32[]{:S(2)}, u32[]{:S(2)}) collective-permute-start(bf16[512,128]{1,0:T(8,128)(2,1)S(1)} %fusion.2), channel_id=1, source_target_pairs={{0,8},{1,5},{2,10},{3,7},{4,12},{5,1},{6,14},{7,3},{8,0},{9,13},{1... | collective-permute-start | bytes 393224 | tf_op jit(solution)/shard_map/ppermute | solution.py:68
  30.1 6.8 %collective-permute-start.10 = (bf16[128,512]{1,0:T(8,128)(2,1)S(1)}, bf16[128,512]{1,0:T(8,128)(2,1)S(1)}, u32[]{:S(2)}, u32[]{:S(2)}) collective-permute-start(bf16[128,512]{1,0:T(8,128)(2,1)S(1)} %slice.55), channel_id=1, source_target_pairs={{0,2},{1,3},{2,0},{3,1},{4,6},{5,7},{6,4},{7,5},{8,10},{9,11},{10,... | collective-permute-start | bytes 393224 | tf_op jit(solution)/shard_map/ppermute | solution.py:72
  31.7 6.0 %collective-permute-start.14 = (bf16[512,128]{1,0:T(8,128)(2,1)S(1)}, bf16[512,128]{1,0:T(8,128)(2,1)S(1)}, u32[]{:S(2)}, u32[]{:S(2)}) collective-permute-start(bf16[512,128]{1,0:T(8,128)(2,1)S(1)} %fusion), channel_id=1, source_target_pairs={{0,4},{1,17},{2,6},{3,19},{4,0},{5,21},{6,2},{7,23},{8,12},{9,25},... | collective-permute-start | bytes 393224 | tf_op jit(solution)/shard_map/ppermute | solution.py:68
  33.3 9.4 %collective-permute-start.13 = (bf16[512,128]{1,0:T(8,128)(2,1)S(1)}, bf16[512,128]{1,0:T(8,128)(2,1)S(1)}, u32[]{:S(2)}, u32[]{:S(2)}) collective-permute-start(bf16[512,128]{1,0:T(8,128)(2,1)S(1)} %fusion.1), channel_id=1, source_target_pairs={{0,16},{1,17},{2,18},{3,19},{4,20},{5,21},{6,22},{7,23},{8,24},{9,... | collective-permute-start | bytes 393224 | tf_op jit(solution)/shard_map/ppermute | solution.py:68
  37.8 7.7 %collective-permute-start.16 = (bf16[512,128]{1,0:T(8,128)(2,1)S(1)}, bf16[512,128]{1,0:T(8,128)(2,1)S(1)}, u32[]{:S(2)}, u32[]{:S(2)}) collective-permute-start(bf16[512,128]{1,0:T(8,128)(2,1)S(1)} %fusion.7.rest_0_), channel_id=1, source_target_pairs={{0,16},{1,9},{2,18},{3,11},{4,20},{5,13},{6,22},{7,15},{8,24},{9,1... | collective-permute-start | bytes 393224 | tf_op jit(solution)/shard_map/ppermute | solution.py:68
  42.7 5.0 %collective-permute-start.15 = (bf16[512,128]{1,0:T(8,128)(2,1)S(1)}, bf16[512,128]{1,0:T(8,128)(2,1)S(1)}, u32[]{:S(2)}, u32[]{:S(2)}) collective-permute-start(bf16[512,128]{1,0:T(8,128)(2,1)S(1)} %fusion.8.rest_0_), channel_id=1, source_target_pairs={{0,8},{1,5},{2,10},{3,7},{4,12},{5,1},{6,14},{7,3},{8,0},{9,13},{1... | collective-permute-start | bytes 393224 | tf_op jit(solution)/shard_map/ppermute | solution.py:68
  45.5 8.9 %collective-permute-start.18 = (bf16[2,512,128]{2,1,0:T(8,128)(2,1)S(1)}, bf16[2,512,128]{2,1,0:T(8,128)(2,1)S(1)}, u32[]{:S(2)}, u32[]{:S(2)}) collective-permute-start(bf16[2,512,128]{2,1,0:T(8,128)(2,1)S(1)} %pad_maximum_fusion), channel_id=1, source_target_pairs={{0,8},{1,5},{2,10},{3,7},{4,12},{5,1},{6,14},{7,3},{8,0},{9,13},{1... | collective-permute-start | bytes 786440 | tf_op jit(solution)/shard_map/ppermute | solution.py:68
  47.8 7.7 %collective-permute-start.17 = (bf16[2,512,128]{2,1,0:T(8,128)(2,1)S(1)}, bf16[2,512,128]{2,1,0:T(8,128)(2,1)S(1)}, u32[]{:S(2)}, u32[]{:S(2)}) collective-permute-start(bf16[2,512,128]{2,1,0:T(8,128)(2,1)S(1)} %pad_maximum_fusion.1), channel_id=1, source_target_pairs={{0,4},{1,9},{2,6},{3,11},{4,0},{5,13},{6,2},{7,15},{8,12},{9,1},{1... | collective-permute-start | bytes 786440 | tf_op jit(solution)/shard_map/ppermute | solution.py:68

commit v4 on v3

--- a/solution.py
+++ b/solution.py
@@ -184,11 +184,11 @@
 
 
 def finish_weights(start, size, chunk, wide_size, grad_scale, half, last, gain_ref, weight_ref, *rest):
-    out, gain_out, held, gains, sent = rest[-5:]
-    sources = [rest[0], rest[1]] if half == 0 else [rest[0].at[0], rest[0].at[1]]
-    before = rest[-6] if len(rest) > 5 + 2 - half else None
+    out, gain_out, held, gains, sent, gain_sent = rest[-6:]
+    places = quarters(wide_size, chunk)[3 * half : 3 + half]
+    sources = rest[: len(places)]
+    before = rest[-7] if len(rest) > 6 + len(places) else None
     gains[...] = jnp.zeros_like(gains) if before is None else before[...]
-    places = quarters(wide_size, chunk)[2 * half : 2 * half + 2]
     copies = []
     for row in range(0, size, TILE):
         rows, here = slice(row, row + TILE), slice(start + row, start + row + TILE)
@@ -199,20 +199,19 @@
             terms = source[rows].astype(F32)
             folded = folded + terms * weight_ref[here, pl.ds(at, TILE)].astype(F32)
             held[part, rows] = terms * column
+            copies.append(
+                pltpu.make_async_copy(
+                    held.at[part, rows], out.at[here, pl.ds(at, TILE)], sent.at[part, row // TILE]
+                )
+            )
+            copies[-1].start()
         line = (start + row) // TILE
         gains[line : line + 1] += jnp.sum(folded.T, axis=0, keepdims=True) * grad_scale
-    for part, at in enumerate(places):
-        copies.append(
-            pltpu.make_async_copy(
-                held.at[part], out.at[start : start + size, pl.ds(at, TILE)], sent.at[part]
-            )
-        )
     if last:
-        copies.append(pltpu.make_async_copy(gains, gain_out, sent.at[2]))
+        copies.append(pltpu.make_async_copy(gains, gain_out, gain_sent))
+        copies[-1].start()
     else:
         gain_out[...] = gains[...]
-    for copy in copies:
-        copy.start()
     for copy in copies:
         copy.wait()
 
@@ -227,9 +226,10 @@
         gain_row, key_weight, *parts, *before,
         anywhere=(at,),
         scratch=[
-            pltpu.VMEM((2, size, TILE), F32),
+            pltpu.VMEM((len(parts), size, TILE), F32),
             pltpu.VMEM(*gain_kind),
-            pltpu.SemaphoreType.DMA((3,)),
+            pltpu.SemaphoreType.DMA((len(parts), size // TILE)),
+            pltpu.SemaphoreType.DMA,
         ],
         input_output_aliases={at: 0} if before else {},
     )
@@ -316,15 +316,15 @@
             latest = totals[k]
     mine = [total.astype(BF16) for total in totals]
     near = [summed(value, chunk=k, stage=1) for k, value in enumerate(mine)]
-    both = []
+    far = [summed(value, chunk=k, stage=0) for k, value in enumerate(mine)]
     for k in range(count):
-        both.append(jnp.stack([mine[k], after(near[k], latest)]))
-        latest = both[-1]
-    far = [summed(value, chunk=k, stage=0) for k, value in enumerate(both)]
+        near[k] = after(near[k], latest)
+        far[k] = latest = after(far[k], near[k])
+    last = [summed(value, chunk=k, stage=0) for k, value in enumerate(near)]
     before = ()
     for half in range(2):
         for k, (start, size) in enumerate(chunks):
-            parts = (after(far[k], latest),) if half else (both[k][0], both[k][1])
+            parts = (after(last[k], latest),) if half else (mine[k], near[k], after(far[k], latest))
             before = write_weights(
                 start, size, k, wide_size, grad_scale, half, half == 1 and k == count - 1,
                 gain_row, key_weight, parts, before,

time: 56.7 us -> 55 us (0.970)
  waiting for transfers between devices: 19.4 us -> 16.4 us
  starting transfers between devices: 26.2 us -> 27.7 us
    ppermute x10 -> x12, waiting for transfers between devices: 10.5 us -> 7.49 us  [swap_wide(): return lax.ppermute(value, BOTH, pairs)]
    ppermute x10 -> x12, starting transfers between devices: 18.8 us -> 20.4 us  [swap_wide(): return lax.ppermute(value, BOTH, pairs)]
  transfers between devices with their start and end apart: 19 -> 21, of which waited for: 10 -> 12; matrix products, arithmetic and copies ran while one was open for 2% -> 2% of each run, Pallas kernels for 11% -> 11%
where the time goes in v4:
time: 55 us; the launch traced here: 54.8 us
  starting transfers between devices  27.7 us (50%)
  waiting for transfers between devices  16.4 us (30%)
  Pallas kernels  6.85 us (12%)
  local copies, waits for them, and re-layouts  2.23 us (4%)
  between operations  0.9 us (2%)
  other arithmetic  0.76 us (1%)
    ppermute x12, starting transfers between devices, swap_wide(): return lax.ppermute(value, BOTH, pairs)  20.4 us
    ppermute x9, waiting for transfers between devices, swap_narrow(): lax.ppermute(value, 'narrow', [(i, i ^ mask) for i in range(narrow_size)])  8.87 us
    ppermute x12, waiting for transfers between devices, swap_wide(): return lax.ppermute(value, BOTH, pairs)  7.49 us
    ppermute x9, starting transfers between devices, swap_narrow(): lax.ppermute(value, 'narrow', [(i, i ^ mask) for i in range(narrow_size)])  7.38 us
    pallas_call x10, Pallas kernels, call(): pl.pallas_call(body, out_shape=[jax.ShapeDtypeStruct(shape, kind) for sha...  6.85 us
    unnamed x10, local copies, waits for them, and re-layouts  2.13 us
  transfers between devices with their start and end apart: 21, of which 12 were waited for; matrix products, arithmetic and copies ran while one was open for 2% of the time, Pallas kernels for 11%

profile of v4, /device:TPU:0, one launch (start us, length us, event | category | flops | bytes accessed | tf_op | source)
XLA Modules:
  0.0 54.8 jit_solution(9824092818766387121)
XLA Ops:
  0.6 1.2 %copy-done.1 = bf16[128,4096]{1,0:T(8,128)(2,1)S(1)} copy-done((bf16[128,4096]{1,0:T(8,128)(2,1)S(1)}, bf16[128,4096]{1,0:T(8,128)(2,1)}, u32[]{:S(2)}) %copy-start.1) | copy-done | bytes 1048600
  1.9 3.0 %collective-permute-start.2 = (bf16[128,1024]{1,0:T(8,128)(2,1)S(1)}, bf16[128,1024]{1,0:T(8,128)(2,1)S(1)}, u32[]{:S(2)}, u32[]{:S(2)}) collective-permute-start(bf16[128,1024]{1,0:T(8,128)(2,1)S(1)} %shard_map.67), channel_id=1, source_target_pairs={{0,2},{1,3},{2,0},{3,1},{4,6},{5,7},{6,4},{7,5},{8,10},{9,11},{10,... | collective-permute-start | bytes 786440 | tf_op jit(solution)/shard_map/ppermute | solution.py:72
  5.4 0.9 %copy-done.3 = bf16[128,512]{1,0:T(8,128)(2,1)S(1)} copy-done((bf16[128,512]{1,0:T(8,128)(2,1)S(1)}, bf16[128,512]{1,0:T(8,128)(2,1)}, u32[]{:S(2)}) %copy-start.3) | copy-done | bytes 131096
  6.7 0.7 %collective-permute-start.4 = (bf16[128,512]{1,0:T(8,128)(2,1)S(1)}, bf16[128,512]{1,0:T(8,128)(2,1)S(1)}, u32[]{:S(2)}, u32[]{:S(2)}) collective-permute-start(bf16[128,512]{1,0:T(8,128)(2,1)S(1)} %get-tuple-element.45.scaled_ref), channel_id=1, source_target_pairs={{0,2},{1,3},{2,0},{3,1},{4,6},{5,7},{6,4},{7,5},{8,10},{9,11},{10,... | collective-permute-start | bytes 393224 | tf_op jit(solution)/shard_map/ppermute | solution.py:72
  7.4 1.4 %collective-permute-start.1 = (bf16[128,1024]{1,0:T(8,128)(2,1)S(1)}, bf16[128,1024]{1,0:T(8,128)(2,1)S(1)}, u32[]{:S(2)}, u32[]{:S(2)}) collective-permute-start(bf16[128,1024]{1,0:T(8,128)(2,1)S(1)} %get-tuple-element.44), channel_id=1, source_target_pairs={{0,2},{1,3},{2,0},{3,1},{4,6},{5,7},{6,4},{7,5},{8,10},{9,11},{10,... | collective-permute-start | bytes 786440 | tf_op jit(solution)/shard_map/ppermute | solution.py:72
  8.8 6.0 %collective-permute-done.4.x_grad = bf16[128,512]{1,0:T(8,128)(2,1)S(1)} collective-permute-done((bf16[128,512]{1,0:T(8,128)(2,1)S(1)}, bf16[128,512]{1,0:T(8,128)(2,1)S(1)}, u32[]{:S(2)}, u32[]{:S(2)}) %collective-permute-start.4) | collective-permute-done | bytes 131104 | tf_op jit(solution)/shard_map/ppermute | solution.py:72
  14.9 0.6 %collective-permute-start.3 = (bf16[128,512]{1,0:T(8,128)(2,1)S(1)}, bf16[128,512]{1,0:T(8,128)(2,1)S(1)}, u32[]{:S(2)}, u32[]{:S(2)}) collective-permute-start(bf16[128,512]{1,0:T(8,128)(2,1)S(1)} %slice.35), channel_id=1, source_target_pairs={{0,1},{1,0},{2,3},{3,2},{4,5},{5,4},{6,7},{7,6},{8,9},{9,8},{10,11... | collective-permute-start | bytes 393224 | tf_op jit(solution)/shard_map/ppermute | solution.py:72
  15.5 0.8 %collective-permute-done.5.last_grad = bf16[128,512]{1,0:T(8,128)(2,1)S(1)} collective-permute-done((bf16[128,512]{1,0:T(8,128)(2,1)S(1)}, bf16[128,512]{1,0:T(8,128)(2,1)S(1)}, u32[]{:S(2)}, u32[]{:S(2)}) %collective-permute-start.5) | collective-permute-done | bytes 131104 | tf_op jit(solution)/shard_map/ppermute | solution.py:72
  17.0 2.2 %collective-permute-start.9 = (bf16[2,512,128]{2,1,0:T(8,128)(2,1)S(1)}, bf16[2,512,128]{2,1,0:T(8,128)(2,1)S(1)}, u32[]{:S(2)}, u32[]{:S(2)}) collective-permute-start(bf16[2,512,128]{2,1,0:T(8,128)(2,1)S(1)} %get-tuple-element.46), channel_id=1, source_target_pairs={{0,8},{1,5},{2,10},{3,7},{4,12},{5,1},{6,14},{7,3},{8,0},{9,13},{1... | collective-permute-start | bytes 786440 | tf_op jit(solution)/shard_map/ppermute | solution.py:68
  19.2 0.5 collective-permute-done.1.x_ref.rest_1_
  19.8 1.3 %collective-permute-done.6.last_ref.rest_3_ = bf16[128,512]{1,0:T(8,128)(2,1)S(1)} collective-permute-done((bf16[128,512]{1,0:T(8,128)(2,1)S(1)}, bf16[128,512]{1,0:T(8,128)(2,1)S(1)}, u32[]{:S(2)}, u32[]{:S(2)}) %collective-permute-start.6) | collective-permute-done | bytes 131104 | tf_op jit(solution)/shard_map/ppermute | solution.py:72
  21.6 1.8 %collective-permute-start.8 = (bf16[2,512,128]{2,1,0:T(8,128)(2,1)S(1)}, bf16[2,512,128]{2,1,0:T(8,128)(2,1)S(1)}, u32[]{:S(2)}, u32[]{:S(2)}) collective-permute-start(bf16[2,512,128]{2,1,0:T(8,128)(2,1)S(1)} %get-tuple-element.48), channel_id=1, source_target_pairs={{0,4},{1,9},{2,6},{3,11},{4,0},{5,13},{6,2},{7,15},{8,12},{9,1},{1... | collective-permute-start | bytes 786440 | tf_op jit(solution)/shard_map/ppermute | solution.py:68
  23.4 0.7 %shard_map.71 = (f32[256,512]{1,0:T(8,128)S(1)}, bf16[256,512]{1,0:T(8,128)(2,1)S(1)}) custom-call(bf16[1,1024]{1,0:T(2,128)(2,1)S(1)} %reshape.35.gain_ref, bf16[1024,512]{1,0:T(8,128)(2,1)S(1)} %copy-done, bf16[128,1024]{1,0:T(8,128)(2,1)S(1)} %get-tuple-element.42.own_ref, bf16[128,1536]{1,0:T(8,128)(2,1)S(1)} %collective-permute-done.core_ref, ...), custom_call_target="tpu_custom_call" | custom-call | tf_op jit(solution)/shard_map/pallas_call | solution.py:82
  24.3 2.7 %collective-permute-start.12 = (bf16[512,128]{1,0:T(8,128)(2,1)S(1)}, bf16[512,128]{1,0:T(8,128)(2,1)S(1)}, u32[]{:S(2)}, u32[]{:S(2)}) collective-permute-start(bf16[512,128]{1,0:T(8,128)(2,1)S(1)} %fusion.3), channel_id=1, source_target_pairs={{0,16},{1,9},{2,18},{3,11},{4,20},{5,13},{6,22},{7,15},{8,24},{9,1... | collective-permute-start | bytes 393224 | tf_op jit(solution)/shard_map/ppermute | solution.py:68
  27.0 1.0 %collective-permute-done.8 = bf16[2,512,128]{2,1,0:T(8,128)(2,1)S(1)} collective-permute-done((bf16[2,512,128]{2,1,0:T(8,128)(2,1)S(1)}, bf16[2,512,128]{2,1,0:T(8,128)(2,1)S(1)}, u32[]{:S(2)}, u32[]{:S(2)}) %collective-permute-start.8) | collective-permute-done | bytes 262176 | tf_op jit(solution)/shard_map/ppermute | solution.py:68
  28.2 1.9 %collective-permute-start.11 = (bf16[512,128]{1,0:T(8,128)(2,1)S(1)}, bf16[512,128]{1,0:T(8,128)(2,1)S(1)}, u32[]{:S(2)}, u32[]{:S(2)}) collective-permute-start(bf16[512,128]{1,0:T(8,128)(2,1)S(1)} %fusion.2), channel_id=1, source_target_pairs={{0,8},{1,5},{2,10},{3,7},{4,12},{5,1},{6,14},{7,3},{8,0},{9,13},{1... | collective-permute-start | bytes 393224 | tf_op jit(solution)/shard_map/ppermute | solution.py:68
  30.1 1.5 %collective-permute-start.10 = (bf16[128,512]{1,0:T(8,128)(2,1)S(1)}, bf16[128,512]{1,0:T(8,128)(2,1)S(1)}, u32[]{:S(2)}, u32[]{:S(2)}) collective-permute-start(bf16[128,512]{1,0:T(8,128)(2,1)S(1)} %slice.55), channel_id=1, source_target_pairs={{0,2},{1,3},{2,0},{3,1},{4,6},{5,7},{6,4},{7,5},{8,10},{9,11},{10,... | collective-permute-start | bytes 393224 | tf_op jit(solution)/shard_map/ppermute | solution.py:72
  31.7 1.6 %collective-permute-start.14 = (bf16[512,128]{1,0:T(8,128)(2,1)S(1)}, bf16[512,128]{1,0:T(8,128)(2,1)S(1)}, u32[]{:S(2)}, u32[]{:S(2)}) collective-permute-start(bf16[512,128]{1,0:T(8,128)(2,1)S(1)} %fusion), channel_id=1, source_target_pairs={{0,4},{1,17},{2,6},{3,19},{4,0},{5,21},{6,2},{7,23},{8,12},{9,25},... | collective-permute-start | bytes 393224 | tf_op jit(solution)/shard_map/ppermute | solution.py:68
  33.3 3.6 %collective-permute-start.13 = (bf16[512,128]{1,0:T(8,128)(2,1)S(1)}, bf16[512,128]{1,0:T(8,128)(2,1)S(1)}, u32[]{:S(2)}, u32[]{:S(2)}) collective-permute-start(bf16[512,128]{1,0:T(8,128)(2,1)S(1)} %fusion.1), channel_id=1, source_target_pairs={{0,16},{1,17},{2,18},{3,19},{4,20},{5,21},{6,22},{7,23},{8,24},{9,... | collective-permute-start | bytes 393224 | tf_op jit(solution)/shard_map/ppermute | solution.py:68
  36.9 0.8 %shard_map.72 = bf16[128,512]{1,0:T(8,128)(2,1)} custom-call(f32[128,512]{1,0:T(8,128)S(1)} %slice.36.mine_ref, bf16[128,512]{1,0:T(8,128)(2,1)S(1)} %collective-permute-done.10.got_ref, f32[128,128]{1,0:T(8,128)S(1)} %get-tuple-element.60.inv_ref, f32[128,128]{1,0:T(8,128)S(1)} %get-tuple-element.82.cos_ref, f32[128,128]{1,0:T(8,128)S(1)} %get-tuple-element.83.sin_ref), custom_call_target="tpu_custom_call" | custom-call | tf_op jit(solution)/shard_map/pallas_call | solution.py:82
  37.8 1.6 %collective-permute-start.17 = (bf16[512,128]{1,0:T(8,128)(2,1)S(1)}, bf16[512,128]{1,0:T(8,128)(2,1)S(1)}, u32[]{:S(2)}, u32[]{:S(2)}) collective-permute-start(bf16[512,128]{1,0:T(8,128)(2,1)S(1)} %fusion.7.rest_0_), channel_id=1, source_target_pairs={{0,16},{1,9},{2,18},{3,11},{4,20},{5,13},{6,22},{7,15},{8,24},{9,1... | collective-permute-start | bytes 393224 | tf_op jit(solution)/shard_map/ppermute | solution.py:68
  39.4 1.5 %collective-permute-start.16 = (bf16[512,128]{1,0:T(8,128)(2,1)S(1)}, bf16[512,128]{1,0:T(8,128)(2,1)S(1)}, u32[]{:S(2)}, u32[]{:S(2)}) collective-permute-start(bf16[512,128]{1,0:T(8,128)(2,1)S(1)} %fusion.7.rest_0_), channel_id=1, source_target_pairs={{0,8},{1,5},{2,10},{3,7},{4,12},{5,1},{6,14},{7,3},{8,0},{9,13},{1... | collective-permute-start | bytes 393224 | tf_op jit(solution)/shard_map/ppermute | solution.py:68
  40.9 1.8 %collective-permute-done.13 = bf16[512,128]{1,0:T(8,128)(2,1)S(1)} collective-permute-done((bf16[512,128]{1,0:T(8,128)(2,1)S(1)}, bf16[512,128]{1,0:T(8,128)(2,1)S(1)}, u32[]{:S(2)}, u32[]{:S(2)}) %collective-permute-start.13) | collective-permute-done | bytes 131104 | tf_op jit(solution)/shard_map/ppermute | solution.py:68
  42.7 1.8 %collective-permute-start.15 = (bf16[512,128]{1,0:T(8,128)(2,1)S(1)}, bf16[512,128]{1,0:T(8,128)(2,1)S(1)}, u32[]{:S(2)}, u32[]{:S(2)}) collective-permute-start(bf16[512,128]{1,0:T(8,128)(2,1)S(1)} %fusion.8.rest_0_), channel_id=1, source_target_pairs={{0,8},{1,5},{2,10},{3,7},{4,12},{5,1},{6,14},{7,3},{8,0},{9,13},{1... | collective-permute-start | bytes 393224 | tf_op jit(solution)/shard_map/ppermute | solution.py:68
  44.6 0.9 %collective-permute-done.17.rest_1_ = bf16[512,128]{1,0:T(8,128)(2,1)S(1)} collective-permute-done((bf16[512,128]{1,0:T(8,128)(2,1)S(1)}, bf16[512,128]{1,0:T(8,128)(2,1)S(1)}, u32[]{:S(2)}, u32[]{:S(2)}) %collective-permute-start.17) | collective-permute-done | bytes 131104 | tf_op jit(solution)/shard_map/ppermute | solution.py:68
  45.9 1.0 %collective-permute-done.16.rest_2_ = bf16[512,128]{1,0:T(8,128)(2,1)S(1)} collective-permute-done((bf16[512,128]{1,0:T(8,128)(2,1)S(1)}, bf16[512,128]{1,0:T(8,128)(2,1)S(1)}, u32[]{:S(2)}, u32[]{:S(2)}) %collective-permute-start.16) | collective-permute-done | bytes 131104 | tf_op jit(solution)/shard_map/ppermute | solution.py:68
  46.8 2.1 %collective-permute-done.15.rest_1_ = bf16[512,128]{1,0:T(8,128)(2,1)S(1)} collective-permute-done((bf16[512,128]{1,0:T(8,128)(2,1)S(1)}, bf16[512,128]{1,0:T(8,128)(2,1)S(1)}, u32[]{:S(2)}, u32[]{:S(2)}) %collective-permute-start.15) | collective-permute-done | bytes 131104 | tf_op jit(solution)/shard_map/ppermute | solution.py:68
  49.0 1.2 %collective-permute-start.18 = (bf16[512,128]{1,0:T(8,128)(2,1)S(1)}, bf16[512,128]{1,0:T(8,128)(2,1)S(1)}, u32[]{:S(2)}, u32[]{:S(2)}) collective-permute-start(bf16[512,128]{1,0:T(8,128)(2,1)S(1)} %collective-permute-done.15.rest_1_), channel_id=1, source_target_pairs={{0,4},{1,9},{2,6},{3,11},{4,0},{5,13},{6,2},{7,15},{8,12},{9,1},{1... | collective-permute-start | bytes 393224 | tf_op jit(solution)/shard_map/ppermute | solution.py:68
  50.5 1.1 %shard_map.73 = (f32[1024,512]{1,0:T(8,128)}, f32[8,128]{1,0:T(8,128)S(1)}) custom-call(bf16[1,1024]{1,0:T(2,128)(2,1)S(1)} %reshape.35.gain_ref, bf16[1024,512]{1,0:T(8,128)(2,1)S(1)} %copy-done, bf16[512,128]{1,0:T(8,128)(2,1)S(1)} %fusion.7.rest_0_, bf16[512,128]{1,0:T(8,128)(2,1)S(1)} %collective-permute-done.17.rest_1_, ...), custom_call_target="tpu_custom_call" | custom-call | tf_op jit(solution)/shard_map/pallas_call | solution.py:82
  51.6 1.1 %shard_map.74 = (f32[1024,512]{1,0:T(8,128)}, f32[8,128]{1,0:T(8,128)S(1)}) custom-call(bf16[1,1024]{1,0:T(2,128)(2,1)S(1)} %reshape.35.gain_ref, bf16[1024,512]{1,0:T(8,128)(2,1)S(1)} %copy-done, bf16[512,128]{1,0:T(8,128)(2,1)S(1)} %fusion.8.rest_0_, bf16[512,128]{1,0:T(8,128)(2,1)S(1)} %collective-permute-done.15.rest_1_, ...), custom_call_target="tpu_custom_call", output_to_operand_aliasing={{0}: (5, {})} | custom-call | tf_op jit(solution)/shard_map/pallas_call | solution.py:82
  52.7 0.9 %shard_map.75 = (f32[1024,512]{1,0:T(8,128)}, f32[8,128]{1,0:T(8,128)S(1)}) custom-call(bf16[1,1024]{1,0:T(2,128)(2,1)S(1)} %reshape.35.gain_ref, bf16[1024,512]{1,0:T(8,128)(2,1)S(1)} %copy-done, bf16[512,128]{1,0:T(8,128)(2,1)S(1)} %collective-permute-done.19.rest_0_, f32[1024,512]{1,0:T(8,128)} %get-tuple-element.73.rest_1_, ...), custom_call_target="tpu_custom_call", output_to_operand_aliasing={{0}: (3, {})} | custom-call | tf_op jit(solution)/shard_map/pallas_call | solution.py:82
  53.9 0.9 %shard_map.76 = (f32[1024,512]{1,0:T(8,128)}, f32[8,128]{1,0:T(8,128)}) custom-call(bf16[1,1024]{1,0:T(2,128)(2,1)S(1)} %reshape.35.gain_ref, bf16[1024,512]{1,0:T(8,128)(2,1)S(1)} %copy-done, bf16[512,128]{1,0:T(8,128)(2,1)S(1)} %collective-permute-done.18.rest_0_, f32[1024,512]{1,0:T(8,128)} %get-tuple-element.76.rest_1_, ...), custom_call_target="tpu_custom_call", output_to_operand_aliasing={{0}: (3, {})} | custom-call | tf_op jit(solution)/shard_map/pallas_call | solution.py:82
  (48 shorter events, 3.8 us)
Async XLA Ops:
  0.6 1.2 %copy-start.1 = (bf16[128,4096]{1,0:T(8,128)(2,1)S(1)}, bf16[128,4096]{1,0:T(8,128)(2,1)}, u32[]{:S(2)}) copy-start(bf16[128,4096]{1,0:T(8,128)(2,1)} %tok_ref.2) | copy-start | bytes 3145732
  1.9 3.5 %copy-start.2 = (bf16[128,4096]{1,0:T(8,128)(2,1)S(1)}, bf16[128,4096]{1,0:T(8,128)(2,1)}, u32[]{:S(2)}) copy-start(bf16[128,4096]{1,0:T(8,128)(2,1)} %tok_ref.2) | copy-start | bytes 3145732
  1.9 17.8 %copy-start.4 = (bf16[1024]{0:T(1024)(128)(2,1)S(1)}, bf16[1024]{0:T(1024)(128)(2,1)}, u32[]{:S(2)}) copy-start(bf16[1024]{0:T(1024)(128)(2,1)} %param.5) | copy-start | bytes 6148
  1.9 13.0 %collective-permute-start.2 = (bf16[128,1024]{1,0:T(8,128)(2,1)S(1)}, bf16[128,1024]{1,0:T(8,128)(2,1)S(1)}, u32[]{:S(2)}, u32[]{:S(2)}) collective-permute-start(bf16[128,1024]{1,0:T(8,128)(2,1)S(1)} %shard_map.67), channel_id=1, source_target_pairs={{0,2},{1,3},{2,0},{3,1},{4,6},{5,7},{6,4},{7,5},{8,10},{9,11},{10,... | collective-permute-start | bytes 786440 | tf_op jit(solution)/shard_map/ppermute | solution.py:72
  5.4 0.9 %copy-start.3 = (bf16[128,512]{1,0:T(8,128)(2,1)S(1)}, bf16[128,512]{1,0:T(8,128)(2,1)}, u32[]{:S(2)}) copy-start(bf16[128,512]{1,0:T(8,128)(2,1)} %grad_ref.1) | copy-start | bytes 393220
  6.3 17.1 %copy-start = (bf16[1024,512]{1,0:T(8,128)(2,1)S(1)}, bf16[1024,512]{1,0:T(8,128)(2,1)}, u32[]{:S(2)}) copy-start(bf16[1024,512]{1,0:T(8,128)(2,1)} %weight_ref.8) | copy-start | bytes 3145732
  6.7 9.8 %collective-permute-start = (bf16[128,1536]{1,0:T(8,128)(2,1)S(1)}, bf16[128,1536]{1,0:T(8,128)(2,1)S(1)}, u32[]{:S(2)}, u32[]{:S(2)}) collective-permute-start(bf16[128,1536]{1,0:T(8,128)(2,1)S(1)} %get-tuple-element.43), channel_id=1, source_target_pairs={{0,1},{1,0},{2,3},{3,2},{4,5},{5,4},{6,7},{7,6},{8,9},{9,8},{10,11... | collective-permute-start | bytes 1179656 | tf_op jit(solution)/shard_map/ppermute | solution.py:72
  6.7 8.1 %collective-permute-start.4 = (bf16[128,512]{1,0:T(8,128)(2,1)S(1)}, bf16[128,512]{1,0:T(8,128)(2,1)S(1)}, u32[]{:S(2)}, u32[]{:S(2)}) collective-permute-start(bf16[128,512]{1,0:T(8,128)(2,1)S(1)} %get-tuple-element.45.scaled_ref), channel_id=1, source_target_pairs={{0,2},{1,3},{2,0},{3,1},{4,6},{5,7},{6,4},{7,5},{8,10},{9,11},{10,... | collective-permute-start | bytes 393224 | tf_op jit(solution)/shard_map/ppermute | solution.py:72
  7.4 12.3 %collective-permute-start.1 = (bf16[128,1024]{1,0:T(8,128)(2,1)S(1)}, bf16[128,1024]{1,0:T(8,128)(2,1)S(1)}, u32[]{:S(2)}, u32[]{:S(2)}) collective-permute-start(bf16[128,1024]{1,0:T(8,128)(2,1)S(1)} %get-tuple-element.44), channel_id=1, source_target_pairs={{0,2},{1,3},{2,0},{3,1},{4,6},{5,7},{6,4},{7,5},{8,10},{9,11},{10,... | collective-permute-start | bytes 786440 | tf_op jit(solution)/shard_map/ppermute | solution.py:72
  14.9 1.3 %collective-permute-start.5 = (bf16[128,512]{1,0:T(8,128)(2,1)S(1)}, bf16[128,512]{1,0:T(8,128)(2,1)S(1)}, u32[]{:S(2)}, u32[]{:S(2)}) collective-permute-start(bf16[128,512]{1,0:T(8,128)(2,1)S(1)} %collective-permute-done.4.x_grad), channel_id=1, source_target_pairs={{0,1},{1,0},{2,3},{3,2},{4,5},{5,4},{6,7},{7,6},{8,9},{9,8},{10,11... | collective-permute-start | bytes 393224 | tf_op jit(solution)/shard_map/ppermute | solution.py:72
  14.9 1.6 %collective-permute-start.3 = (bf16[128,512]{1,0:T(8,128)(2,1)S(1)}, bf16[128,512]{1,0:T(8,128)(2,1)S(1)}, u32[]{:S(2)}, u32[]{:S(2)}) collective-permute-start(bf16[128,512]{1,0:T(8,128)(2,1)S(1)} %slice.35), channel_id=1, source_target_pairs={{0,1},{1,0},{2,3},{3,2},{4,5},{5,4},{6,7},{7,6},{8,9},{9,8},{10,11... | collective-permute-start | bytes 393224 | tf_op jit(solution)/shard_map/ppermute | solution.py:72
  17.0 7.3 %collective-permute-start.9 = (bf16[2,512,128]{2,1,0:T(8,128)(2,1)S(1)}, bf16[2,512,128]{2,1,0:T(8,128)(2,1)S(1)}, u32[]{:S(2)}, u32[]{:S(2)}) collective-permute-start(bf16[2,512,128]{2,1,0:T(8,128)(2,1)S(1)} %get-tuple-element.46), channel_id=1, source_target_pairs={{0,8},{1,5},{2,10},{3,7},{4,12},{5,1},{6,14},{7,3},{8,0},{9,13},{1... | collective-permute-start | bytes 786440 | tf_op jit(solution)/shard_map/ppermute | solution.py:68
  19.7 1.4 %collective-permute-start.6 = (bf16[128,512]{1,0:T(8,128)(2,1)S(1)}, bf16[128,512]{1,0:T(8,128)(2,1)S(1)}, u32[]{:S(2)}, u32[]{:S(2)}) collective-permute-start(bf16[128,512]{1,0:T(8,128)(2,1)S(1)} %slice.28), channel_id=1, source_target_pairs={{0,1},{1,0},{2,3},{3,2},{4,5},{5,4},{6,7},{7,6},{8,9},{9,8},{10,11... | collective-permute-start | bytes 393224 | tf_op jit(solution)/shard_map/ppermute | solution.py:72
  21.6 6.4 %collective-permute-start.8 = (bf16[2,512,128]{2,1,0:T(8,128)(2,1)S(1)}, bf16[2,512,128]{2,1,0:T(8,128)(2,1)S(1)}, u32[]{:S(2)}, u32[]{:S(2)}) collective-permute-start(bf16[2,512,128]{2,1,0:T(8,128)(2,1)S(1)} %get-tuple-element.48), channel_id=1, source_target_pairs={{0,4},{1,9},{2,6},{3,11},{4,0},{5,13},{6,2},{7,15},{8,12},{9,1},{1... | collective-permute-start | bytes 786440 | tf_op jit(solution)/shard_map/ppermute | solution.py:68
  24.1 3.9 %collective-permute-start.7 = (bf16[256,512]{1,0:T(8,128)(2,1)S(1)}, bf16[256,512]{1,0:T(8,128)(2,1)S(1)}, u32[]{:S(2)}, u32[]{:S(2)}) collective-permute-start(bf16[256,512]{1,0:T(8,128)(2,1)S(1)} %get-tuple-element.51), channel_id=1, source_target_pairs={{0,1},{1,0},{2,3},{3,2},{4,5},{5,4},{6,7},{7,6},{8,9},{9,8},{10,11... | collective-permute-start | bytes 786440 | tf_op jit(solution)/shard_map/ppermute | solution.py:72
  24.3 7.3 %collective-permute-start.12 = (bf16[512,128]{1,0:T(8,128)(2,1)S(1)}, bf16[512,128]{1,0:T(8,128)(2,1)S(1)}, u32[]{:S(2)}, u32[]{:S(2)}) collective-permute-start(bf16[512,128]{1,0:T(8,128)(2,1)S(1)} %fusion.3), channel_id=1, source_target_pairs={{0,16},{1,9},{2,18},{3,11},{4,20},{5,13},{6,22},{7,15},{8,24},{9,1... | collective-permute-start | bytes 393224 | tf_op jit(solution)/shard_map/ppermute | solution.py:68
  28.2 5.0 %collective-permute-start.11 = (bf16[512,128]{1,0:T(8,128)(2,1)S(1)}, bf16[512,128]{1,0:T(8,128)(2,1)S(1)}, u32[]{:S(2)}, u32[]{:S(2)}) collective-permute-start(bf16[512,128]{1,0:T(8,128)(2,1)S(1)} %fusion.2), channel_id=1, source_target_pairs={{0,8},{1,5},{2,10},{3,7},{4,12},{5,1},{6,14},{7,3},{8,0},{9,13},{1... | collective-permute-start | bytes 393224 | tf_op jit(solution)/shard_map/ppermute | solution.py:68
  30.1 6.8 %collective-permute-start.10 = (bf16[128,512]{1,0:T(8,128)(2,1)S(1)}, bf16[128,512]{1,0:T(8,128)(2,1)S(1)}, u32[]{:S(2)}, u32[]{:S(2)}) collective-permute-start(bf16[128,512]{1,0:T(8,128)(2,1)S(1)} %slice.55), channel_id=1, source_target_pairs={{0,2},{1,3},{2,0},{3,1},{4,6},{5,7},{6,4},{7,5},{8,10},{9,11},{10,... | collective-permute-start | bytes 393224 | tf_op jit(solution)/shard_map/ppermute | solution.py:72
  31.7 6.0 %collective-permute-start.14 = (bf16[512,128]{1,0:T(8,128)(2,1)S(1)}, bf16[512,128]{1,0:T(8,128)(2,1)S(1)}, u32[]{:S(2)}, u32[]{:S(2)}) collective-permute-start(bf16[512,128]{1,0:T(8,128)(2,1)S(1)} %fusion), channel_id=1, source_target_pairs={{0,4},{1,17},{2,6},{3,19},{4,0},{5,21},{6,2},{7,23},{8,12},{9,25},... | collective-permute-start | bytes 393224 | tf_op jit(solution)/shard_map/ppermute | solution.py:68
  33.3 9.4 %collective-permute-start.13 = (bf16[512,128]{1,0:T(8,128)(2,1)S(1)}, bf16[512,128]{1,0:T(8,128)(2,1)S(1)}, u32[]{:S(2)}, u32[]{:S(2)}) collective-permute-start(bf16[512,128]{1,0:T(8,128)(2,1)S(1)} %fusion.1), channel_id=1, source_target_pairs={{0,16},{1,17},{2,18},{3,19},{4,20},{5,21},{6,22},{7,23},{8,24},{9,... | collective-permute-start | bytes 393224 | tf_op jit(solution)/shard_map/ppermute | solution.py:68
  37.8 7.7 %collective-permute-start.17 = (bf16[512,128]{1,0:T(8,128)(2,1)S(1)}, bf16[512,128]{1,0:T(8,128)(2,1)S(1)}, u32[]{:S(2)}, u32[]{:S(2)}) collective-permute-start(bf16[512,128]{1,0:T(8,128)(2,1)S(1)} %fusion.7.rest_0_), channel_id=1, source_target_pairs={{0,16},{1,9},{2,18},{3,11},{4,20},{5,13},{6,22},{7,15},{8,24},{9,1... | collective-permute-start | bytes 393224 | tf_op jit(solution)/shard_map/ppermute | solution.py:68
  39.4 7.4 %collective-permute-start.16 = (bf16[512,128]{1,0:T(8,128)(2,1)S(1)}, bf16[512,128]{1,0:T(8,128)(2,1)S(1)}, u32[]{:S(2)}, u32[]{:S(2)}) collective-permute-start(bf16[512,128]{1,0:T(8,128)(2,1)S(1)} %fusion.7.rest_0_), channel_id=1, source_target_pairs={{0,8},{1,5},{2,10},{3,7},{4,12},{5,1},{6,14},{7,3},{8,0},{9,13},{1... | collective-permute-start | bytes 393224 | tf_op jit(solution)/shard_map/ppermute | solution.py:68
  42.7 6.2 %collective-permute-start.15 = (bf16[512,128]{1,0:T(8,128)(2,1)S(1)}, bf16[512,128]{1,0:T(8,128)(2,1)S(1)}, u32[]{:S(2)}, u32[]{:S(2)}) collective-permute-start(bf16[512,128]{1,0:T(8,128)(2,1)S(1)} %fusion.8.rest_0_), channel_id=1, source_target_pairs={{0,8},{1,5},{2,10},{3,7},{4,12},{5,1},{6,14},{7,3},{8,0},{9,13},{1... | collective-permute-start | bytes 393224 | tf_op jit(solution)/shard_map/ppermute | solution.py:68
  44.6 5.9 %collective-permute-start.20 = (bf16[512,128]{1,0:T(8,128)(2,1)S(1)}, bf16[512,128]{1,0:T(8,128)(2,1)S(1)}, u32[]{:S(2)}, u32[]{:S(2)}) collective-permute-start(bf16[512,128]{1,0:T(8,128)(2,1)S(1)} %fusion.8.rest_0_), channel_id=1, source_target_pairs={{0,4},{1,9},{2,6},{3,11},{4,0},{5,13},{6,2},{7,15},{8,12},{9,1},{1... | collective-permute-start | bytes 393224 | tf_op jit(solution)/shard_map/ppermute | solution.py:68
  45.4 7.3 %collective-permute-start.19 = (bf16[512,128]{1,0:T(8,128)(2,1)S(1)}, bf16[512,128]{1,0:T(8,128)(2,1)S(1)}, u32[]{:S(2)}, u32[]{:S(2)}) collective-permute-start(bf16[512,128]{1,0:T(8,128)(2,1)S(1)} %collective-permute-done.17.rest_1_), channel_id=1, source_target_pairs={{0,8},{1,5},{2,10},{3,7},{4,12},{5,1},{6,14},{7,3},{8,0},{9,13},{1... | collective-permute-start | bytes 393224 | tf_op jit(solution)/shard_map/ppermute | solution.py:68
  49.0 5.0 %collective-permute-start.18 = (bf16[512,128]{1,0:T(8,128)(2,1)S(1)}, bf16[512,128]{1,0:T(8,128)(2,1)S(1)}, u32[]{:S(2)}, u32[]{:S(2)}) collective-permute-start(bf16[512,128]{1,0:T(8,128)(2,1)S(1)} %collective-permute-done.15.rest_1_), channel_id=1, source_target_pairs={{0,4},{1,9},{2,6},{3,11},{4,0},{5,13},{6,2},{7,15},{8,12},{9,1},{1... | collective-permute-start | bytes 393224 | tf_op jit(solution)/shard_map/ppermute | solution.py:68

commit v5 on v4

--- a/solution.py
+++ b/solution.py
@@ -297,17 +297,13 @@
     for k in range(count):
         totals.append(state[k][0] + after(got[k], latest).astype(F32))
         latest = totals[-1]
-    pair = keep + after(got_core, latest).astype(F32)
-    got_x = swap(pair[rows:].astype(BF16), mask=over)
-    latest = pair
     got = [summed(total[1].astype(BF16), chunk=k, stage=1) for k, total in enumerate(totals)]
     for k in range(count):
         totals[k] = totals[k][0] + after(got[k], latest).astype(F32)
         latest = totals[k]
-    (keys,) = call(
-        finish_keys, [((rows, KV), BF16)], pair[:rows], after(got_x, latest), inv_rms, cosine, sine
-    )
-    latest = keys
+    pair = keep + after(got_core, latest).astype(F32)
+    got_x = swap(pair[rows:].astype(BF16), mask=over)
+    latest = pair
     for stage in range(2, wide_size.bit_length() - 1):
         rounded = [total.astype(BF16) for total in totals]
         got = [summed(value, chunk=k, stage=stage) for k, value in enumerate(rounded)]
@@ -317,19 +313,28 @@
     mine = [total.astype(BF16) for total in totals]
     near = [summed(value, chunk=k, stage=1) for k, value in enumerate(mine)]
     far = [summed(value, chunk=k, stage=0) for k, value in enumerate(mine)]
+    def write(k, half, parts):
+        start, size = chunks[k]
+        final = half == 1 and k == count - 1
+        return write_weights(
+            start, size, k, wide_size, grad_scale, half, final, gain_row, key_weight, parts, before
+        )
+
+    before = ()
+    last = []
     for k in range(count):
         near[k] = after(near[k], latest)
-        far[k] = latest = after(far[k], near[k])
-    last = [summed(value, chunk=k, stage=0) for k, value in enumerate(near)]
-    before = ()
-    for half in range(2):
-        for k, (start, size) in enumerate(chunks):
-            parts = (after(last[k], latest),) if half else (mine[k], near[k], after(far[k], latest))
-            before = write_weights(
-                start, size, k, wide_size, grad_scale, half, half == 1 and k == count - 1,
-                gain_row, key_weight, parts, before,
-            )
-            latest = before[1]
+        last.append(summed(near[k], chunk=k, stage=0))
+        far[k] = after(far[k], near[k])
+        before = write(k, 0, (mine[k], near[k], far[k]))
+        latest = before[1]
+    (keys,) = call(
+        finish_keys, [((rows, KV), BF16)], pair[:rows], after(got_x, latest), inv_rms, cosine, sine
+    )
+    latest = keys
+    for k in range(count):
+        before = write(k, 1, (after(last[k], latest),))
+        latest = before[1]
     weight_grad, gain_grad = before
     return keys, weight_grad, gain_grad.reshape(own)
 

time: 55 us -> 54.7 us (level)
  waiting for transfers between devices: 16.4 us -> 13.6 us
  starting transfers between devices: 27.7 us -> 30.2 us
    ppermute x12, waiting for transfers between devices: 7.49 us -> 4.69 us  [swap_wide(): return lax.ppermute(value, BOTH, pairs)]
    ppermute x12, starting transfers between devices: 20.4 us -> 22.8 us  [swap_wide(): return lax.ppermute(value, BOTH, pairs)]
  transfers between devices with their start and end apart: 21 -> 21, of which waited for: 12 -> 11; matrix products, arithmetic and copies ran while one was open for 2% -> 2% of each run, Pallas kernels for 11% -> 11%
where the time goes in v5:
time: 54.7 us; the launch traced here: 54.5 us
  starting transfers between devices  30.2 us (55%)
  waiting for transfers between devices  13.6 us (25%)
  Pallas kernels  6.86 us (13%)
  local copies, waits for them, and re-layouts  2.22 us (4%)
  between operations  0.91 us (2%)
  other arithmetic  0.75 us (1%)
    ppermute x12, starting transfers between devices, swap_wide(): return lax.ppermute(value, BOTH, pairs)  22.8 us
    ppermute x9, waiting for transfers between devices, swap_narrow(): lax.ppermute(value, 'narrow', [(i, i ^ mask) for i in range(narrow_size)])  8.87 us
    ppermute x9, starting transfers between devices, swap_narrow(): lax.ppermute(value, 'narrow', [(i, i ^ mask) for i in range(narrow_size)])  7.42 us
    pallas_call x10, Pallas kernels, call(): pl.pallas_call(body, out_shape=[jax.ShapeDtypeStruct(shape, kind) for sha...  6.86 us
    ppermute x12, waiting for transfers between devices, swap_wide(): return lax.ppermute(value, BOTH, pairs)  4.69 us
    unnamed x10, local copies, waits for them, and re-layouts  2.13 us
  transfers between devices with their start and end apart: 21, of which 11 were waited for; matrix products, arithmetic and copies ran while one was open for 2% of the time, Pallas kernels for 11%

profile of v5, /device:TPU:0, one launch (start us, length us, event | category | flops | bytes accessed | tf_op | source)
XLA Modules:
  0.0 54.5 jit_solution(15480582183147798667)
XLA Ops:
  0.6 1.2 %copy-done.1 = bf16[128,4096]{1,0:T(8,128)(2,1)S(1)} copy-done((bf16[128,4096]{1,0:T(8,128)(2,1)S(1)}, bf16[128,4096]{1,0:T(8,128)(2,1)}, u32[]{:S(2)}) %copy-start.1) | copy-done | bytes 1048600
  1.9 3.0 %collective-permute-start.2 = (bf16[128,1024]{1,0:T(8,128)(2,1)S(1)}, bf16[128,1024]{1,0:T(8,128)(2,1)S(1)}, u32[]{:S(2)}, u32[]{:S(2)}) collective-permute-start(bf16[128,1024]{1,0:T(8,128)(2,1)S(1)} %shard_map.67), channel_id=1, source_target_pairs={{0,2},{1,3},{2,0},{3,1},{4,6},{5,7},{6,4},{7,5},{8,10},{9,11},{10,... | collective-permute-start | bytes 786440 | tf_op jit(solution)/shard_map/ppermute | solution.py:72
  5.4 0.9 %copy-done.3 = bf16[128,512]{1,0:T(8,128)(2,1)S(1)} copy-done((bf16[128,512]{1,0:T(8,128)(2,1)S(1)}, bf16[128,512]{1,0:T(8,128)(2,1)}, u32[]{:S(2)}) %copy-start.3) | copy-done | bytes 131096
  6.7 0.7 %collective-permute-start.4 = (bf16[128,512]{1,0:T(8,128)(2,1)S(1)}, bf16[128,512]{1,0:T(8,128)(2,1)S(1)}, u32[]{:S(2)}, u32[]{:S(2)}) collective-permute-start(bf16[128,512]{1,0:T(8,128)(2,1)S(1)} %get-tuple-element.43.scaled_ref), channel_id=1, source_target_pairs={{0,2},{1,3},{2,0},{3,1},{4,6},{5,7},{6,4},{7,5},{8,10},{9,11},{10,... | collective-permute-start | bytes 393224 | tf_op jit(solution)/shard_map/ppermute | solution.py:72
  7.4 1.4 %collective-permute-start.1 = (bf16[128,1024]{1,0:T(8,128)(2,1)S(1)}, bf16[128,1024]{1,0:T(8,128)(2,1)S(1)}, u32[]{:S(2)}, u32[]{:S(2)}) collective-permute-start(bf16[128,1024]{1,0:T(8,128)(2,1)S(1)} %get-tuple-element.42), channel_id=1, source_target_pairs={{0,2},{1,3},{2,0},{3,1},{4,6},{5,7},{6,4},{7,5},{8,10},{9,11},{10,... | collective-permute-start | bytes 786440 | tf_op jit(solution)/shard_map/ppermute | solution.py:72
  8.8 6.0 %collective-permute-done.4.x_grad = bf16[128,512]{1,0:T(8,128)(2,1)S(1)} collective-permute-done((bf16[128,512]{1,0:T(8,128)(2,1)S(1)}, bf16[128,512]{1,0:T(8,128)(2,1)S(1)}, u32[]{:S(2)}, u32[]{:S(2)}) %collective-permute-start.4) | collective-permute-done | bytes 131104 | tf_op jit(solution)/shard_map/ppermute | solution.py:72
  14.9 0.6 %collective-permute-start.3 = (bf16[128,512]{1,0:T(8,128)(2,1)S(1)}, bf16[128,512]{1,0:T(8,128)(2,1)S(1)}, u32[]{:S(2)}, u32[]{:S(2)}) collective-permute-start(bf16[128,512]{1,0:T(8,128)(2,1)S(1)} %slice.35), channel_id=1, source_target_pairs={{0,1},{1,0},{2,3},{3,2},{4,5},{5,4},{6,7},{7,6},{8,9},{9,8},{10,11... | collective-permute-start | bytes 393224 | tf_op jit(solution)/shard_map/ppermute | solution.py:72
  15.5 0.8 %collective-permute-done.5.last_grad = bf16[128,512]{1,0:T(8,128)(2,1)S(1)} collective-permute-done((bf16[128,512]{1,0:T(8,128)(2,1)S(1)}, bf16[128,512]{1,0:T(8,128)(2,1)S(1)}, u32[]{:S(2)}, u32[]{:S(2)}) %collective-permute-start.5) | collective-permute-done | bytes 131104 | tf_op jit(solution)/shard_map/ppermute | solution.py:72
  17.0 2.2 %collective-permute-start.9 = (bf16[2,512,128]{2,1,0:T(8,128)(2,1)S(1)}, bf16[2,512,128]{2,1,0:T(8,128)(2,1)S(1)}, u32[]{:S(2)}, u32[]{:S(2)}) collective-permute-start(bf16[2,512,128]{2,1,0:T(8,128)(2,1)S(1)} %get-tuple-element.44), channel_id=1, source_target_pairs={{0,8},{1,5},{2,10},{3,7},{4,12},{5,1},{6,14},{7,3},{8,0},{9,13},{1... | collective-permute-start | bytes 786440 | tf_op jit(solution)/shard_map/ppermute | solution.py:68
  19.8 1.3 %collective-permute-done.6.last_ref.rest_3_ = bf16[128,512]{1,0:T(8,128)(2,1)S(1)} collective-permute-done((bf16[128,512]{1,0:T(8,128)(2,1)S(1)}, bf16[128,512]{1,0:T(8,128)(2,1)S(1)}, u32[]{:S(2)}, u32[]{:S(2)}) %collective-permute-start.6) | collective-permute-done | bytes 131104 | tf_op jit(solution)/shard_map/ppermute | solution.py:72
  21.6 1.8 %collective-permute-start.8 = (bf16[2,512,128]{2,1,0:T(8,128)(2,1)S(1)}, bf16[2,512,128]{2,1,0:T(8,128)(2,1)S(1)}, u32[]{:S(2)}, u32[]{:S(2)}) collective-permute-start(bf16[2,512,128]{2,1,0:T(8,128)(2,1)S(1)} %get-tuple-element.46), channel_id=1, source_target_pairs={{0,4},{1,9},{2,6},{3,11},{4,0},{5,13},{6,2},{7,15},{8,12},{9,1},{1... | collective-permute-start | bytes 786440 | tf_op jit(solution)/shard_map/ppermute | solution.py:68
  23.4 0.7 %shard_map.71 = (f32[256,512]{1,0:T(8,128)S(1)}, bf16[256,512]{1,0:T(8,128)(2,1)S(1)}) custom-call(bf16[1,1024]{1,0:T(2,128)(2,1)S(1)} %reshape.35.gain_ref, bf16[1024,512]{1,0:T(8,128)(2,1)S(1)} %copy-done, bf16[128,1024]{1,0:T(8,128)(2,1)S(1)} %get-tuple-element.40.own_ref, bf16[128,1536]{1,0:T(8,128)(2,1)S(1)} %collective-permute-done.core_ref, ...), custom_call_target="tpu_custom_call" | custom-call | tf_op jit(solution)/shard_map/pallas_call | solution.py:82
  24.3 2.7 %collective-permute-start.11 = (bf16[512,128]{1,0:T(8,128)(2,1)S(1)}, bf16[512,128]{1,0:T(8,128)(2,1)S(1)}, u32[]{:S(2)}, u32[]{:S(2)}) collective-permute-start(bf16[512,128]{1,0:T(8,128)(2,1)S(1)} %fusion.3), channel_id=1, source_target_pairs={{0,16},{1,9},{2,18},{3,11},{4,20},{5,13},{6,22},{7,15},{8,24},{9,1... | collective-permute-start | bytes 393224 | tf_op jit(solution)/shard_map/ppermute | solution.py:68
  27.0 1.0 %collective-permute-done.8 = bf16[2,512,128]{2,1,0:T(8,128)(2,1)S(1)} collective-permute-done((bf16[2,512,128]{2,1,0:T(8,128)(2,1)S(1)}, bf16[2,512,128]{2,1,0:T(8,128)(2,1)S(1)}, u32[]{:S(2)}, u32[]{:S(2)}) %collective-permute-start.8) | collective-permute-done | bytes 262176 | tf_op jit(solution)/shard_map/ppermute | solution.py:68
  28.1 1.9 %collective-permute-start.10 = (bf16[512,128]{1,0:T(8,128)(2,1)S(1)}, bf16[512,128]{1,0:T(8,128)(2,1)S(1)}, u32[]{:S(2)}, u32[]{:S(2)}) collective-permute-start(bf16[512,128]{1,0:T(8,128)(2,1)S(1)} %fusion.2), channel_id=1, source_target_pairs={{0,8},{1,5},{2,10},{3,7},{4,12},{5,1},{6,14},{7,3},{8,0},{9,13},{1... | collective-permute-start | bytes 393224 | tf_op jit(solution)/shard_map/ppermute | solution.py:68
  30.0 0.7 %collective-permute-done.11 = bf16[512,128]{1,0:T(8,128)(2,1)S(1)} collective-permute-done((bf16[512,128]{1,0:T(8,128)(2,1)S(1)}, bf16[512,128]{1,0:T(8,128)(2,1)S(1)}, u32[]{:S(2)}, u32[]{:S(2)}) %collective-permute-start.11) | collective-permute-done | bytes 131104 | tf_op jit(solution)/shard_map/ppermute | solution.py:68
  30.8 1.5 %collective-permute-start.14 = (bf16[512,128]{1,0:T(8,128)(2,1)S(1)}, bf16[512,128]{1,0:T(8,128)(2,1)S(1)}, u32[]{:S(2)}, u32[]{:S(2)}) collective-permute-start(bf16[512,128]{1,0:T(8,128)(2,1)S(1)} %fusion), channel_id=1, source_target_pairs={{0,4},{1,17},{2,6},{3,19},{4,0},{5,21},{6,2},{7,23},{8,12},{9,25},... | collective-permute-start | bytes 393224 | tf_op jit(solution)/shard_map/ppermute | solution.py:68
  32.3 0.9 %collective-permute-done.10 = bf16[512,128]{1,0:T(8,128)(2,1)S(1)} collective-permute-done((bf16[512,128]{1,0:T(8,128)(2,1)S(1)}, bf16[512,128]{1,0:T(8,128)(2,1)S(1)}, u32[]{:S(2)}, u32[]{:S(2)}) %collective-permute-start.10) | collective-permute-done | bytes 131104 | tf_op jit(solution)/shard_map/ppermute | solution.py:68
  33.2 4.0 %collective-permute-start.13 = (bf16[512,128]{1,0:T(8,128)(2,1)S(1)}, bf16[512,128]{1,0:T(8,128)(2,1)S(1)}, u32[]{:S(2)}, u32[]{:S(2)}) collective-permute-start(bf16[512,128]{1,0:T(8,128)(2,1)S(1)} %fusion.1), channel_id=1, source_target_pairs={{0,16},{1,17},{2,18},{3,19},{4,20},{5,21},{6,22},{7,23},{8,24},{9,... | collective-permute-start | bytes 393224 | tf_op jit(solution)/shard_map/ppermute | solution.py:68
  37.3 1.6 %collective-permute-start.17 = (bf16[512,128]{1,0:T(8,128)(2,1)S(1)}, bf16[512,128]{1,0:T(8,128)(2,1)S(1)}, u32[]{:S(2)}, u32[]{:S(2)}) collective-permute-start(bf16[512,128]{1,0:T(8,128)(2,1)S(1)} %fusion.7.rest_0_), channel_id=1, source_target_pairs={{0,8},{1,5},{2,10},{3,7},{4,12},{5,1},{6,14},{7,3},{8,0},{9,13},{1... | collective-permute-start | bytes 393224 | tf_op jit(solution)/shard_map/ppermute | solution.py:68
  39.0 1.9 %collective-permute-start.16 = (bf16[512,128]{1,0:T(8,128)(2,1)S(1)}, bf16[512,128]{1,0:T(8,128)(2,1)S(1)}, u32[]{:S(2)}, u32[]{:S(2)}) collective-permute-start(bf16[512,128]{1,0:T(8,128)(2,1)S(1)} %fusion.7.rest_0_), channel_id=1, source_target_pairs={{0,16},{1,9},{2,18},{3,11},{4,20},{5,13},{6,22},{7,15},{8,24},{9,1... | collective-permute-start | bytes 393224 | tf_op jit(solution)/shard_map/ppermute | solution.py:68
  40.9 1.2 %collective-permute-done.13 = bf16[512,128]{1,0:T(8,128)(2,1)S(1)} collective-permute-done((bf16[512,128]{1,0:T(8,128)(2,1)S(1)}, bf16[512,128]{1,0:T(8,128)(2,1)S(1)}, u32[]{:S(2)}, u32[]{:S(2)}) %collective-permute-start.13) | collective-permute-done | bytes 131104 | tf_op jit(solution)/shard_map/ppermute | solution.py:68
  42.7 1.3 %collective-permute-start.18 = (bf16[512,128]{1,0:T(8,128)(2,1)S(1)}, bf16[512,128]{1,0:T(8,128)(2,1)S(1)}, u32[]{:S(2)}, u32[]{:S(2)}) collective-permute-start(bf16[512,128]{1,0:T(8,128)(2,1)S(1)} %fusion.8.rest_0_), channel_id=1, source_target_pairs={{0,4},{1,9},{2,6},{3,11},{4,0},{5,13},{6,2},{7,15},{8,12},{9,1},{1... | collective-permute-start | bytes 393224 | tf_op jit(solution)/shard_map/ppermute | solution.py:68
  44.0 1.5 %collective-permute-start.12 = (bf16[128,512]{1,0:T(8,128)(2,1)S(1)}, bf16[128,512]{1,0:T(8,128)(2,1)S(1)}, u32[]{:S(2)}, u32[]{:S(2)}) collective-permute-start(bf16[128,512]{1,0:T(8,128)(2,1)S(1)} %slice.55), channel_id=1, source_target_pairs={{0,2},{1,3},{2,0},{3,1},{4,6},{5,7},{6,4},{7,5},{8,10},{9,11},{10,... | collective-permute-start | bytes 393224 | tf_op jit(solution)/shard_map/ppermute | solution.py:72
  45.6 1.8 %collective-permute-start.20 = (bf16[512,128]{1,0:T(8,128)(2,1)S(1)}, bf16[512,128]{1,0:T(8,128)(2,1)S(1)}, u32[]{:S(2)}, u32[]{:S(2)}) collective-permute-start(bf16[512,128]{1,0:T(8,128)(2,1)S(1)} %collective-permute-done.16.rest_1_), channel_id=1, source_target_pairs={{0,8},{1,5},{2,10},{3,7},{4,12},{5,1},{6,14},{7,3},{8,0},{9,13},{1... | collective-permute-start | bytes 393224 | tf_op jit(solution)/shard_map/ppermute | solution.py:68
  47.5 1.1 %shard_map.72 = (f32[1024,512]{1,0:T(8,128)}, f32[8,128]{1,0:T(8,128)S(1)}) custom-call(bf16[1,1024]{1,0:T(2,128)(2,1)S(1)} %reshape.35.gain_ref, bf16[1024,512]{1,0:T(8,128)(2,1)S(1)} %copy-done, bf16[512,128]{1,0:T(8,128)(2,1)S(1)} %fusion.7.rest_0_, bf16[512,128]{1,0:T(8,128)(2,1)S(1)} %collective-permute-done.16.rest_1_, ...), custom_call_target="tpu_custom_call" | custom-call | tf_op jit(solution)/shard_map/pallas_call | solution.py:82
  48.6 1.5 %collective-permute-start.19 = (bf16[512,128]{1,0:T(8,128)(2,1)S(1)}, bf16[512,128]{1,0:T(8,128)(2,1)S(1)}, u32[]{:S(2)}, u32[]{:S(2)}) collective-permute-start(bf16[512,128]{1,0:T(8,128)(2,1)S(1)} %collective-permute-done.15.rest_1_), channel_id=1, source_target_pairs={{0,4},{1,9},{2,6},{3,11},{4,0},{5,13},{6,2},{7,15},{8,12},{9,1},{1... | collective-permute-start | bytes 393224 | tf_op jit(solution)/shard_map/ppermute | solution.py:68
  50.1 1.1 %shard_map.73 = (f32[1024,512]{1,0:T(8,128)}, f32[8,128]{1,0:T(8,128)S(1)}) custom-call(bf16[1,1024]{1,0:T(2,128)(2,1)S(1)} %reshape.35.gain_ref, bf16[1024,512]{1,0:T(8,128)(2,1)S(1)} %copy-done, bf16[512,128]{1,0:T(8,128)(2,1)S(1)} %fusion.8.rest_0_, bf16[512,128]{1,0:T(8,128)(2,1)S(1)} %collective-permute-done.15.rest_1_, ...), custom_call_target="tpu_custom_call", output_to_operand_aliasing={{0}: (5, {})} | custom-call | tf_op jit(solution)/shard_map/pallas_call | solution.py:82
  51.2 0.8 %shard_map.74 = bf16[128,512]{1,0:T(8,128)(2,1)} custom-call(f32[128,512]{1,0:T(8,128)S(1)} %slice.40.mine_ref, bf16[128,512]{1,0:T(8,128)(2,1)S(1)} %collective-permute-done.12.got_ref, f32[128,128]{1,0:T(8,128)S(1)} %get-tuple-element.67.inv_ref, f32[128,128]{1,0:T(8,128)S(1)} %get-tuple-element.78.cos_ref, f32[128,128]{1,0:T(8,128)S(1)} %get-tuple-element.79.sin_ref), custom_call_target="tpu_custom_call" | custom-call | tf_op jit(solution)/shard_map/pallas_call | solution.py:82
  52.0 0.9 %shard_map.75 = (f32[1024,512]{1,0:T(8,128)}, f32[8,128]{1,0:T(8,128)S(1)}) custom-call(bf16[1,1024]{1,0:T(2,128)(2,1)S(1)} %reshape.35.gain_ref, bf16[1024,512]{1,0:T(8,128)(2,1)S(1)} %copy-done, bf16[512,128]{1,0:T(8,128)(2,1)S(1)} %collective-permute-done.20.rest_0_, f32[1024,512]{1,0:T(8,128)} %get-tuple-element.69.rest_1_, ...), custom_call_target="tpu_custom_call", output_to_operand_aliasing={{0}: (3, {})} | custom-call | tf_op jit(solution)/shard_map/pallas_call | solution.py:82
  52.9 0.7 %collective-permute-done.19.rest_0_ = bf16[512,128]{1,0:T(8,128)(2,1)S(1)} collective-permute-done((bf16[512,128]{1,0:T(8,128)(2,1)S(1)}, bf16[512,128]{1,0:T(8,128)(2,1)S(1)}, u32[]{:S(2)}, u32[]{:S(2)}) %collective-permute-start.19) | collective-permute-done | bytes 131104 | tf_op jit(solution)/shard_map/ppermute | solution.py:68
  53.6 0.9 %shard_map.76 = (f32[1024,512]{1,0:T(8,128)}, f32[8,128]{1,0:T(8,128)}) custom-call(bf16[1,1024]{1,0:T(2,128)(2,1)S(1)} %reshape.35.gain_ref, bf16[1024,512]{1,0:T(8,128)(2,1)S(1)} %copy-done, bf16[512,128]{1,0:T(8,128)(2,1)S(1)} %collective-permute-done.19.rest_0_, f32[1024,512]{1,0:T(8,128)} %get-tuple-element.72.rest_1_, ...), custom_call_target="tpu_custom_call", output_to_operand_aliasing={{0}: (3, {})} | custom-call | tf_op jit(solution)/shard_map/pallas_call | solution.py:82
  (48 shorter events, 3.9 us)
Async XLA Ops:
  0.6 1.2 %copy-start.1 = (bf16[128,4096]{1,0:T(8,128)(2,1)S(1)}, bf16[128,4096]{1,0:T(8,128)(2,1)}, u32[]{:S(2)}) copy-start(bf16[128,4096]{1,0:T(8,128)(2,1)} %tok_ref.2) | copy-start | bytes 3145732
  1.9 3.5 %copy-start.2 = (bf16[128,4096]{1,0:T(8,128)(2,1)S(1)}, bf16[128,4096]{1,0:T(8,128)(2,1)}, u32[]{:S(2)}) copy-start(bf16[128,4096]{1,0:T(8,128)(2,1)} %tok_ref.2) | copy-start | bytes 3145732
  1.9 17.8 %copy-start.4 = (bf16[1024]{0:T(1024)(128)(2,1)S(1)}, bf16[1024]{0:T(1024)(128)(2,1)}, u32[]{:S(2)}) copy-start(bf16[1024]{0:T(1024)(128)(2,1)} %param.5) | copy-start | bytes 6148
  1.9 13.0 %collective-permute-start.2 = (bf16[128,1024]{1,0:T(8,128)(2,1)S(1)}, bf16[128,1024]{1,0:T(8,128)(2,1)S(1)}, u32[]{:S(2)}, u32[]{:S(2)}) collective-permute-start(bf16[128,1024]{1,0:T(8,128)(2,1)S(1)} %shard_map.67), channel_id=1, source_target_pairs={{0,2},{1,3},{2,0},{3,1},{4,6},{5,7},{6,4},{7,5},{8,10},{9,11},{10,... | collective-permute-start | bytes 786440 | tf_op jit(solution)/shard_map/ppermute | solution.py:72
  5.4 0.9 %copy-start.3 = (bf16[128,512]{1,0:T(8,128)(2,1)S(1)}, bf16[128,512]{1,0:T(8,128)(2,1)}, u32[]{:S(2)}) copy-start(bf16[128,512]{1,0:T(8,128)(2,1)} %grad_ref.1) | copy-start | bytes 393220
  6.3 17.1 %copy-start = (bf16[1024,512]{1,0:T(8,128)(2,1)S(1)}, bf16[1024,512]{1,0:T(8,128)(2,1)}, u32[]{:S(2)}) copy-start(bf16[1024,512]{1,0:T(8,128)(2,1)} %weight_ref.8) | copy-start | bytes 3145732
  6.7 9.8 %collective-permute-start = (bf16[128,1536]{1,0:T(8,128)(2,1)S(1)}, bf16[128,1536]{1,0:T(8,128)(2,1)S(1)}, u32[]{:S(2)}, u32[]{:S(2)}) collective-permute-start(bf16[128,1536]{1,0:T(8,128)(2,1)S(1)} %get-tuple-element.41), channel_id=1, source_target_pairs={{0,1},{1,0},{2,3},{3,2},{4,5},{5,4},{6,7},{7,6},{8,9},{9,8},{10,11... | collective-permute-start | bytes 1179656 | tf_op jit(solution)/shard_map/ppermute | solution.py:72
  6.7 8.1 %collective-permute-start.4 = (bf16[128,512]{1,0:T(8,128)(2,1)S(1)}, bf16[128,512]{1,0:T(8,128)(2,1)S(1)}, u32[]{:S(2)}, u32[]{:S(2)}) collective-permute-start(bf16[128,512]{1,0:T(8,128)(2,1)S(1)} %get-tuple-element.43.scaled_ref), channel_id=1, source_target_pairs={{0,2},{1,3},{2,0},{3,1},{4,6},{5,7},{6,4},{7,5},{8,10},{9,11},{10,... | collective-permute-start | bytes 393224 | tf_op jit(solution)/shard_map/ppermute | solution.py:72
  7.4 12.3 %collective-permute-start.1 = (bf16[128,1024]{1,0:T(8,128)(2,1)S(1)}, bf16[128,1024]{1,0:T(8,128)(2,1)S(1)}, u32[]{:S(2)}, u32[]{:S(2)}) collective-permute-start(bf16[128,1024]{1,0:T(8,128)(2,1)S(1)} %get-tuple-element.42), channel_id=1, source_target_pairs={{0,2},{1,3},{2,0},{3,1},{4,6},{5,7},{6,4},{7,5},{8,10},{9,11},{10,... | collective-permute-start | bytes 786440 | tf_op jit(solution)/shard_map/ppermute | solution.py:72
  14.9 1.3 %collective-permute-start.5 = (bf16[128,512]{1,0:T(8,128)(2,1)S(1)}, bf16[128,512]{1,0:T(8,128)(2,1)S(1)}, u32[]{:S(2)}, u32[]{:S(2)}) collective-permute-start(bf16[128,512]{1,0:T(8,128)(2,1)S(1)} %collective-permute-done.4.x_grad), channel_id=1, source_target_pairs={{0,1},{1,0},{2,3},{3,2},{4,5},{5,4},{6,7},{7,6},{8,9},{9,8},{10,11... | collective-permute-start | bytes 393224 | tf_op jit(solution)/shard_map/ppermute | solution.py:72
  14.9 1.6 %collective-permute-start.3 = (bf16[128,512]{1,0:T(8,128)(2,1)S(1)}, bf16[128,512]{1,0:T(8,128)(2,1)S(1)}, u32[]{:S(2)}, u32[]{:S(2)}) collective-permute-start(bf16[128,512]{1,0:T(8,128)(2,1)S(1)} %slice.35), channel_id=1, source_target_pairs={{0,1},{1,0},{2,3},{3,2},{4,5},{5,4},{6,7},{7,6},{8,9},{9,8},{10,11... | collective-permute-start | bytes 393224 | tf_op jit(solution)/shard_map/ppermute | solution.py:72
  17.0 7.3 %collective-permute-start.9 = (bf16[2,512,128]{2,1,0:T(8,128)(2,1)S(1)}, bf16[2,512,128]{2,1,0:T(8,128)(2,1)S(1)}, u32[]{:S(2)}, u32[]{:S(2)}) collective-permute-start(bf16[2,512,128]{2,1,0:T(8,128)(2,1)S(1)} %get-tuple-element.44), channel_id=1, source_target_pairs={{0,8},{1,5},{2,10},{3,7},{4,12},{5,1},{6,14},{7,3},{8,0},{9,13},{1... | collective-permute-start | bytes 786440 | tf_op jit(solution)/shard_map/ppermute | solution.py:68
  19.7 1.4 %collective-permute-start.6 = (bf16[128,512]{1,0:T(8,128)(2,1)S(1)}, bf16[128,512]{1,0:T(8,128)(2,1)S(1)}, u32[]{:S(2)}, u32[]{:S(2)}) collective-permute-start(bf16[128,512]{1,0:T(8,128)(2,1)S(1)} %slice.28), channel_id=1, source_target_pairs={{0,1},{1,0},{2,3},{3,2},{4,5},{5,4},{6,7},{7,6},{8,9},{9,8},{10,11... | collective-permute-start | bytes 393224 | tf_op jit(solution)/shard_map/ppermute | solution.py:72
  21.6 6.4 %collective-permute-start.8 = (bf16[2,512,128]{2,1,0:T(8,128)(2,1)S(1)}, bf16[2,512,128]{2,1,0:T(8,128)(2,1)S(1)}, u32[]{:S(2)}, u32[]{:S(2)}) collective-permute-start(bf16[2,512,128]{2,1,0:T(8,128)(2,1)S(1)} %get-tuple-element.46), channel_id=1, source_target_pairs={{0,4},{1,9},{2,6},{3,11},{4,0},{5,13},{6,2},{7,15},{8,12},{9,1},{1... | collective-permute-start | bytes 786440 | tf_op jit(solution)/shard_map/ppermute | solution.py:68
  24.1 13.0 %collective-permute-start.7 = (bf16[256,512]{1,0:T(8,128)(2,1)S(1)}, bf16[256,512]{1,0:T(8,128)(2,1)S(1)}, u32[]{:S(2)}, u32[]{:S(2)}) collective-permute-start(bf16[256,512]{1,0:T(8,128)(2,1)S(1)} %get-tuple-element.49), channel_id=1, source_target_pairs={{0,1},{1,0},{2,3},{3,2},{4,5},{5,4},{6,7},{7,6},{8,9},{9,8},{10,11... | collective-permute-start | bytes 786440 | tf_op jit(solution)/shard_map/ppermute | solution.py:72
  24.3 6.4 %collective-permute-start.11 = (bf16[512,128]{1,0:T(8,128)(2,1)S(1)}, bf16[512,128]{1,0:T(8,128)(2,1)S(1)}, u32[]{:S(2)}, u32[]{:S(2)}) collective-permute-start(bf16[512,128]{1,0:T(8,128)(2,1)S(1)} %fusion.3), channel_id=1, source_target_pairs={{0,16},{1,9},{2,18},{3,11},{4,20},{5,13},{6,22},{7,15},{8,24},{9,1... | collective-permute-start | bytes 393224 | tf_op jit(solution)/shard_map/ppermute | solution.py:68
  28.1 5.0 %collective-permute-start.10 = (bf16[512,128]{1,0:T(8,128)(2,1)S(1)}, bf16[512,128]{1,0:T(8,128)(2,1)S(1)}, u32[]{:S(2)}, u32[]{:S(2)}) collective-permute-start(bf16[512,128]{1,0:T(8,128)(2,1)S(1)} %fusion.2), channel_id=1, source_target_pairs={{0,8},{1,5},{2,10},{3,7},{4,12},{5,1},{6,14},{7,3},{8,0},{9,13},{1... | collective-permute-start | bytes 393224 | tf_op jit(solution)/shard_map/ppermute | solution.py:68
  30.8 6.5 %collective-permute-start.14 = (bf16[512,128]{1,0:T(8,128)(2,1)S(1)}, bf16[512,128]{1,0:T(8,128)(2,1)S(1)}, u32[]{:S(2)}, u32[]{:S(2)}) collective-permute-start(bf16[512,128]{1,0:T(8,128)(2,1)S(1)} %fusion), channel_id=1, source_target_pairs={{0,4},{1,17},{2,6},{3,19},{4,0},{5,21},{6,2},{7,23},{8,12},{9,25},... | collective-permute-start | bytes 393224 | tf_op jit(solution)/shard_map/ppermute | solution.py:68
  33.2 9.0 %collective-permute-start.13 = (bf16[512,128]{1,0:T(8,128)(2,1)S(1)}, bf16[512,128]{1,0:T(8,128)(2,1)S(1)}, u32[]{:S(2)}, u32[]{:S(2)}) collective-permute-start(bf16[512,128]{1,0:T(8,128)(2,1)S(1)} %fusion.1), channel_id=1, source_target_pairs={{0,16},{1,17},{2,18},{3,19},{4,20},{5,21},{6,22},{7,23},{8,24},{9,... | collective-permute-start | bytes 393224 | tf_op jit(solution)/shard_map/ppermute | solution.py:68
  37.3 10.1 %collective-permute-start.17 = (bf16[512,128]{1,0:T(8,128)(2,1)S(1)}, bf16[512,128]{1,0:T(8,128)(2,1)S(1)}, u32[]{:S(2)}, u32[]{:S(2)}) collective-permute-start(bf16[512,128]{1,0:T(8,128)(2,1)S(1)} %fusion.7.rest_0_), channel_id=1, source_target_pairs={{0,8},{1,5},{2,10},{3,7},{4,12},{5,1},{6,14},{7,3},{8,0},{9,13},{1... | collective-permute-start | bytes 393224 | tf_op jit(solution)/shard_map/ppermute | solution.py:68
  39.0 6.7 %collective-permute-start.16 = (bf16[512,128]{1,0:T(8,128)(2,1)S(1)}, bf16[512,128]{1,0:T(8,128)(2,1)S(1)}, u32[]{:S(2)}, u32[]{:S(2)}) collective-permute-start(bf16[512,128]{1,0:T(8,128)(2,1)S(1)} %fusion.7.rest_0_), channel_id=1, source_target_pairs={{0,16},{1,9},{2,18},{3,11},{4,20},{5,13},{6,22},{7,15},{8,24},{9,1... | collective-permute-start | bytes 393224 | tf_op jit(solution)/shard_map/ppermute | solution.py:68
  42.2 6.4 %collective-permute-start.15 = (bf16[512,128]{1,0:T(8,128)(2,1)S(1)}, bf16[512,128]{1,0:T(8,128)(2,1)S(1)}, u32[]{:S(2)}, u32[]{:S(2)}) collective-permute-start(bf16[512,128]{1,0:T(8,128)(2,1)S(1)} %fusion.8.rest_0_), channel_id=1, source_target_pairs={{0,8},{1,5},{2,10},{3,7},{4,12},{5,1},{6,14},{7,3},{8,0},{9,13},{1... | collective-permute-start | bytes 393224 | tf_op jit(solution)/shard_map/ppermute | solution.py:68
  42.7 7.4 %collective-permute-start.18 = (bf16[512,128]{1,0:T(8,128)(2,1)S(1)}, bf16[512,128]{1,0:T(8,128)(2,1)S(1)}, u32[]{:S(2)}, u32[]{:S(2)}) collective-permute-start(bf16[512,128]{1,0:T(8,128)(2,1)S(1)} %fusion.8.rest_0_), channel_id=1, source_target_pairs={{0,4},{1,9},{2,6},{3,11},{4,0},{5,13},{6,2},{7,15},{8,12},{9,1},{1... | collective-permute-start | bytes 393224 | tf_op jit(solution)/shard_map/ppermute | solution.py:68
  44.0 7.3 %collective-permute-start.12 = (bf16[128,512]{1,0:T(8,128)(2,1)S(1)}, bf16[128,512]{1,0:T(8,128)(2,1)S(1)}, u32[]{:S(2)}, u32[]{:S(2)}) collective-permute-start(bf16[128,512]{1,0:T(8,128)(2,1)S(1)} %slice.55), channel_id=1, source_target_pairs={{0,2},{1,3},{2,0},{3,1},{4,6},{5,7},{6,4},{7,5},{8,10},{9,11},{10,... | collective-permute-start | bytes 393224 | tf_op jit(solution)/shard_map/ppermute | solution.py:72
  45.6 6.4 %collective-permute-start.20 = (bf16[512,128]{1,0:T(8,128)(2,1)S(1)}, bf16[512,128]{1,0:T(8,128)(2,1)S(1)}, u32[]{:S(2)}, u32[]{:S(2)}) collective-permute-start(bf16[512,128]{1,0:T(8,128)(2,1)S(1)} %collective-permute-done.16.rest_1_), channel_id=1, source_target_pairs={{0,8},{1,5},{2,10},{3,7},{4,12},{5,1},{6,14},{7,3},{8,0},{9,13},{1... | collective-permute-start | bytes 393224 | tf_op jit(solution)/shard_map/ppermute | solution.py:68
  48.6 5.0 %collective-permute-start.19 = (bf16[512,128]{1,0:T(8,128)(2,1)S(1)}, bf16[512,128]{1,0:T(8,128)(2,1)S(1)}, u32[]{:S(2)}, u32[]{:S(2)}) collective-permute-start(bf16[512,128]{1,0:T(8,128)(2,1)S(1)} %collective-permute-done.15.rest_1_), channel_id=1, source_target_pairs={{0,4},{1,9},{2,6},{3,11},{4,0},{5,13},{6,2},{7,15},{8,12},{9,1},{1... | collective-permute-start | bytes 393224 | tf_op jit(solution)/shard_map/ppermute | solution.py:68

commit v6 on v5

--- a/solution.py
+++ b/solution.py
@@ -59,12 +59,13 @@
     )
 
 
-def swap_wide(value, wide_size, narrow_size, chunk, stage):
+def swap_wide(value, wide_size, narrow_size, chunk, *stages):
     pairs = []
     for wide in range(wide_size):
         for narrow in range(narrow_size):
-            bit = stage_bits(wide_size, chunk, narrow & 1)[stage]
-            pairs.append((wide * narrow_size + narrow, (wide ^ (1 << bit)) * narrow_size + narrow))
+            bits = stage_bits(wide_size, chunk, narrow & 1)
+            other = wide ^ sum(1 << bits[stage] for stage in stages)
+            pairs.append((wide * narrow_size + narrow, other * narrow_size + narrow))
     return lax.ppermute(value, BOTH, pairs)
 
 
@@ -183,30 +184,34 @@
     keys[...] = rotate(projected, cos_ref[...], sin_ref[...], -1.0).astype(BF16)
 
 
-def finish_weights(start, size, chunk, wide_size, grad_scale, half, last, gain_ref, weight_ref, *rest):
+def finish_weights(jobs, wide_size, grad_scale, last, gain_ref, weight_ref, *rest):
     out, gain_out, held, gains, sent, gain_sent = rest[-6:]
-    places = quarters(wide_size, chunk)[3 * half : 3 + half]
-    sources = rest[: len(places)]
-    before = rest[-7] if len(rest) > 6 + len(places) else None
+    total = sum(count for *_, count in jobs)
+    before = rest[-7] if len(rest) > 6 + total else None
     gains[...] = jnp.zeros_like(gains) if before is None else before[...]
-    copies = []
-    for row in range(0, size, TILE):
-        rows, here = slice(row, row + TILE), slice(start + row, start + row + TILE)
-        gain = gain_ref[0:1, here].astype(F32) * grad_scale
-        column = jnp.broadcast_to(gain, (TILE, TILE)).T
-        folded = jnp.zeros((TILE, TILE), F32)
-        for part, (source, at) in enumerate(zip(sources, places, strict=True)):
-            terms = source[rows].astype(F32)
-            folded = folded + terms * weight_ref[here, pl.ds(at, TILE)].astype(F32)
-            held[part, rows] = terms * column
-            copies.append(
-                pltpu.make_async_copy(
-                    held.at[part, rows], out.at[here, pl.ds(at, TILE)], sent.at[part, row // TILE]
+    copies, slot = [], 0
+    for start, size, chunk, begin, count in jobs:
+        places = quarters(wide_size, chunk)[begin : begin + count]
+        for row in range(0, size, TILE):
+            rows, here = slice(row, row + TILE), slice(start + row, start + row + TILE)
+            gain = gain_ref[0:1, here].astype(F32) * grad_scale
+            column = jnp.broadcast_to(gain, (TILE, TILE)).T
+            folded = jnp.zeros((TILE, TILE), F32)
+            for part, at in enumerate(places):
+                terms = rest[slot + part][rows].astype(F32)
+                folded = folded + terms * weight_ref[here, pl.ds(at, TILE)].astype(F32)
+                held[slot + part, rows] = terms * column
+                copies.append(
+                    pltpu.make_async_copy(
+                        held.at[slot + part, rows],
+                        out.at[here, pl.ds(at, TILE)],
+                        sent.at[slot + part, row // TILE],
+                    )
                 )
-            )
-            copies[-1].start()
-        line = (start + row) // TILE
-        gains[line : line + 1] += jnp.sum(folded.T, axis=0, keepdims=True) * grad_scale
+                copies[-1].start()
+            line = (start + row) // TILE
+            gains[line : line + 1] += jnp.sum(folded.T, axis=0, keepdims=True) * grad_scale
+        slot += count
     if last:
         copies.append(pltpu.make_async_copy(gains, gain_out, gain_sent))
         copies[-1].start()
@@ -216,12 +221,13 @@
         copy.wait()
 
 
-def write_weights(start, size, chunk, wide_size, grad_scale, half, last, gain_row, key_weight, parts, before):
+def write_weights(jobs, wide_size, grad_scale, last, gain_row, key_weight, parts, before):
     own = key_weight.shape[0]
     at = 2 + len(parts)
     gain_kind = ((own // TILE, TILE), F32)
+    size = max(job[1] for job in jobs)
     return call(
-        functools.partial(finish_weights, start, size, chunk, wide_size, grad_scale, half, last),
+        functools.partial(finish_weights, jobs, wide_size, grad_scale, last),
         [((own, KV), F32, "far"), (*gain_kind, "far") if last else gain_kind],
         gain_row, key_weight, *parts, *before,
         anywhere=(at,),
@@ -241,7 +247,10 @@
     own = key_weight.shape[0]
     core, over = 1, 2
     swap = functools.partial(swap_narrow, narrow_size=narrow_size)
-    summed = functools.partial(swap_wide, wide_size=wide_size, narrow_size=narrow_size)
+
+    def summed(value, chunk, *stages):
+        return swap_wide(value, wide_size, narrow_size, chunk, *stages)
+
     chunks = []
     for eighths in CHUNKS:
         chunks.append((sum(size for _, size in chunks), own * eighths // 8))
@@ -293,11 +302,11 @@
 
     count = len(chunks)
     totals = []
-    got = [summed(send_half, chunk=k, stage=0) for k, (_, send_half) in enumerate(state)]
+    got = [summed(send_half, k, 0) for k, (_, send_half) in enumerate(state)]
     for k in range(count):
         totals.append(state[k][0] + after(got[k], latest).astype(F32))
         latest = totals[-1]
-    got = [summed(total[1].astype(BF16), chunk=k, stage=1) for k, total in enumerate(totals)]
+    got = [summed(total[1].astype(BF16), k, 1) for k, total in enumerate(totals)]
     for k in range(count):
         totals[k] = totals[k][0] + after(got[k], latest).astype(F32)
         latest = totals[k]
@@ -306,35 +315,29 @@
     latest = pair
     for stage in range(2, wide_size.bit_length() - 1):
         rounded = [total.astype(BF16) for total in totals]
-        got = [summed(value, chunk=k, stage=stage) for k, value in enumerate(rounded)]
+        got = [summed(value, k, stage) for k, value in enumerate(rounded)]
         for k in range(count):
             totals[k] = rounded[k].astype(F32) + after(got[k], latest).astype(F32)
             latest = totals[k]
     mine = [total.astype(BF16) for total in totals]
-    near = [summed(value, chunk=k, stage=1) for k, value in enumerate(mine)]
-    far = [summed(value, chunk=k, stage=0) for k, value in enumerate(mine)]
-    def write(k, half, parts):
-        start, size = chunks[k]
-        final = half == 1 and k == count - 1
+    near = [summed(value, k, 1) for k, value in enumerate(mine)]
+    far = [summed(value, k, 0) for k, value in enumerate(mine)]
+    def write(begin, parts, final, before):
+        jobs = [(*chunks[k], k, begin, len(of_chunk)) for k, of_chunk in enumerate(parts)]
         return write_weights(
-            start, size, k, wide_size, grad_scale, half, final, gain_row, key_weight, parts, before
+            jobs, wide_size, grad_scale, final, gain_row, key_weight, sum(parts, ()), before
         )
 
-    before = ()
-    last = []
-    for k in range(count):
-        near[k] = after(near[k], latest)
-        last.append(summed(near[k], chunk=k, stage=0))
-        far[k] = after(far[k], near[k])
-        before = write(k, 0, (mine[k], near[k], far[k]))
-        latest = before[1]
+    near[0] = after(near[0], latest)
+    passed_on = summed(near[0], 0, 0)
+    straight = summed(mine[1], 1, 0, 1)
+    far[0] = after(far[0], near[0])
+    near[1] = after(near[1], far[0])
+    before = write(0, ((mine[0], near[0], far[0]), (mine[1], near[1], far[1])), False, ())
     (keys,) = call(
-        finish_keys, [((rows, KV), BF16)], pair[:rows], after(got_x, latest), inv_rms, cosine, sine
-    )
-    latest = keys
-    for k in range(count):
-        before = write(k, 1, (after(last[k], latest),))
-        latest = before[1]
+        finish_keys, [((rows, KV), BF16)], pair[:rows], after(got_x, before[1], straight), inv_rms, cosine, sine
+    )
+    before = write(3, ((after(passed_on, keys),), (straight,)), True, before)
     weight_grad, gain_grad = before
     return keys, weight_grad, gain_grad.reshape(own)
 

time: 54.7 us -> 54.6 us (level)
  waiting for transfers between devices: 13.6 us -> 15.4 us
  Pallas kernels: 6.86 us -> 5.39 us
    ppermute x12, waiting for transfers between devices: 4.69 us -> 6.53 us  [swap_wide(): return lax.ppermute(value, BOTH, pairs)]
    pallas_call x10 -> x8, Pallas kernels: 6.86 us -> 5.39 us  [call(): pl.pallas_call(body, out_shape=[jax.ShapeDtypeStruct(shape, kind) for sha...]
  transfers between devices with their start and end apart: 21 -> 21, of which waited for: 11 -> 13; matrix products, arithmetic and copies ran while one was open for 2% -> 2% of each run, Pallas kernels for 11% -> 8%
where the time goes in v6:
time: 54.6 us; the launch traced here: 54.4 us
  starting transfers between devices  29.7 us (54%)
  waiting for transfers between devices  15.4 us (28%)
  Pallas kernels  5.39 us (10%)
  local copies, waits for them, and re-layouts  2.22 us (4%)
  between operations  0.88 us (2%)
  other arithmetic  0.74 us (1%)
    ppermute x12, starting transfers between devices, swap_wide(): return lax.ppermute(value, BOTH, pairs)  22.3 us
    ppermute x9, waiting for transfers between devices, swap_narrow(): lax.ppermute(value, 'narrow', [(i, i ^ mask) for i in range(narrow_size)])  8.87 us
    ppermute x9, starting transfers between devices, swap_narrow(): lax.ppermute(value, 'narrow', [(i, i ^ mask) for i in range(narrow_size)])  7.43 us
    ppermute x12, waiting for transfers between devices, swap_wide(): return lax.ppermute(value, BOTH, pairs)  6.53 us
    pallas_call x8, Pallas kernels, call(): pl.pallas_call(body, out_shape=[jax.ShapeDtypeStruct(shape, kind) for sha...  5.39 us
    unnamed x10, local copies, waits for them, and re-layouts  2.13 us
  transfers between devices with their start and end apart: 21, of which 13 were waited for; matrix products, arithmetic and copies ran while one was open for 2% of the time, Pallas kernels for 8%

profile of v6, /device:TPU:0, one launch (start us, length us, event | category | flops | bytes accessed | tf_op | source)
XLA Modules:
  0.0 54.4 jit_solution(2991521930721834997)
XLA Ops:
  0.6 1.2 %copy-done.1 = bf16[128,4096]{1,0:T(8,128)(2,1)S(1)} copy-done((bf16[128,4096]{1,0:T(8,128)(2,1)S(1)}, bf16[128,4096]{1,0:T(8,128)(2,1)}, u32[]{:S(2)}) %copy-start.1) | copy-done | bytes 1048600
  1.9 3.0 %collective-permute-start.2 = (bf16[128,1024]{1,0:T(8,128)(2,1)S(1)}, bf16[128,1024]{1,0:T(8,128)(2,1)S(1)}, u32[]{:S(2)}, u32[]{:S(2)}) collective-permute-start(bf16[128,1024]{1,0:T(8,128)(2,1)S(1)} %shard_map.67), channel_id=1, source_target_pairs={{0,2},{1,3},{2,0},{3,1},{4,6},{5,7},{6,4},{7,5},{8,10},{9,11},{10,... | collective-permute-start | bytes 786440 | tf_op jit(solution)/shard_map/ppermute | solution.py:73
  5.4 0.9 %copy-done.3 = bf16[128,512]{1,0:T(8,128)(2,1)S(1)} copy-done((bf16[128,512]{1,0:T(8,128)(2,1)S(1)}, bf16[128,512]{1,0:T(8,128)(2,1)}, u32[]{:S(2)}) %copy-start.3) | copy-done | bytes 131096
  6.7 0.7 %collective-permute-start.4 = (bf16[128,512]{1,0:T(8,128)(2,1)S(1)}, bf16[128,512]{1,0:T(8,128)(2,1)S(1)}, u32[]{:S(2)}, u32[]{:S(2)}) collective-permute-start(bf16[128,512]{1,0:T(8,128)(2,1)S(1)} %get-tuple-element.37.scaled_ref), channel_id=1, source_target_pairs={{0,2},{1,3},{2,0},{3,1},{4,6},{5,7},{6,4},{7,5},{8,10},{9,11},{10,... | collective-permute-start | bytes 393224 | tf_op jit(solution)/shard_map/ppermute | solution.py:73
  7.4 1.4 %collective-permute-start.1 = (bf16[128,1024]{1,0:T(8,128)(2,1)S(1)}, bf16[128,1024]{1,0:T(8,128)(2,1)S(1)}, u32[]{:S(2)}, u32[]{:S(2)}) collective-permute-start(bf16[128,1024]{1,0:T(8,128)(2,1)S(1)} %get-tuple-element.36), channel_id=1, source_target_pairs={{0,2},{1,3},{2,0},{3,1},{4,6},{5,7},{6,4},{7,5},{8,10},{9,11},{10,... | collective-permute-start | bytes 786440 | tf_op jit(solution)/shard_map/ppermute | solution.py:73
  8.8 6.0 %collective-permute-done.4.x_grad = bf16[128,512]{1,0:T(8,128)(2,1)S(1)} collective-permute-done((bf16[128,512]{1,0:T(8,128)(2,1)S(1)}, bf16[128,512]{1,0:T(8,128)(2,1)S(1)}, u32[]{:S(2)}, u32[]{:S(2)}) %collective-permute-start.4) | collective-permute-done | bytes 131104 | tf_op jit(solution)/shard_map/ppermute | solution.py:73
  14.9 0.6 %collective-permute-start.3 = (bf16[128,512]{1,0:T(8,128)(2,1)S(1)}, bf16[128,512]{1,0:T(8,128)(2,1)S(1)}, u32[]{:S(2)}, u32[]{:S(2)}) collective-permute-start(bf16[128,512]{1,0:T(8,128)(2,1)S(1)} %slice.35), channel_id=1, source_target_pairs={{0,1},{1,0},{2,3},{3,2},{4,5},{5,4},{6,7},{7,6},{8,9},{9,8},{10,11... | collective-permute-start | bytes 393224 | tf_op jit(solution)/shard_map/ppermute | solution.py:73
  15.5 0.8 %collective-permute-done.5.last_grad = bf16[128,512]{1,0:T(8,128)(2,1)S(1)} collective-permute-done((bf16[128,512]{1,0:T(8,128)(2,1)S(1)}, bf16[128,512]{1,0:T(8,128)(2,1)S(1)}, u32[]{:S(2)}, u32[]{:S(2)}) %collective-permute-start.5) | collective-permute-done | bytes 131104 | tf_op jit(solution)/shard_map/ppermute | solution.py:73
  17.0 2.2 %collective-permute-start.9 = (bf16[2,512,128]{2,1,0:T(8,128)(2,1)S(1)}, bf16[2,512,128]{2,1,0:T(8,128)(2,1)S(1)}, u32[]{:S(2)}, u32[]{:S(2)}) collective-permute-start(bf16[2,512,128]{2,1,0:T(8,128)(2,1)S(1)} %get-tuple-element.38), channel_id=1, source_target_pairs={{0,8},{1,5},{2,10},{3,7},{4,12},{5,1},{6,14},{7,3},{8,0},{9,13},{1... | collective-permute-start | bytes 786440 | tf_op jit(solution)/shard_map/ppermute | solution.py:69
  19.2 0.5 collective-permute-done.1.x_ref.rest_1_
  19.8 1.3 %collective-permute-done.6.last_ref.rest_3_ = bf16[128,512]{1,0:T(8,128)(2,1)S(1)} collective-permute-done((bf16[128,512]{1,0:T(8,128)(2,1)S(1)}, bf16[128,512]{1,0:T(8,128)(2,1)S(1)}, u32[]{:S(2)}, u32[]{:S(2)}) %collective-permute-start.6) | collective-permute-done | bytes 131104 | tf_op jit(solution)/shard_map/ppermute | solution.py:73
  21.6 1.8 %collective-permute-start.8 = (bf16[2,512,128]{2,1,0:T(8,128)(2,1)S(1)}, bf16[2,512,128]{2,1,0:T(8,128)(2,1)S(1)}, u32[]{:S(2)}, u32[]{:S(2)}) collective-permute-start(bf16[2,512,128]{2,1,0:T(8,128)(2,1)S(1)} %get-tuple-element.40), channel_id=1, source_target_pairs={{0,4},{1,9},{2,6},{3,11},{4,0},{5,13},{6,2},{7,15},{8,12},{9,1},{1... | collective-permute-start | bytes 786440 | tf_op jit(solution)/shard_map/ppermute | solution.py:69
  23.4 0.7 %shard_map.71 = (f32[256,512]{1,0:T(8,128)S(1)}, bf16[256,512]{1,0:T(8,128)(2,1)S(1)}) custom-call(bf16[1,1024]{1,0:T(2,128)(2,1)S(1)} %reshape.35.gain_ref, bf16[1024,512]{1,0:T(8,128)(2,1)S(1)} %copy-done, bf16[128,1024]{1,0:T(8,128)(2,1)S(1)} %get-tuple-element.34.own_ref, bf16[128,1536]{1,0:T(8,128)(2,1)S(1)} %collective-permute-done.core_ref, ...), custom_call_target="tpu_custom_call" | custom-call | tf_op jit(solution)/shard_map/pallas_call | solution.py:83
  24.3 2.7 %collective-permute-start.11 = (bf16[512,128]{1,0:T(8,128)(2,1)S(1)}, bf16[512,128]{1,0:T(8,128)(2,1)S(1)}, u32[]{:S(2)}, u32[]{:S(2)}) collective-permute-start(bf16[512,128]{1,0:T(8,128)(2,1)S(1)} %fusion.3), channel_id=1, source_target_pairs={{0,16},{1,9},{2,18},{3,11},{4,20},{5,13},{6,22},{7,15},{8,24},{9,1... | collective-permute-start | bytes 393224 | tf_op jit(solution)/shard_map/ppermute | solution.py:69
  27.0 1.0 %collective-permute-done.8 = bf16[2,512,128]{2,1,0:T(8,128)(2,1)S(1)} collective-permute-done((bf16[2,512,128]{2,1,0:T(8,128)(2,1)S(1)}, bf16[2,512,128]{2,1,0:T(8,128)(2,1)S(1)}, u32[]{:S(2)}, u32[]{:S(2)}) %collective-permute-start.8) | collective-permute-done | bytes 262176 | tf_op jit(solution)/shard_map/ppermute | solution.py:69
  28.1 1.9 %collective-permute-start.10 = (bf16[512,128]{1,0:T(8,128)(2,1)S(1)}, bf16[512,128]{1,0:T(8,128)(2,1)S(1)}, u32[]{:S(2)}, u32[]{:S(2)}) collective-permute-start(bf16[512,128]{1,0:T(8,128)(2,1)S(1)} %fusion.2), channel_id=1, source_target_pairs={{0,8},{1,5},{2,10},{3,7},{4,12},{5,1},{6,14},{7,3},{8,0},{9,13},{1... | collective-permute-start | bytes 393224 | tf_op jit(solution)/shard_map/ppermute | solution.py:69
  30.0 0.7 %collective-permute-done.11 = bf16[512,128]{1,0:T(8,128)(2,1)S(1)} collective-permute-done((bf16[512,128]{1,0:T(8,128)(2,1)S(1)}, bf16[512,128]{1,0:T(8,128)(2,1)S(1)}, u32[]{:S(2)}, u32[]{:S(2)}) %collective-permute-start.11) | collective-permute-done | bytes 131104 | tf_op jit(solution)/shard_map/ppermute | solution.py:69
  30.8 1.5 %collective-permute-start.13 = (bf16[512,128]{1,0:T(8,128)(2,1)S(1)}, bf16[512,128]{1,0:T(8,128)(2,1)S(1)}, u32[]{:S(2)}, u32[]{:S(2)}) collective-permute-start(bf16[512,128]{1,0:T(8,128)(2,1)S(1)} %fusion), channel_id=1, source_target_pairs={{0,4},{1,17},{2,6},{3,19},{4,0},{5,21},{6,2},{7,23},{8,12},{9,25},... | collective-permute-start | bytes 393224 | tf_op jit(solution)/shard_map/ppermute | solution.py:69
  32.3 0.9 %collective-permute-done.10 = bf16[512,128]{1,0:T(8,128)(2,1)S(1)} collective-permute-done((bf16[512,128]{1,0:T(8,128)(2,1)S(1)}, bf16[512,128]{1,0:T(8,128)(2,1)S(1)}, u32[]{:S(2)}, u32[]{:S(2)}) %collective-permute-start.10) | collective-permute-done | bytes 131104 | tf_op jit(solution)/shard_map/ppermute | solution.py:69
  33.2 4.0 %collective-permute-start.15 = (bf16[512,128]{1,0:T(8,128)(2,1)S(1)}, bf16[512,128]{1,0:T(8,128)(2,1)S(1)}, u32[]{:S(2)}, u32[]{:S(2)}) collective-permute-start(bf16[512,128]{1,0:T(8,128)(2,1)S(1)} %fusion.1), channel_id=1, source_target_pairs={{0,16},{1,17},{2,18},{3,19},{4,20},{5,21},{6,22},{7,23},{8,24},{9,... | collective-permute-start | bytes 393224 | tf_op jit(solution)/shard_map/ppermute | solution.py:69
  37.3 1.6 %collective-permute-start.16 = (bf16[512,128]{1,0:T(8,128)(2,1)S(1)}, bf16[512,128]{1,0:T(8,128)(2,1)S(1)}, u32[]{:S(2)}, u32[]{:S(2)}) collective-permute-start(bf16[512,128]{1,0:T(8,128)(2,1)S(1)} %fusion.7.rest_0_), channel_id=1, source_target_pairs={{0,8},{1,5},{2,10},{3,7},{4,12},{5,1},{6,14},{7,3},{8,0},{9,13},{1... | collective-permute-start | bytes 393224 | tf_op jit(solution)/shard_map/ppermute | solution.py:69
  38.9 1.9 %collective-permute-start.14 = (bf16[512,128]{1,0:T(8,128)(2,1)S(1)}, bf16[512,128]{1,0:T(8,128)(2,1)S(1)}, u32[]{:S(2)}, u32[]{:S(2)}) collective-permute-start(bf16[512,128]{1,0:T(8,128)(2,1)S(1)} %fusion.7.rest_0_), channel_id=1, source_target_pairs={{0,16},{1,9},{2,18},{3,11},{4,20},{5,13},{6,22},{7,15},{8,24},{9,1... | collective-permute-start | bytes 393224 | tf_op jit(solution)/shard_map/ppermute | solution.py:69
  40.9 1.2 %collective-permute-done.15 = bf16[512,128]{1,0:T(8,128)(2,1)S(1)} collective-permute-done((bf16[512,128]{1,0:T(8,128)(2,1)S(1)}, bf16[512,128]{1,0:T(8,128)(2,1)S(1)}, u32[]{:S(2)}, u32[]{:S(2)}) %collective-permute-start.15) | collective-permute-done | bytes 131104 | tf_op jit(solution)/shard_map/ppermute | solution.py:69
  42.2 0.5 collective-permute-start.17
  42.7 1.3 %collective-permute-start.18 = (bf16[512,128]{1,0:T(8,128)(2,1)S(1)}, bf16[512,128]{1,0:T(8,128)(2,1)S(1)}, u32[]{:S(2)}, u32[]{:S(2)}) collective-permute-start(bf16[512,128]{1,0:T(8,128)(2,1)S(1)} %fusion.8.rest_3_), channel_id=1, source_target_pairs={{0,4},{1,9},{2,6},{3,11},{4,0},{5,13},{6,2},{7,15},{8,12},{9,1},{1... | collective-permute-start | bytes 393224 | tf_op jit(solution)/shard_map/ppermute | solution.py:69
  44.0 1.5 %collective-permute-start.12 = (bf16[128,512]{1,0:T(8,128)(2,1)S(1)}, bf16[128,512]{1,0:T(8,128)(2,1)S(1)}, u32[]{:S(2)}, u32[]{:S(2)}) collective-permute-start(bf16[128,512]{1,0:T(8,128)(2,1)S(1)} %slice.55), channel_id=1, source_target_pairs={{0,2},{1,3},{2,0},{3,1},{4,6},{5,7},{6,4},{7,5},{8,10},{9,11},{10,... | collective-permute-start | bytes 393224 | tf_op jit(solution)/shard_map/ppermute | solution.py:73
  45.6 2.7 %collective-permute-start.19 = (bf16[512,128]{1,0:T(8,128)(2,1)S(1)}, bf16[512,128]{1,0:T(8,128)(2,1)S(1)}, u32[]{:S(2)}, u32[]{:S(2)}) collective-permute-start(bf16[512,128]{1,0:T(8,128)(2,1)S(1)} %fusion.8.rest_3_), channel_id=1, source_target_pairs={{0,12},{1,13},{2,14},{3,15},{4,8},{5,9},{6,10},{7,11},{8,4},{9,5},... | collective-permute-start | bytes 393224 | tf_op jit(solution)/shard_map/ppermute | solution.py:69
  48.7 1.4 %shard_map.72 = (f32[1024,512]{1,0:T(8,128)}, f32[8,128]{1,0:T(8,128)S(1)}) custom-call(bf16[1,1024]{1,0:T(2,128)(2,1)S(1)} %reshape.35.gain_ref, bf16[1024,512]{1,0:T(8,128)(2,1)S(1)} %copy-done, bf16[512,128]{1,0:T(8,128)(2,1)S(1)} %fusion.7.rest_0_, bf16[512,128]{1,0:T(8,128)(2,1)S(1)} %collective-permute-done.14.rest_1_, ...), custom_call_target="tpu_custom_call" | custom-call | tf_op jit(solution)/shard_map/pallas_call | solution.py:83
  50.2 1.4 %collective-permute-done.19.rest_1_ = bf16[512,128]{1,0:T(8,128)(2,1)S(1)} collective-permute-done((bf16[512,128]{1,0:T(8,128)(2,1)S(1)}, bf16[512,128]{1,0:T(8,128)(2,1)S(1)}, u32[]{:S(2)}, u32[]{:S(2)}) %collective-permute-start.19) | collective-permute-done | bytes 131104 | tf_op jit(solution)/shard_map/ppermute | solution.py:69
  51.6 0.8 %shard_map.73 = bf16[128,512]{1,0:T(8,128)(2,1)} custom-call(f32[128,512]{1,0:T(8,128)S(1)} %slice.40.mine_ref, bf16[128,512]{1,0:T(8,128)(2,1)S(1)} %collective-permute-done.12.got_ref, f32[128,128]{1,0:T(8,128)S(1)} %get-tuple-element.58.inv_ref, f32[128,128]{1,0:T(8,128)S(1)} %get-tuple-element.66.cos_ref, f32[128,128]{1,0:T(8,128)S(1)} %get-tuple-element.67.sin_ref), custom_call_target="tpu_custom_call" | custom-call | tf_op jit(solution)/shard_map/pallas_call | solution.py:83
  52.4 0.9 %collective-permute-done.20.rest_0_ = bf16[512,128]{1,0:T(8,128)(2,1)S(1)} collective-permute-done((bf16[512,128]{1,0:T(8,128)(2,1)S(1)}, bf16[512,128]{1,0:T(8,128)(2,1)S(1)}, u32[]{:S(2)}, u32[]{:S(2)}) %collective-permute-start.20) | collective-permute-done | bytes 131104 | tf_op jit(solution)/shard_map/ppermute | solution.py:69
  53.3 1.1 %shard_map.74 = (f32[1024,512]{1,0:T(8,128)}, f32[8,128]{1,0:T(8,128)}) custom-call(bf16[1,1024]{1,0:T(2,128)(2,1)S(1)} %reshape.35.gain_ref, bf16[1024,512]{1,0:T(8,128)(2,1)S(1)} %copy-done, bf16[512,128]{1,0:T(8,128)(2,1)S(1)} %collective-permute-done.20.rest_0_, ...), custom_call_target="tpu_custom_call", output_to_operand_aliasing={{0}: (4, {})} | custom-call | tf_op jit(solution)/shard_map/pallas_call | solution.py:83
  (46 shorter events, 3.2 us)
Async XLA Ops:
  0.6 1.2 %copy-start.1 = (bf16[128,4096]{1,0:T(8,128)(2,1)S(1)}, bf16[128,4096]{1,0:T(8,128)(2,1)}, u32[]{:S(2)}) copy-start(bf16[128,4096]{1,0:T(8,128)(2,1)} %tok_ref.2) | copy-start | bytes 3145732
  1.9 3.5 %copy-start.2 = (bf16[128,4096]{1,0:T(8,128)(2,1)S(1)}, bf16[128,4096]{1,0:T(8,128)(2,1)}, u32[]{:S(2)}) copy-start(bf16[128,4096]{1,0:T(8,128)(2,1)} %tok_ref.2) | copy-start | bytes 3145732
  1.9 17.8 %copy-start.4 = (bf16[1024]{0:T(1024)(128)(2,1)S(1)}, bf16[1024]{0:T(1024)(128)(2,1)}, u32[]{:S(2)}) copy-start(bf16[1024]{0:T(1024)(128)(2,1)} %param.5) | copy-start | bytes 6148
  1.9 13.0 %collective-permute-start.2 = (bf16[128,1024]{1,0:T(8,128)(2,1)S(1)}, bf16[128,1024]{1,0:T(8,128)(2,1)S(1)}, u32[]{:S(2)}, u32[]{:S(2)}) collective-permute-start(bf16[128,1024]{1,0:T(8,128)(2,1)S(1)} %shard_map.67), channel_id=1, source_target_pairs={{0,2},{1,3},{2,0},{3,1},{4,6},{5,7},{6,4},{7,5},{8,10},{9,11},{10,... | collective-permute-start | bytes 786440 | tf_op jit(solution)/shard_map/ppermute | solution.py:73
  5.4 0.9 %copy-start.3 = (bf16[128,512]{1,0:T(8,128)(2,1)S(1)}, bf16[128,512]{1,0:T(8,128)(2,1)}, u32[]{:S(2)}) copy-start(bf16[128,512]{1,0:T(8,128)(2,1)} %grad_ref.1) | copy-start | bytes 393220
  6.3 17.1 %copy-start = (bf16[1024,512]{1,0:T(8,128)(2,1)S(1)}, bf16[1024,512]{1,0:T(8,128)(2,1)}, u32[]{:S(2)}) copy-start(bf16[1024,512]{1,0:T(8,128)(2,1)} %weight_ref.4) | copy-start | bytes 3145732
  6.7 9.8 %collective-permute-start = (bf16[128,1536]{1,0:T(8,128)(2,1)S(1)}, bf16[128,1536]{1,0:T(8,128)(2,1)S(1)}, u32[]{:S(2)}, u32[]{:S(2)}) collective-permute-start(bf16[128,1536]{1,0:T(8,128)(2,1)S(1)} %get-tuple-element.35), channel_id=1, source_target_pairs={{0,1},{1,0},{2,3},{3,2},{4,5},{5,4},{6,7},{7,6},{8,9},{9,8},{10,11... | collective-permute-start | bytes 1179656 | tf_op jit(solution)/shard_map/ppermute | solution.py:73
  6.7 8.1 %collective-permute-start.4 = (bf16[128,512]{1,0:T(8,128)(2,1)S(1)}, bf16[128,512]{1,0:T(8,128)(2,1)S(1)}, u32[]{:S(2)}, u32[]{:S(2)}) collective-permute-start(bf16[128,512]{1,0:T(8,128)(2,1)S(1)} %get-tuple-element.37.scaled_ref), channel_id=1, source_target_pairs={{0,2},{1,3},{2,0},{3,1},{4,6},{5,7},{6,4},{7,5},{8,10},{9,11},{10,... | collective-permute-start | bytes 393224 | tf_op jit(solution)/shard_map/ppermute | solution.py:73
  7.4 12.3 %collective-permute-start.1 = (bf16[128,1024]{1,0:T(8,128)(2,1)S(1)}, bf16[128,1024]{1,0:T(8,128)(2,1)S(1)}, u32[]{:S(2)}, u32[]{:S(2)}) collective-permute-start(bf16[128,1024]{1,0:T(8,128)(2,1)S(1)} %get-tuple-element.36), channel_id=1, source_target_pairs={{0,2},{1,3},{2,0},{3,1},{4,6},{5,7},{6,4},{7,5},{8,10},{9,11},{10,... | collective-permute-start | bytes 786440 | tf_op jit(solution)/shard_map/ppermute | solution.py:73
  14.9 1.3 %collective-permute-start.5 = (bf16[128,512]{1,0:T(8,128)(2,1)S(1)}, bf16[128,512]{1,0:T(8,128)(2,1)S(1)}, u32[]{:S(2)}, u32[]{:S(2)}) collective-permute-start(bf16[128,512]{1,0:T(8,128)(2,1)S(1)} %collective-permute-done.4.x_grad), channel_id=1, source_target_pairs={{0,1},{1,0},{2,3},{3,2},{4,5},{5,4},{6,7},{7,6},{8,9},{9,8},{10,11... | collective-permute-start | bytes 393224 | tf_op jit(solution)/shard_map/ppermute | solution.py:73
  14.9 1.6 %collective-permute-start.3 = (bf16[128,512]{1,0:T(8,128)(2,1)S(1)}, bf16[128,512]{1,0:T(8,128)(2,1)S(1)}, u32[]{:S(2)}, u32[]{:S(2)}) collective-permute-start(bf16[128,512]{1,0:T(8,128)(2,1)S(1)} %slice.35), channel_id=1, source_target_pairs={{0,1},{1,0},{2,3},{3,2},{4,5},{5,4},{6,7},{7,6},{8,9},{9,8},{10,11... | collective-permute-start | bytes 393224 | tf_op jit(solution)/shard_map/ppermute | solution.py:73
  17.0 7.3 %collective-permute-start.9 = (bf16[2,512,128]{2,1,0:T(8,128)(2,1)S(1)}, bf16[2,512,128]{2,1,0:T(8,128)(2,1)S(1)}, u32[]{:S(2)}, u32[]{:S(2)}) collective-permute-start(bf16[2,512,128]{2,1,0:T(8,128)(2,1)S(1)} %get-tuple-element.38), channel_id=1, source_target_pairs={{0,8},{1,5},{2,10},{3,7},{4,12},{5,1},{6,14},{7,3},{8,0},{9,13},{1... | collective-permute-start | bytes 786440 | tf_op jit(solution)/shard_map/ppermute | solution.py:69
  19.7 1.4 %collective-permute-start.6 = (bf16[128,512]{1,0:T(8,128)(2,1)S(1)}, bf16[128,512]{1,0:T(8,128)(2,1)S(1)}, u32[]{:S(2)}, u32[]{:S(2)}) collective-permute-start(bf16[128,512]{1,0:T(8,128)(2,1)S(1)} %slice.28), channel_id=1, source_target_pairs={{0,1},{1,0},{2,3},{3,2},{4,5},{5,4},{6,7},{7,6},{8,9},{9,8},{10,11... | collective-permute-start | bytes 393224 | tf_op jit(solution)/shard_map/ppermute | solution.py:73
  21.6 6.4 %collective-permute-start.8 = (bf16[2,512,128]{2,1,0:T(8,128)(2,1)S(1)}, bf16[2,512,128]{2,1,0:T(8,128)(2,1)S(1)}, u32[]{:S(2)}, u32[]{:S(2)}) collective-permute-start(bf16[2,512,128]{2,1,0:T(8,128)(2,1)S(1)} %get-tuple-element.40), channel_id=1, source_target_pairs={{0,4},{1,9},{2,6},{3,11},{4,0},{5,13},{6,2},{7,15},{8,12},{9,1},{1... | collective-permute-start | bytes 786440 | tf_op jit(solution)/shard_map/ppermute | solution.py:69
  24.1 13.0 %collective-permute-start.7 = (bf16[256,512]{1,0:T(8,128)(2,1)S(1)}, bf16[256,512]{1,0:T(8,128)(2,1)S(1)}, u32[]{:S(2)}, u32[]{:S(2)}) collective-permute-start(bf16[256,512]{1,0:T(8,128)(2,1)S(1)} %get-tuple-element.43), channel_id=1, source_target_pairs={{0,1},{1,0},{2,3},{3,2},{4,5},{5,4},{6,7},{7,6},{8,9},{9,8},{10,11... | collective-permute-start | bytes 786440 | tf_op jit(solution)/shard_map/ppermute | solution.py:73
  24.3 6.4 %collective-permute-start.11 = (bf16[512,128]{1,0:T(8,128)(2,1)S(1)}, bf16[512,128]{1,0:T(8,128)(2,1)S(1)}, u32[]{:S(2)}, u32[]{:S(2)}) collective-permute-start(bf16[512,128]{1,0:T(8,128)(2,1)S(1)} %fusion.3), channel_id=1, source_target_pairs={{0,16},{1,9},{2,18},{3,11},{4,20},{5,13},{6,22},{7,15},{8,24},{9,1... | collective-permute-start | bytes 393224 | tf_op jit(solution)/shard_map/ppermute | solution.py:69
  28.1 5.0 %collective-permute-start.10 = (bf16[512,128]{1,0:T(8,128)(2,1)S(1)}, bf16[512,128]{1,0:T(8,128)(2,1)S(1)}, u32[]{:S(2)}, u32[]{:S(2)}) collective-permute-start(bf16[512,128]{1,0:T(8,128)(2,1)S(1)} %fusion.2), channel_id=1, source_target_pairs={{0,8},{1,5},{2,10},{3,7},{4,12},{5,1},{6,14},{7,3},{8,0},{9,13},{1... | collective-permute-start | bytes 393224 | tf_op jit(solution)/shard_map/ppermute | solution.py:69
  30.8 6.5 %collective-permute-start.13 = (bf16[512,128]{1,0:T(8,128)(2,1)S(1)}, bf16[512,128]{1,0:T(8,128)(2,1)S(1)}, u32[]{:S(2)}, u32[]{:S(2)}) collective-permute-start(bf16[512,128]{1,0:T(8,128)(2,1)S(1)} %fusion), channel_id=1, source_target_pairs={{0,4},{1,17},{2,6},{3,19},{4,0},{5,21},{6,2},{7,23},{8,12},{9,25},... | collective-permute-start | bytes 393224 | tf_op jit(solution)/shard_map/ppermute | solution.py:69
  33.2 8.9 %collective-permute-start.15 = (bf16[512,128]{1,0:T(8,128)(2,1)S(1)}, bf16[512,128]{1,0:T(8,128)(2,1)S(1)}, u32[]{:S(2)}, u32[]{:S(2)}) collective-permute-start(bf16[512,128]{1,0:T(8,128)(2,1)S(1)} %fusion.1), channel_id=1, source_target_pairs={{0,16},{1,17},{2,18},{3,19},{4,20},{5,21},{6,22},{7,23},{8,24},{9,... | collective-permute-start | bytes 393224 | tf_op jit(solution)/shard_map/ppermute | solution.py:69
  37.3 11.0 %collective-permute-start.16 = (bf16[512,128]{1,0:T(8,128)(2,1)S(1)}, bf16[512,128]{1,0:T(8,128)(2,1)S(1)}, u32[]{:S(2)}, u32[]{:S(2)}) collective-permute-start(bf16[512,128]{1,0:T(8,128)(2,1)S(1)} %fusion.7.rest_0_), channel_id=1, source_target_pairs={{0,8},{1,5},{2,10},{3,7},{4,12},{5,1},{6,14},{7,3},{8,0},{9,13},{1... | collective-permute-start | bytes 393224 | tf_op jit(solution)/shard_map/ppermute | solution.py:69
  38.9 6.7 %collective-permute-start.14 = (bf16[512,128]{1,0:T(8,128)(2,1)S(1)}, bf16[512,128]{1,0:T(8,128)(2,1)S(1)}, u32[]{:S(2)}, u32[]{:S(2)}) collective-permute-start(bf16[512,128]{1,0:T(8,128)(2,1)S(1)} %fusion.7.rest_0_), channel_id=1, source_target_pairs={{0,16},{1,9},{2,18},{3,11},{4,20},{5,13},{6,22},{7,15},{8,24},{9,1... | collective-permute-start | bytes 393224 | tf_op jit(solution)/shard_map/ppermute | solution.py:69
  42.2 6.6 %collective-permute-start.17 = (bf16[512,128]{1,0:T(8,128)(2,1)S(1)}, bf16[512,128]{1,0:T(8,128)(2,1)S(1)}, u32[]{:S(2)}, u32[]{:S(2)}) collective-permute-start(bf16[512,128]{1,0:T(8,128)(2,1)S(1)} %fusion.8.rest_3_), channel_id=1, source_target_pairs={{0,8},{1,5},{2,10},{3,7},{4,12},{5,1},{6,14},{7,3},{8,0},{9,13},{1... | collective-permute-start | bytes 393224 | tf_op jit(solution)/shard_map/ppermute | solution.py:69
  42.7 6.1 %collective-permute-start.18 = (bf16[512,128]{1,0:T(8,128)(2,1)S(1)}, bf16[512,128]{1,0:T(8,128)(2,1)S(1)}, u32[]{:S(2)}, u32[]{:S(2)}) collective-permute-start(bf16[512,128]{1,0:T(8,128)(2,1)S(1)} %fusion.8.rest_3_), channel_id=1, source_target_pairs={{0,4},{1,9},{2,6},{3,11},{4,0},{5,13},{6,2},{7,15},{8,12},{9,1},{1... | collective-permute-start | bytes 393224 | tf_op jit(solution)/shard_map/ppermute | solution.py:69
  44.0 6.2 %collective-permute-start.12 = (bf16[128,512]{1,0:T(8,128)(2,1)S(1)}, bf16[128,512]{1,0:T(8,128)(2,1)S(1)}, u32[]{:S(2)}, u32[]{:S(2)}) collective-permute-start(bf16[128,512]{1,0:T(8,128)(2,1)S(1)} %slice.55), channel_id=1, source_target_pairs={{0,2},{1,3},{2,0},{3,1},{4,6},{5,7},{6,4},{7,5},{8,10},{9,11},{10,... | collective-permute-start | bytes 393224 | tf_op jit(solution)/shard_map/ppermute | solution.py:73
  45.6 6.0 %collective-permute-start.19 = (bf16[512,128]{1,0:T(8,128)(2,1)S(1)}, bf16[512,128]{1,0:T(8,128)(2,1)S(1)}, u32[]{:S(2)}, u32[]{:S(2)}) collective-permute-start(bf16[512,128]{1,0:T(8,128)(2,1)S(1)} %fusion.8.rest_3_), channel_id=1, source_target_pairs={{0,12},{1,13},{2,14},{3,15},{4,8},{5,9},{6,10},{7,11},{8,4},{9,5},... | collective-permute-start | bytes 393224 | tf_op jit(solution)/shard_map/ppermute | solution.py:69
  48.3 5.0 %collective-permute-start.20 = (bf16[512,128]{1,0:T(8,128)(2,1)S(1)}, bf16[512,128]{1,0:T(8,128)(2,1)S(1)}, u32[]{:S(2)}, u32[]{:S(2)}) collective-permute-start(bf16[512,128]{1,0:T(8,128)(2,1)S(1)} %collective-permute-done.14.rest_1_), channel_id=1, source_target_pairs={{0,8},{1,5},{2,10},{3,7},{4,12},{5,1},{6,14},{7,3},{8,0},{9,13},{1... | collective-permute-start | bytes 393224 | tf_op jit(solution)/shard_map/ppermute | solution.py:69

commit v7 on v5

--- a/solution.py
+++ b/solution.py
@@ -59,12 +59,13 @@
     )
 
 
-def swap_wide(value, wide_size, narrow_size, chunk, stage):
+def swap_wide(value, wide_size, narrow_size, chunk, *stages):
     pairs = []
     for wide in range(wide_size):
         for narrow in range(narrow_size):
-            bit = stage_bits(wide_size, chunk, narrow & 1)[stage]
-            pairs.append((wide * narrow_size + narrow, (wide ^ (1 << bit)) * narrow_size + narrow))
+            bits = stage_bits(wide_size, chunk, narrow & 1)
+            other = wide ^ sum(1 << bits[stage] for stage in stages)
+            pairs.append((wide * narrow_size + narrow, other * narrow_size + narrow))
     return lax.ppermute(value, BOTH, pairs)
 
 
@@ -92,21 +93,6 @@
 
 def features_at(own, mask, start):
     return pl.multiple_of((lax.axis_index("narrow") ^ mask) * own + start, TILE)
-
-
-def first_tokens(own, size, tok_ref, x_out, arrived):
-    copies = [
-        pltpu.make_async_copy(
-            tok_ref.at[:, pl.ds(features_at(own, mask, 0), size)],
-            x_out.at[:, pl.ds(at * size, size)],
-            arrived.at[at],
-        )
-        for at, mask in enumerate((2, 3))
-    ]
-    for copy in copies:
-        copy.start()
-    for copy in copies:
-        copy.wait()
 
 
 def prepare(own, chunks, tok_ref, grad_ref, cos_ref, sin_ref, scaled_out, core_out, own_out, inv_out, *x_outs):
@@ -241,18 +227,23 @@
     own = key_weight.shape[0]
     core, over = 1, 2
     swap = functools.partial(swap_narrow, narrow_size=narrow_size)
-    summed = functools.partial(swap_wide, wide_size=wide_size, narrow_size=narrow_size)
+
+    def summed(value, chunk, *stages):
+        return swap_wide(value, wide_size, narrow_size, chunk, *stages)
+
     chunks = []
     for eighths in CHUNKS:
         chunks.append((sum(size for _, size in chunks), own * eighths // 8))
     gain_row = norm_gain.reshape(1, own)
 
-    (x_first,) = call(
-        functools.partial(first_tokens, own, chunks[0][1]),
-        [((rows, 2 * chunks[0][1]), BF16)],
-        tokens,
-        anywhere=(0,),
-        scratch=[pltpu.SemaphoreType.DMA((2,))],
+    x_first = jnp.concatenate(
+        [
+            lax.dynamic_slice(
+                tokens, (0, (lax.axis_index("narrow") ^ mask) * own), (rows, chunks[0][1])
+            )
+            for mask in (2, 3)
+        ],
+        axis=1,
     )
     x_in = [swap(x_first, mask=over)]
     scaled, core_out, own_tokens, inv_rms, *x_outs = call(
@@ -293,11 +284,11 @@
 
     count = len(chunks)
     totals = []
-    got = [summed(send_half, chunk=k, stage=0) for k, (_, send_half) in enumerate(state)]
+    got = [summed(send_half, k, 0) for k, (_, send_half) in enumerate(state)]
     for k in range(count):
         totals.append(state[k][0] + after(got[k], latest).astype(F32))
         latest = totals[-1]
-    got = [summed(total[1].astype(BF16), chunk=k, stage=1) for k, total in enumerate(totals)]
+    got = [summed(total[1].astype(BF16), k, 1) for k, total in enumerate(totals)]
     for k in range(count):
         totals[k] = totals[k][0] + after(got[k], latest).astype(F32)
         latest = totals[k]
@@ -306,13 +297,13 @@
     latest = pair
     for stage in range(2, wide_size.bit_length() - 1):
         rounded = [total.astype(BF16) for total in totals]
-        got = [summed(value, chunk=k, stage=stage) for k, value in enumerate(rounded)]
+        got = [summed(value, k, stage) for k, value in enumerate(rounded)]
         for k in range(count):
             totals[k] = rounded[k].astype(F32) + after(got[k], latest).astype(F32)
             latest = totals[k]
     mine = [total.astype(BF16) for total in totals]
-    near = [summed(value, chunk=k, stage=1) for k, value in enumerate(mine)]
-    far = [summed(value, chunk=k, stage=0) for k, value in enumerate(mine)]
+    near = [summed(value, k, 1) for k, value in enumerate(mine)]
+    far = [summed(value, k, 0) for k, value in enumerate(mine)]
     def write(k, half, parts):
         start, size = chunks[k]
         final = half == 1 and k == count - 1
@@ -321,10 +312,11 @@
         )
 
     before = ()
+    straight = {k: summed(mine[k], k, 0, 1) for k in (1,)}
     last = []
     for k in range(count):
         near[k] = after(near[k], latest)
-        last.append(summed(near[k], chunk=k, stage=0))
+        last.append(straight[k] if k in straight else summed(near[k], k, 0))
         far[k] = after(far[k], near[k])
         before = write(k, 0, (mine[k], near[k], far[k]))
         latest = before[1]

time: 54.7 us -> 54.1 us (0.989)
  waiting for transfers between devices: 13.6 us -> 12.4 us
  starting transfers between devices: 30.2 us -> 31 us
    unnamed x10 -> x8, local copies, waits for them, and re-layouts: 2.13 us -> 0.91 us
    ppermute x12, waiting for transfers between devices: 4.69 us -> 3.56 us  [swap_wide(): return lax.ppermute(value, BOTH, pairs)]
    dynamic_slice x0 -> x1, local copies, waits for them, and re-layouts: none -> 1.08 us  [by_permutes(): lax.dynamic_slice(tokens, (0, (lax.axis_index('narrow') ^ mask) * own), (...]
    ppermute x12, starting transfers between devices: 22.8 us -> 23.5 us  [swap_wide(): return lax.ppermute(value, BOTH, pairs)]
    pallas_call x10 -> x9, Pallas kernels: 6.86 us -> 6.8 us  [call(): pl.pallas_call(body, out_shape=[jax.ShapeDtypeStruct(shape, kind) for sha...]
  transfers between devices with their start and end apart: 21 -> 21, of which waited for: 11 -> 9; matrix products, arithmetic and copies ran while one was open for 2% -> 2% of each run, Pallas kernels for 11% -> 11%
where the time goes in v7:
time: 54.1 us; the launch traced here: 54 us
  starting transfers between devices  31 us (57%)
  waiting for transfers between devices  12.4 us (23%)
  Pallas kernels  6.8 us (13%)
  local copies, waits for them, and re-layouts  2.08 us (4%)
  between operations  0.93 us (2%)
  other arithmetic  0.76 us (1%)
    ppermute x12, starting transfers between devices, swap_wide(): return lax.ppermute(value, BOTH, pairs)  23.5 us
    ppermute x9, waiting for transfers between devices, swap_narrow(): lax.ppermute(value, 'narrow', [(i, i ^ mask) for i in range(narrow_size)])  8.86 us
    ppermute x9, starting transfers between devices, swap_narrow(): lax.ppermute(value, 'narrow', [(i, i ^ mask) for i in range(narrow_size)])  7.44 us
    pallas_call x9, Pallas kernels, call(): pl.pallas_call(body, out_shape=[jax.ShapeDtypeStruct(shape, kind) for sha...  6.8 us
    ppermute x12, waiting for transfers between devices, swap_wide(): return lax.ppermute(value, BOTH, pairs)  3.56 us
  transfers between devices with their start and end apart: 21, of which 9 were waited for; matrix products, arithmetic and copies ran while one was open for 2% of the time, Pallas kernels for 11%

profile of v7, /device:TPU:0, one launch (start us, length us, event | category | flops | bytes accessed | tf_op | source)
XLA Modules:
  0.0 54.0 jit_solution(436399318640857548)
XLA Ops:
  0.7 1.1 %constant_dynamic-slice_fusion.1 = (bf16[128,512]{1,0:T(8,128)(2,1)S(1)}, bf16[128,512]{1,0:T(8,128)(2,1)S(1)}) fusion(bf16[128,4096]{1,0:T(8,128)(2,1)} %tok_ref, s32[]{:T(128)S(6)} %select_n.17, s32[]{:T(128)S(6)} %select_n.18), kind=kLoop, calls=%fused_computation.27 | loop fusion | bytes 524296 | tf_op jit(solution)/shard_map/dynamic_slice | solution.py:241
  1.8 3.0 %collective-permute-start.2 = (bf16[128,1024]{1,0:T(8,128)(2,1)S(1)}, bf16[128,1024]{1,0:T(8,128)(2,1)S(1)}, u32[]{:S(2)}, u32[]{:S(2)}) collective-permute-start(bf16[128,1024]{1,0:T(8,128)(2,1)S(1)} %pad_maximum_fusion), channel_id=1, source_target_pairs={{0,2},{1,3},{2,0},{3,1},{4,6},{5,7},{6,4},{7,5},{8,10},{9,11},{10,... | collective-permute-start | bytes 786440 | tf_op jit(solution)/shard_map/ppermute | solution.py:73
  5.3 0.9 %copy-done.2 = bf16[128,512]{1,0:T(8,128)(2,1)S(1)} copy-done((bf16[128,512]{1,0:T(8,128)(2,1)S(1)}, bf16[128,512]{1,0:T(8,128)(2,1)}, u32[]{:S(2)}) %copy-start.2) | copy-done | bytes 131096
  6.7 2.0 %collective-permute-start.1 = (bf16[128,1024]{1,0:T(8,128)(2,1)S(1)}, bf16[128,1024]{1,0:T(8,128)(2,1)S(1)}, u32[]{:S(2)}, u32[]{:S(2)}) collective-permute-start(bf16[128,1024]{1,0:T(8,128)(2,1)S(1)} %get-tuple-element.42), channel_id=1, source_target_pairs={{0,2},{1,3},{2,0},{3,1},{4,6},{5,7},{6,4},{7,5},{8,10},{9,11},{10,... | collective-permute-start | bytes 786440 | tf_op jit(solution)/shard_map/ppermute | solution.py:73
  8.7 6.0 %collective-permute-done.4.x_grad = bf16[128,512]{1,0:T(8,128)(2,1)S(1)} collective-permute-done((bf16[128,512]{1,0:T(8,128)(2,1)S(1)}, bf16[128,512]{1,0:T(8,128)(2,1)S(1)}, u32[]{:S(2)}, u32[]{:S(2)}) %collective-permute-start.4) | collective-permute-done | bytes 131104 | tf_op jit(solution)/shard_map/ppermute | solution.py:73
  14.7 0.6 %collective-permute-start.3 = (bf16[128,512]{1,0:T(8,128)(2,1)S(1)}, bf16[128,512]{1,0:T(8,128)(2,1)S(1)}, u32[]{:S(2)}, u32[]{:S(2)}) collective-permute-start(bf16[128,512]{1,0:T(8,128)(2,1)S(1)} %slice.35), channel_id=1, source_target_pairs={{0,1},{1,0},{2,3},{3,2},{4,5},{5,4},{6,7},{7,6},{8,9},{9,8},{10,11... | collective-permute-start | bytes 393224 | tf_op jit(solution)/shard_map/ppermute | solution.py:73
  15.3 0.8 %collective-permute-done.5.last_grad = bf16[128,512]{1,0:T(8,128)(2,1)S(1)} collective-permute-done((bf16[128,512]{1,0:T(8,128)(2,1)S(1)}, bf16[128,512]{1,0:T(8,128)(2,1)S(1)}, u32[]{:S(2)}, u32[]{:S(2)}) %collective-permute-start.5) | collective-permute-done | bytes 131104 | tf_op jit(solution)/shard_map/ppermute | solution.py:73
  16.3 0.5 shard_map.68
  16.8 2.2 %collective-permute-start.9 = (bf16[2,512,128]{2,1,0:T(8,128)(2,1)S(1)}, bf16[2,512,128]{2,1,0:T(8,128)(2,1)S(1)}, u32[]{:S(2)}, u32[]{:S(2)}) collective-permute-start(bf16[2,512,128]{2,1,0:T(8,128)(2,1)S(1)} %get-tuple-element.44), channel_id=1, source_target_pairs={{0,8},{1,5},{2,10},{3,7},{4,12},{5,1},{6,14},{7,3},{8,0},{9,13},{1... | collective-permute-start | bytes 786440 | tf_op jit(solution)/shard_map/ppermute | solution.py:69
  19.0 0.5 collective-permute-done.1.x_ref.rest_1_
  19.6 1.3 %collective-permute-done.6.last_ref.rest_3_ = bf16[128,512]{1,0:T(8,128)(2,1)S(1)} collective-permute-done((bf16[128,512]{1,0:T(8,128)(2,1)S(1)}, bf16[128,512]{1,0:T(8,128)(2,1)S(1)}, u32[]{:S(2)}, u32[]{:S(2)}) %collective-permute-start.6) | collective-permute-done | bytes 131104 | tf_op jit(solution)/shard_map/ppermute | solution.py:73
  21.4 1.8 %collective-permute-start.8 = (bf16[2,512,128]{2,1,0:T(8,128)(2,1)S(1)}, bf16[2,512,128]{2,1,0:T(8,128)(2,1)S(1)}, u32[]{:S(2)}, u32[]{:S(2)}) collective-permute-start(bf16[2,512,128]{2,1,0:T(8,128)(2,1)S(1)} %get-tuple-element.46), channel_id=1, source_target_pairs={{0,4},{1,9},{2,6},{3,11},{4,0},{5,13},{6,2},{7,15},{8,12},{9,1},{1... | collective-permute-start | bytes 786440 | tf_op jit(solution)/shard_map/ppermute | solution.py:69
  23.3 0.7 %shard_map.70 = (f32[256,512]{1,0:T(8,128)S(1)}, bf16[256,512]{1,0:T(8,128)(2,1)S(1)}) custom-call(bf16[1,1024]{1,0:T(2,128)(2,1)S(1)} %reshape.35.gain_ref, bf16[1024,512]{1,0:T(8,128)(2,1)S(1)} %copy-done, bf16[128,1024]{1,0:T(8,128)(2,1)S(1)} %get-tuple-element.40.own_ref, bf16[128,1536]{1,0:T(8,128)(2,1)S(1)} %collective-permute-done.core_ref, ...), custom_call_target="tpu_custom_call" | custom-call | tf_op jit(solution)/shard_map/pallas_call | solution.py:83
  24.1 2.7 %collective-permute-start.11 = (bf16[512,128]{1,0:T(8,128)(2,1)S(1)}, bf16[512,128]{1,0:T(8,128)(2,1)S(1)}, u32[]{:S(2)}, u32[]{:S(2)}) collective-permute-start(bf16[512,128]{1,0:T(8,128)(2,1)S(1)} %fusion.3), channel_id=1, source_target_pairs={{0,16},{1,9},{2,18},{3,11},{4,20},{5,13},{6,22},{7,15},{8,24},{9,1... | collective-permute-start | bytes 393224 | tf_op jit(solution)/shard_map/ppermute | solution.py:69
  26.8 1.1 %collective-permute-done.8 = bf16[2,512,128]{2,1,0:T(8,128)(2,1)S(1)} collective-permute-done((bf16[2,512,128]{2,1,0:T(8,128)(2,1)S(1)}, bf16[2,512,128]{2,1,0:T(8,128)(2,1)S(1)}, u32[]{:S(2)}, u32[]{:S(2)}) %collective-permute-start.8) | collective-permute-done | bytes 262176 | tf_op jit(solution)/shard_map/ppermute | solution.py:69
  27.9 1.9 %collective-permute-start.10 = (bf16[512,128]{1,0:T(8,128)(2,1)S(1)}, bf16[512,128]{1,0:T(8,128)(2,1)S(1)}, u32[]{:S(2)}, u32[]{:S(2)}) collective-permute-start(bf16[512,128]{1,0:T(8,128)(2,1)S(1)} %fusion.2), channel_id=1, source_target_pairs={{0,8},{1,5},{2,10},{3,7},{4,12},{5,1},{6,14},{7,3},{8,0},{9,13},{1... | collective-permute-start | bytes 393224 | tf_op jit(solution)/shard_map/ppermute | solution.py:69
  29.8 0.6 %collective-permute-done.11 = bf16[512,128]{1,0:T(8,128)(2,1)S(1)} collective-permute-done((bf16[512,128]{1,0:T(8,128)(2,1)S(1)}, bf16[512,128]{1,0:T(8,128)(2,1)S(1)}, u32[]{:S(2)}, u32[]{:S(2)}) %collective-permute-start.11) | collective-permute-done | bytes 131104 | tf_op jit(solution)/shard_map/ppermute | solution.py:69
  30.4 1.7 %collective-permute-start.14 = (bf16[512,128]{1,0:T(8,128)(2,1)S(1)}, bf16[512,128]{1,0:T(8,128)(2,1)S(1)}, u32[]{:S(2)}, u32[]{:S(2)}) collective-permute-start(bf16[512,128]{1,0:T(8,128)(2,1)S(1)} %fusion), channel_id=1, source_target_pairs={{0,4},{1,17},{2,6},{3,19},{4,0},{5,21},{6,2},{7,23},{8,12},{9,25},... | collective-permute-start | bytes 393224 | tf_op jit(solution)/shard_map/ppermute | solution.py:69
  32.1 0.9 %collective-permute-done.10 = bf16[512,128]{1,0:T(8,128)(2,1)S(1)} collective-permute-done((bf16[512,128]{1,0:T(8,128)(2,1)S(1)}, bf16[512,128]{1,0:T(8,128)(2,1)S(1)}, u32[]{:S(2)}, u32[]{:S(2)}) %collective-permute-start.10) | collective-permute-done | bytes 131104 | tf_op jit(solution)/shard_map/ppermute | solution.py:69
  33.0 4.0 %collective-permute-start.13 = (bf16[512,128]{1,0:T(8,128)(2,1)S(1)}, bf16[512,128]{1,0:T(8,128)(2,1)S(1)}, u32[]{:S(2)}, u32[]{:S(2)}) collective-permute-start(bf16[512,128]{1,0:T(8,128)(2,1)S(1)} %fusion.1), channel_id=1, source_target_pairs={{0,16},{1,17},{2,18},{3,19},{4,20},{5,21},{6,22},{7,23},{8,24},{9,... | collective-permute-start | bytes 393224 | tf_op jit(solution)/shard_map/ppermute | solution.py:69
  37.1 0.8 %collective-permute-start.16 = (bf16[512,128]{1,0:T(8,128)(2,1)S(1)}, bf16[512,128]{1,0:T(8,128)(2,1)S(1)}, u32[]{:S(2)}, u32[]{:S(2)}) collective-permute-start(bf16[512,128]{1,0:T(8,128)(2,1)S(1)} %fusion.7.rest_0_), channel_id=1, source_target_pairs={{0,16},{1,9},{2,18},{3,11},{4,20},{5,13},{6,22},{7,15},{8,24},{9,1... | collective-permute-start | bytes 393224 | tf_op jit(solution)/shard_map/ppermute | solution.py:69
  37.9 2.8 %collective-permute-start.17 = (bf16[512,128]{1,0:T(8,128)(2,1)S(1)}, bf16[512,128]{1,0:T(8,128)(2,1)S(1)}, u32[]{:S(2)}, u32[]{:S(2)}) collective-permute-start(bf16[512,128]{1,0:T(8,128)(2,1)S(1)} %fusion.7.rest_0_), channel_id=1, source_target_pairs={{0,8},{1,5},{2,10},{3,7},{4,12},{5,1},{6,14},{7,3},{8,0},{9,13},{1... | collective-permute-start | bytes 393224 | tf_op jit(solution)/shard_map/ppermute | solution.py:69
  40.7 1.0 %collective-permute-done.13 = bf16[512,128]{1,0:T(8,128)(2,1)S(1)} collective-permute-done((bf16[512,128]{1,0:T(8,128)(2,1)S(1)}, bf16[512,128]{1,0:T(8,128)(2,1)S(1)}, u32[]{:S(2)}, u32[]{:S(2)}) %collective-permute-start.13) | collective-permute-done | bytes 131104 | tf_op jit(solution)/shard_map/ppermute | solution.py:69
  41.8 1.5 %collective-permute-start.15 = (bf16[512,128]{1,0:T(8,128)(2,1)S(1)}, bf16[512,128]{1,0:T(8,128)(2,1)S(1)}, u32[]{:S(2)}, u32[]{:S(2)}) collective-permute-start(bf16[512,128]{1,0:T(8,128)(2,1)S(1)} %fusion.8.rest_0_), channel_id=1, source_target_pairs={{0,8},{1,5},{2,10},{3,7},{4,12},{5,1},{6,14},{7,3},{8,0},{9,13},{1... | collective-permute-start | bytes 393224 | tf_op jit(solution)/shard_map/ppermute | solution.py:69
  43.8 1.6 %collective-permute-start.12 = (bf16[128,512]{1,0:T(8,128)(2,1)S(1)}, bf16[128,512]{1,0:T(8,128)(2,1)S(1)}, u32[]{:S(2)}, u32[]{:S(2)}) collective-permute-start(bf16[128,512]{1,0:T(8,128)(2,1)S(1)} %slice.55), channel_id=1, source_target_pairs={{0,2},{1,3},{2,0},{3,1},{4,6},{5,7},{6,4},{7,5},{8,10},{9,11},{10,... | collective-permute-start | bytes 393224 | tf_op jit(solution)/shard_map/ppermute | solution.py:73
  45.3 1.8 %collective-permute-start.20 = (bf16[512,128]{1,0:T(8,128)(2,1)S(1)}, bf16[512,128]{1,0:T(8,128)(2,1)S(1)}, u32[]{:S(2)}, u32[]{:S(2)}) collective-permute-start(bf16[512,128]{1,0:T(8,128)(2,1)S(1)} %collective-permute-done.16.rest_1_), channel_id=1, source_target_pairs={{0,8},{1,5},{2,10},{3,7},{4,12},{5,1},{6,14},{7,3},{8,0},{9,13},{1... | collective-permute-start | bytes 393224 | tf_op jit(solution)/shard_map/ppermute | solution.py:69
  47.2 1.9 %collective-permute-start.19 = (bf16[512,128]{1,0:T(8,128)(2,1)S(1)}, bf16[512,128]{1,0:T(8,128)(2,1)S(1)}, u32[]{:S(2)}, u32[]{:S(2)}) collective-permute-start(bf16[512,128]{1,0:T(8,128)(2,1)S(1)} %fusion.8.rest_0_), channel_id=1, source_target_pairs={{0,12},{1,13},{2,14},{3,15},{4,8},{5,9},{6,10},{7,11},{8,4},{9,5},... | collective-permute-start | bytes 393224 | tf_op jit(solution)/shard_map/ppermute | solution.py:69
  49.1 1.1 %shard_map.71 = (f32[1024,512]{1,0:T(8,128)}, f32[8,128]{1,0:T(8,128)S(1)}) custom-call(bf16[1,1024]{1,0:T(2,128)(2,1)S(1)} %reshape.35.gain_ref, bf16[1024,512]{1,0:T(8,128)(2,1)S(1)} %copy-done, bf16[512,128]{1,0:T(8,128)(2,1)S(1)} %fusion.7.rest_0_, bf16[512,128]{1,0:T(8,128)(2,1)S(1)} %collective-permute-done.16.rest_1_, ...), custom_call_target="tpu_custom_call" | custom-call | tf_op jit(solution)/shard_map/pallas_call | solution.py:83
  50.2 1.1 %shard_map.72 = (f32[1024,512]{1,0:T(8,128)}, f32[8,128]{1,0:T(8,128)S(1)}) custom-call(bf16[1,1024]{1,0:T(2,128)(2,1)S(1)} %reshape.35.gain_ref, bf16[1024,512]{1,0:T(8,128)(2,1)S(1)} %copy-done, bf16[512,128]{1,0:T(8,128)(2,1)S(1)} %fusion.8.rest_0_, bf16[512,128]{1,0:T(8,128)(2,1)S(1)} %collective-permute-done.15.rest_1_, ...), custom_call_target="tpu_custom_call", output_to_operand_aliasing={{0}: (5, {})} | custom-call | tf_op jit(solution)/shard_map/pallas_call | solution.py:83
  51.3 0.8 %shard_map.73 = bf16[128,512]{1,0:T(8,128)(2,1)} custom-call(f32[128,512]{1,0:T(8,128)S(1)} %slice.40.mine_ref, bf16[128,512]{1,0:T(8,128)(2,1)S(1)} %collective-permute-done.12.got_ref, f32[128,128]{1,0:T(8,128)S(1)} %get-tuple-element.67.inv_ref, f32[128,128]{1,0:T(8,128)S(1)} %get-tuple-element.80.cos_ref, f32[128,128]{1,0:T(8,128)S(1)} %get-tuple-element.81.sin_ref), custom_call_target="tpu_custom_call" | custom-call | tf_op jit(solution)/shard_map/pallas_call | solution.py:83
  52.1 0.9 %shard_map.74 = (f32[1024,512]{1,0:T(8,128)}, f32[8,128]{1,0:T(8,128)S(1)}) custom-call(bf16[1,1024]{1,0:T(2,128)(2,1)S(1)} %reshape.35.gain_ref, bf16[1024,512]{1,0:T(8,128)(2,1)S(1)} %copy-done, bf16[512,128]{1,0:T(8,128)(2,1)S(1)} %collective-permute-done.20.rest_0_, f32[1024,512]{1,0:T(8,128)} %get-tuple-element.69.rest_1_, ...), custom_call_target="tpu_custom_call", output_to_operand_aliasing={{0}: (3, {})} | custom-call | tf_op jit(solution)/shard_map/pallas_call | solution.py:83
  53.1 0.9 %shard_map.75 = (f32[1024,512]{1,0:T(8,128)}, f32[8,128]{1,0:T(8,128)}) custom-call(bf16[1,1024]{1,0:T(2,128)(2,1)S(1)} %reshape.35.gain_ref, bf16[1024,512]{1,0:T(8,128)(2,1)S(1)} %copy-done, bf16[512,128]{1,0:T(8,128)(2,1)S(1)} %collective-permute-done.19.rest_0_, f32[1024,512]{1,0:T(8,128)} %get-tuple-element.72.rest_1_, ...), custom_call_target="tpu_custom_call", output_to_operand_aliasing={{0}: (3, {})} | custom-call | tf_op jit(solution)/shard_map/pallas_call | solution.py:83
  (47 shorter events, 2.7 us)
Async XLA Ops:
  0.6 4.6 %copy-start.1 = (bf16[128,4096]{1,0:T(8,128)(2,1)S(1)}, bf16[128,4096]{1,0:T(8,128)(2,1)}, u32[]{:S(2)}) copy-start(bf16[128,4096]{1,0:T(8,128)(2,1)} %tok_ref) | copy-start | bytes 3145732
  1.7 17.9 %copy-start.3 = (bf16[1024]{0:T(1024)(128)(2,1)S(1)}, bf16[1024]{0:T(1024)(128)(2,1)}, u32[]{:S(2)}) copy-start(bf16[1024]{0:T(1024)(128)(2,1)} %param.5) | copy-start | bytes 6148
  1.8 13.0 %collective-permute-start.2 = (bf16[128,1024]{1,0:T(8,128)(2,1)S(1)}, bf16[128,1024]{1,0:T(8,128)(2,1)S(1)}, u32[]{:S(2)}, u32[]{:S(2)}) collective-permute-start(bf16[128,1024]{1,0:T(8,128)(2,1)S(1)} %pad_maximum_fusion), channel_id=1, source_target_pairs={{0,2},{1,3},{2,0},{3,1},{4,6},{5,7},{6,4},{7,5},{8,10},{9,11},{10,... | collective-permute-start | bytes 786440 | tf_op jit(solution)/shard_map/ppermute | solution.py:73
  5.2 0.9 %copy-start.2 = (bf16[128,512]{1,0:T(8,128)(2,1)S(1)}, bf16[128,512]{1,0:T(8,128)(2,1)}, u32[]{:S(2)}) copy-start(bf16[128,512]{1,0:T(8,128)(2,1)} %grad_ref.1) | copy-start | bytes 393220
  6.1 17.1 %copy-start = (bf16[1024,512]{1,0:T(8,128)(2,1)S(1)}, bf16[1024,512]{1,0:T(8,128)(2,1)}, u32[]{:S(2)}) copy-start(bf16[1024,512]{1,0:T(8,128)(2,1)} %weight_ref.8) | copy-start | bytes 3145732
  6.5 9.8 %collective-permute-start = (bf16[128,1536]{1,0:T(8,128)(2,1)S(1)}, bf16[128,1536]{1,0:T(8,128)(2,1)S(1)}, u32[]{:S(2)}, u32[]{:S(2)}) collective-permute-start(bf16[128,1536]{1,0:T(8,128)(2,1)S(1)} %get-tuple-element.41), channel_id=1, source_target_pairs={{0,1},{1,0},{2,3},{3,2},{4,5},{5,4},{6,7},{7,6},{8,9},{9,8},{10,11... | collective-permute-start | bytes 1179656 | tf_op jit(solution)/shard_map/ppermute | solution.py:73
  6.6 8.1 %collective-permute-start.4 = (bf16[128,512]{1,0:T(8,128)(2,1)S(1)}, bf16[128,512]{1,0:T(8,128)(2,1)S(1)}, u32[]{:S(2)}, u32[]{:S(2)}) collective-permute-start(bf16[128,512]{1,0:T(8,128)(2,1)S(1)} %get-tuple-element.43.scaled_ref), channel_id=1, source_target_pairs={{0,2},{1,3},{2,0},{3,1},{4,6},{5,7},{6,4},{7,5},{8,10},{9,11},{10,... | collective-permute-start | bytes 393224 | tf_op jit(solution)/shard_map/ppermute | solution.py:73
  6.7 12.8 %collective-permute-start.1 = (bf16[128,1024]{1,0:T(8,128)(2,1)S(1)}, bf16[128,1024]{1,0:T(8,128)(2,1)S(1)}, u32[]{:S(2)}, u32[]{:S(2)}) collective-permute-start(bf16[128,1024]{1,0:T(8,128)(2,1)S(1)} %get-tuple-element.42), channel_id=1, source_target_pairs={{0,2},{1,3},{2,0},{3,1},{4,6},{5,7},{6,4},{7,5},{8,10},{9,11},{10,... | collective-permute-start | bytes 786440 | tf_op jit(solution)/shard_map/ppermute | solution.py:73
  14.7 1.3 %collective-permute-start.5 = (bf16[128,512]{1,0:T(8,128)(2,1)S(1)}, bf16[128,512]{1,0:T(8,128)(2,1)S(1)}, u32[]{:S(2)}, u32[]{:S(2)}) collective-permute-start(bf16[128,512]{1,0:T(8,128)(2,1)S(1)} %collective-permute-done.4.x_grad), channel_id=1, source_target_pairs={{0,1},{1,0},{2,3},{3,2},{4,5},{5,4},{6,7},{7,6},{8,9},{9,8},{10,11... | collective-permute-start | bytes 393224 | tf_op jit(solution)/shard_map/ppermute | solution.py:73
  14.7 1.6 %collective-permute-start.3 = (bf16[128,512]{1,0:T(8,128)(2,1)S(1)}, bf16[128,512]{1,0:T(8,128)(2,1)S(1)}, u32[]{:S(2)}, u32[]{:S(2)}) collective-permute-start(bf16[128,512]{1,0:T(8,128)(2,1)S(1)} %slice.35), channel_id=1, source_target_pairs={{0,1},{1,0},{2,3},{3,2},{4,5},{5,4},{6,7},{7,6},{8,9},{9,8},{10,11... | collective-permute-start | bytes 393224 | tf_op jit(solution)/shard_map/ppermute | solution.py:73
  16.8 7.3 %collective-permute-start.9 = (bf16[2,512,128]{2,1,0:T(8,128)(2,1)S(1)}, bf16[2,512,128]{2,1,0:T(8,128)(2,1)S(1)}, u32[]{:S(2)}, u32[]{:S(2)}) collective-permute-start(bf16[2,512,128]{2,1,0:T(8,128)(2,1)S(1)} %get-tuple-element.44), channel_id=1, source_target_pairs={{0,8},{1,5},{2,10},{3,7},{4,12},{5,1},{6,14},{7,3},{8,0},{9,13},{1... | collective-permute-start | bytes 786440 | tf_op jit(solution)/shard_map/ppermute | solution.py:69
  19.5 1.4 %collective-permute-start.6 = (bf16[128,512]{1,0:T(8,128)(2,1)S(1)}, bf16[128,512]{1,0:T(8,128)(2,1)S(1)}, u32[]{:S(2)}, u32[]{:S(2)}) collective-permute-start(bf16[128,512]{1,0:T(8,128)(2,1)S(1)} %slice.28), channel_id=1, source_target_pairs={{0,1},{1,0},{2,3},{3,2},{4,5},{5,4},{6,7},{7,6},{8,9},{9,8},{10,11... | collective-permute-start | bytes 393224 | tf_op jit(solution)/shard_map/ppermute | solution.py:73
  21.4 6.4 %collective-permute-start.8 = (bf16[2,512,128]{2,1,0:T(8,128)(2,1)S(1)}, bf16[2,512,128]{2,1,0:T(8,128)(2,1)S(1)}, u32[]{:S(2)}, u32[]{:S(2)}) collective-permute-start(bf16[2,512,128]{2,1,0:T(8,128)(2,1)S(1)} %get-tuple-element.46), channel_id=1, source_target_pairs={{0,4},{1,9},{2,6},{3,11},{4,0},{5,13},{6,2},{7,15},{8,12},{9,1},{1... | collective-permute-start | bytes 786440 | tf_op jit(solution)/shard_map/ppermute | solution.py:69
  24.0 13.0 %collective-permute-start.7 = (bf16[256,512]{1,0:T(8,128)(2,1)S(1)}, bf16[256,512]{1,0:T(8,128)(2,1)S(1)}, u32[]{:S(2)}, u32[]{:S(2)}) collective-permute-start(bf16[256,512]{1,0:T(8,128)(2,1)S(1)} %get-tuple-element.49), channel_id=1, source_target_pairs={{0,1},{1,0},{2,3},{3,2},{4,5},{5,4},{6,7},{7,6},{8,9},{9,8},{10,11... | collective-permute-start | bytes 786440 | tf_op jit(solution)/shard_map/ppermute | solution.py:73
  24.1 6.2 %collective-permute-start.11 = (bf16[512,128]{1,0:T(8,128)(2,1)S(1)}, bf16[512,128]{1,0:T(8,128)(2,1)S(1)}, u32[]{:S(2)}, u32[]{:S(2)}) collective-permute-start(bf16[512,128]{1,0:T(8,128)(2,1)S(1)} %fusion.3), channel_id=1, source_target_pairs={{0,16},{1,9},{2,18},{3,11},{4,20},{5,13},{6,22},{7,15},{8,24},{9,1... | collective-permute-start | bytes 393224 | tf_op jit(solution)/shard_map/ppermute | solution.py:69
  27.9 5.0 %collective-permute-start.10 = (bf16[512,128]{1,0:T(8,128)(2,1)S(1)}, bf16[512,128]{1,0:T(8,128)(2,1)S(1)}, u32[]{:S(2)}, u32[]{:S(2)}) collective-permute-start(bf16[512,128]{1,0:T(8,128)(2,1)S(1)} %fusion.2), channel_id=1, source_target_pairs={{0,8},{1,5},{2,10},{3,7},{4,12},{5,1},{6,14},{7,3},{8,0},{9,13},{1... | collective-permute-start | bytes 393224 | tf_op jit(solution)/shard_map/ppermute | solution.py:69
  30.4 6.6 %collective-permute-start.14 = (bf16[512,128]{1,0:T(8,128)(2,1)S(1)}, bf16[512,128]{1,0:T(8,128)(2,1)S(1)}, u32[]{:S(2)}, u32[]{:S(2)}) collective-permute-start(bf16[512,128]{1,0:T(8,128)(2,1)S(1)} %fusion), channel_id=1, source_target_pairs={{0,4},{1,17},{2,6},{3,19},{4,0},{5,21},{6,2},{7,23},{8,12},{9,25},... | collective-permute-start | bytes 393224 | tf_op jit(solution)/shard_map/ppermute | solution.py:69
  33.0 8.7 %collective-permute-start.13 = (bf16[512,128]{1,0:T(8,128)(2,1)S(1)}, bf16[512,128]{1,0:T(8,128)(2,1)S(1)}, u32[]{:S(2)}, u32[]{:S(2)}) collective-permute-start(bf16[512,128]{1,0:T(8,128)(2,1)S(1)} %fusion.1), channel_id=1, source_target_pairs={{0,16},{1,17},{2,18},{3,19},{4,20},{5,21},{6,22},{7,23},{8,24},{9,... | collective-permute-start | bytes 393224 | tf_op jit(solution)/shard_map/ppermute | solution.py:69
  37.1 8.2 %collective-permute-start.16 = (bf16[512,128]{1,0:T(8,128)(2,1)S(1)}, bf16[512,128]{1,0:T(8,128)(2,1)S(1)}, u32[]{:S(2)}, u32[]{:S(2)}) collective-permute-start(bf16[512,128]{1,0:T(8,128)(2,1)S(1)} %fusion.7.rest_0_), channel_id=1, source_target_pairs={{0,16},{1,9},{2,18},{3,11},{4,20},{5,13},{6,22},{7,15},{8,24},{9,1... | collective-permute-start | bytes 393224 | tf_op jit(solution)/shard_map/ppermute | solution.py:69
  37.9 9.2 %collective-permute-start.17 = (bf16[512,128]{1,0:T(8,128)(2,1)S(1)}, bf16[512,128]{1,0:T(8,128)(2,1)S(1)}, u32[]{:S(2)}, u32[]{:S(2)}) collective-permute-start(bf16[512,128]{1,0:T(8,128)(2,1)S(1)} %fusion.7.rest_0_), channel_id=1, source_target_pairs={{0,8},{1,5},{2,10},{3,7},{4,12},{5,1},{6,14},{7,3},{8,0},{9,13},{1... | collective-permute-start | bytes 393224 | tf_op jit(solution)/shard_map/ppermute | solution.py:69
  41.8 8.4 %collective-permute-start.15 = (bf16[512,128]{1,0:T(8,128)(2,1)S(1)}, bf16[512,128]{1,0:T(8,128)(2,1)S(1)}, u32[]{:S(2)}, u32[]{:S(2)}) collective-permute-start(bf16[512,128]{1,0:T(8,128)(2,1)S(1)} %fusion.8.rest_0_), channel_id=1, source_target_pairs={{0,8},{1,5},{2,10},{3,7},{4,12},{5,1},{6,14},{7,3},{8,0},{9,13},{1... | collective-permute-start | bytes 393224 | tf_op jit(solution)/shard_map/ppermute | solution.py:69
  43.3 6.9 %collective-permute-start.18 = (bf16[512,128]{1,0:T(8,128)(2,1)S(1)}, bf16[512,128]{1,0:T(8,128)(2,1)S(1)}, u32[]{:S(2)}, u32[]{:S(2)}) collective-permute-start(bf16[512,128]{1,0:T(8,128)(2,1)S(1)} %fusion.8.rest_0_), channel_id=1, source_target_pairs={{0,4},{1,9},{2,6},{3,11},{4,0},{5,13},{6,2},{7,15},{8,12},{9,1},{1... | collective-permute-start | bytes 393224 | tf_op jit(solution)/shard_map/ppermute | solution.py:69
  43.8 7.5 %collective-permute-start.12 = (bf16[128,512]{1,0:T(8,128)(2,1)S(1)}, bf16[128,512]{1,0:T(8,128)(2,1)S(1)}, u32[]{:S(2)}, u32[]{:S(2)}) collective-permute-start(bf16[128,512]{1,0:T(8,128)(2,1)S(1)} %slice.55), channel_id=1, source_target_pairs={{0,2},{1,3},{2,0},{3,1},{4,6},{5,7},{6,4},{7,5},{8,10},{9,11},{10,... | collective-permute-start | bytes 393224 | tf_op jit(solution)/shard_map/ppermute | solution.py:73
  45.3 6.8 %collective-permute-start.20 = (bf16[512,128]{1,0:T(8,128)(2,1)S(1)}, bf16[512,128]{1,0:T(8,128)(2,1)S(1)}, u32[]{:S(2)}, u32[]{:S(2)}) collective-permute-start(bf16[512,128]{1,0:T(8,128)(2,1)S(1)} %collective-permute-done.16.rest_1_), channel_id=1, source_target_pairs={{0,8},{1,5},{2,10},{3,7},{4,12},{5,1},{6,14},{7,3},{8,0},{9,13},{1... | collective-permute-start | bytes 393224 | tf_op jit(solution)/shard_map/ppermute | solution.py:69
  47.2 5.9 %collective-permute-start.19 = (bf16[512,128]{1,0:T(8,128)(2,1)S(1)}, bf16[512,128]{1,0:T(8,128)(2,1)S(1)}, u32[]{:S(2)}, u32[]{:S(2)}) collective-permute-start(bf16[512,128]{1,0:T(8,128)(2,1)S(1)} %fusion.8.rest_0_), channel_id=1, source_target_pairs={{0,12},{1,13},{2,14},{3,15},{4,8},{5,9},{6,10},{7,11},{8,4},{9,5},... | collective-permute-start | bytes 393224 | tf_op jit(solution)/shard_map/ppermute | solution.py:69

commit v8 on v6

--- a/solution.py
+++ b/solution.py
@@ -93,21 +93,6 @@
 
 def features_at(own, mask, start):
     return pl.multiple_of((lax.axis_index("narrow") ^ mask) * own + start, TILE)
-
-
-def first_tokens(own, size, tok_ref, x_out, arrived):
-    copies = [
-        pltpu.make_async_copy(
-            tok_ref.at[:, pl.ds(features_at(own, mask, 0), size)],
-            x_out.at[:, pl.ds(at * size, size)],
-            arrived.at[at],
-        )
-        for at, mask in enumerate((2, 3))
-    ]
-    for copy in copies:
-        copy.start()
-    for copy in copies:
-        copy.wait()
 
 
 def prepare(own, chunks, tok_ref, grad_ref, cos_ref, sin_ref, scaled_out, core_out, own_out, inv_out, *x_outs):
@@ -256,12 +241,14 @@
         chunks.append((sum(size for _, size in chunks), own * eighths // 8))
     gain_row = norm_gain.reshape(1, own)
 
-    (x_first,) = call(
-        functools.partial(first_tokens, own, chunks[0][1]),
-        [((rows, 2 * chunks[0][1]), BF16)],
-        tokens,
-        anywhere=(0,),
-        scratch=[pltpu.SemaphoreType.DMA((2,))],
+    x_first = jnp.concatenate(
+        [
+            lax.dynamic_slice(
+                tokens, (0, (lax.axis_index("narrow") ^ mask) * own), (rows, chunks[0][1])
+            )
+            for mask in (2, 3)
+        ],
+        axis=1,
     )
     x_in = [swap(x_first, mask=over)]
     scaled, core_out, own_tokens, inv_rms, *x_outs = call(
@@ -322,22 +309,25 @@
     mine = [total.astype(BF16) for total in totals]
     near = [summed(value, k, 1) for k, value in enumerate(mine)]
     far = [summed(value, k, 0) for k, value in enumerate(mine)]
-    def write(begin, parts, final, before):
-        jobs = [(*chunks[k], k, begin, len(of_chunk)) for k, of_chunk in enumerate(parts)]
+    def write(of_chunks, begin, parts, final, before):
+        jobs = [(*chunks[k], k, begin, len(part)) for k, part in zip(of_chunks, parts, strict=True)]
         return write_weights(
             jobs, wide_size, grad_scale, final, gain_row, key_weight, sum(parts, ()), before
         )
 
-    near[0] = after(near[0], latest)
-    passed_on = summed(near[0], 0, 0)
-    straight = summed(mine[1], 1, 0, 1)
-    far[0] = after(far[0], near[0])
-    near[1] = after(near[1], far[0])
-    before = write(0, ((mine[0], near[0], far[0]), (mine[1], near[1], far[1])), False, ())
+    before = ()
+    last = []
+    straight = {1: summed(mine[1], 1, 0, 1)}
+    for k in range(count):
+        near[k] = after(near[k], latest)
+        last.append(straight[k] if k in straight else summed(near[k], k, 0))
+        far[k] = after(far[k], near[k])
+        before = write((k,), 0, ((mine[k], near[k], far[k]),), False, before)
+        latest = before[1]
     (keys,) = call(
-        finish_keys, [((rows, KV), BF16)], pair[:rows], after(got_x, before[1], straight), inv_rms, cosine, sine
-    )
-    before = write(3, ((after(passed_on, keys),), (straight,)), True, before)
+        finish_keys, [((rows, KV), BF16)], pair[:rows], after(got_x, latest), inv_rms, cosine, sine
+    )
+    before = write((0, 1), 3, ((after(last[0], keys),), (last[1],)), True, before)
     weight_grad, gain_grad = before
     return keys, weight_grad, gain_grad.reshape(own)
 

time: 54.6 us -> 54.3 us (level)
  waiting for transfers between devices: 15.4 us -> 13.3 us
  starting transfers between devices: 29.7 us -> 31 us
  Pallas kernels: 5.39 us -> 6.06 us
    ppermute x12, waiting for transfers between devices: 6.53 us -> 4.45 us  [swap_wide(): return lax.ppermute(value, BOTH, pairs)]
    unnamed x10 -> x8, local copies, waits for them, and re-layouts: 2.13 us -> 0.91 us
    ppermute x12, starting transfers between devices: 22.3 us -> 23.5 us  [swap_wide(): return lax.ppermute(value, BOTH, pairs)]
    dynamic_slice x0 -> x1, local copies, waits for them, and re-layouts: none -> 1.08 us  [by_permutes(): lax.dynamic_slice(tokens, (0, (lax.axis_index('narrow') ^ mask) * own), (...]
    pallas_call x8, Pallas kernels: 5.39 us -> 6.06 us  [call(): pl.pallas_call(body, out_shape=[jax.ShapeDtypeStruct(shape, kind) for sha...]
  transfers between devices with their start and end apart: 21 -> 21, of which waited for: 13 -> 10; matrix products, arithmetic and copies ran while one was open for 2% -> 2% of each run, Pallas kernels for 8% -> 9%
where the time goes in v8:
time: 54.3 us; the launch traced here: 54.1 us
  starting transfers between devices  31 us (57%)
  waiting for transfers between devices  13.3 us (24%)
  Pallas kernels  6.06 us (11%)
  local copies, waits for them, and re-layouts  2.08 us (4%)
  between operations  0.92 us (2%)
  other arithmetic  0.77 us (1%)
    ppermute x12, starting transfers between devices, swap_wide(): return lax.ppermute(value, BOTH, pairs)  23.5 us
    ppermute x9, waiting for transfers between devices, swap_narrow(): lax.ppermute(value, 'narrow', [(i, i ^ mask) for i in range(narrow_size)])  8.86 us
    ppermute x9, starting transfers between devices, swap_narrow(): lax.ppermute(value, 'narrow', [(i, i ^ mask) for i in range(narrow_size)])  7.44 us
    pallas_call x8, Pallas kernels, call(): pl.pallas_call(body, out_shape=[jax.ShapeDtypeStruct(shape, kind) for sha...  6.06 us
    ppermute x12, waiting for transfers between devices, swap_wide(): return lax.ppermute(value, BOTH, pairs)  4.45 us
  transfers between devices with their start and end apart: 21, of which 10 were waited for; matrix products, arithmetic and copies ran while one was open for 2% of the time, Pallas kernels for 9%

profile of v8, /device:TPU:0, one launch (start us, length us, event | category | flops | bytes accessed | tf_op | source)
XLA Modules:
  0.0 54.1 jit_solution(15147060319327792745)
XLA Ops:
  0.7 1.1 %constant_dynamic-slice_fusion.1 = (bf16[128,512]{1,0:T(8,128)(2,1)S(1)}, bf16[128,512]{1,0:T(8,128)(2,1)S(1)}) fusion(bf16[128,4096]{1,0:T(8,128)(2,1)} %tok_ref, s32[]{:T(128)S(6)} %select_n.17, s32[]{:T(128)S(6)} %select_n.18), kind=kLoop, calls=%fused_computation.27 | loop fusion | bytes 524296 | tf_op jit(solution)/shard_map/dynamic_slice | solution.py:246
  1.8 3.0 %collective-permute-start.2 = (bf16[128,1024]{1,0:T(8,128)(2,1)S(1)}, bf16[128,1024]{1,0:T(8,128)(2,1)S(1)}, u32[]{:S(2)}, u32[]{:S(2)}) collective-permute-start(bf16[128,1024]{1,0:T(8,128)(2,1)S(1)} %pad_maximum_fusion), channel_id=1, source_target_pairs={{0,2},{1,3},{2,0},{3,1},{4,6},{5,7},{6,4},{7,5},{8,10},{9,11},{10,... | collective-permute-start | bytes 786440 | tf_op jit(solution)/shard_map/ppermute | solution.py:73
  5.3 0.9 %copy-done.2 = bf16[128,512]{1,0:T(8,128)(2,1)S(1)} copy-done((bf16[128,512]{1,0:T(8,128)(2,1)S(1)}, bf16[128,512]{1,0:T(8,128)(2,1)}, u32[]{:S(2)}) %copy-start.2) | copy-done | bytes 131096
  6.7 2.0 %collective-permute-start.1 = (bf16[128,1024]{1,0:T(8,128)(2,1)S(1)}, bf16[128,1024]{1,0:T(8,128)(2,1)S(1)}, u32[]{:S(2)}, u32[]{:S(2)}) collective-permute-start(bf16[128,1024]{1,0:T(8,128)(2,1)S(1)} %get-tuple-element.39), channel_id=1, source_target_pairs={{0,2},{1,3},{2,0},{3,1},{4,6},{5,7},{6,4},{7,5},{8,10},{9,11},{10,... | collective-permute-start | bytes 786440 | tf_op jit(solution)/shard_map/ppermute | solution.py:73
  8.7 6.0 %collective-permute-done.4.x_grad = bf16[128,512]{1,0:T(8,128)(2,1)S(1)} collective-permute-done((bf16[128,512]{1,0:T(8,128)(2,1)S(1)}, bf16[128,512]{1,0:T(8,128)(2,1)S(1)}, u32[]{:S(2)}, u32[]{:S(2)}) %collective-permute-start.4) | collective-permute-done | bytes 131104 | tf_op jit(solution)/shard_map/ppermute | solution.py:73
  14.7 0.6 %collective-permute-start.3 = (bf16[128,512]{1,0:T(8,128)(2,1)S(1)}, bf16[128,512]{1,0:T(8,128)(2,1)S(1)}, u32[]{:S(2)}, u32[]{:S(2)}) collective-permute-start(bf16[128,512]{1,0:T(8,128)(2,1)S(1)} %slice.35), channel_id=1, source_target_pairs={{0,1},{1,0},{2,3},{3,2},{4,5},{5,4},{6,7},{7,6},{8,9},{9,8},{10,11... | collective-permute-start | bytes 393224 | tf_op jit(solution)/shard_map/ppermute | solution.py:73
  15.3 0.8 %collective-permute-done.5.last_grad = bf16[128,512]{1,0:T(8,128)(2,1)S(1)} collective-permute-done((bf16[128,512]{1,0:T(8,128)(2,1)S(1)}, bf16[128,512]{1,0:T(8,128)(2,1)S(1)}, u32[]{:S(2)}, u32[]{:S(2)}) %collective-permute-start.5) | collective-permute-done | bytes 131104 | tf_op jit(solution)/shard_map/ppermute | solution.py:73
  16.3 0.5 shard_map.68
  16.8 2.2 %collective-permute-start.9 = (bf16[2,512,128]{2,1,0:T(8,128)(2,1)S(1)}, bf16[2,512,128]{2,1,0:T(8,128)(2,1)S(1)}, u32[]{:S(2)}, u32[]{:S(2)}) collective-permute-start(bf16[2,512,128]{2,1,0:T(8,128)(2,1)S(1)} %get-tuple-element.41), channel_id=1, source_target_pairs={{0,8},{1,5},{2,10},{3,7},{4,12},{5,1},{6,14},{7,3},{8,0},{9,13},{1... | collective-permute-start | bytes 786440 | tf_op jit(solution)/shard_map/ppermute | solution.py:69
  19.0 0.5 collective-permute-done.1.x_ref.rest_1_
  19.6 1.3 %collective-permute-done.6.last_ref.rest_3_ = bf16[128,512]{1,0:T(8,128)(2,1)S(1)} collective-permute-done((bf16[128,512]{1,0:T(8,128)(2,1)S(1)}, bf16[128,512]{1,0:T(8,128)(2,1)S(1)}, u32[]{:S(2)}, u32[]{:S(2)}) %collective-permute-start.6) | collective-permute-done | bytes 131104 | tf_op jit(solution)/shard_map/ppermute | solution.py:73
  21.4 1.8 %collective-permute-start.8 = (bf16[2,512,128]{2,1,0:T(8,128)(2,1)S(1)}, bf16[2,512,128]{2,1,0:T(8,128)(2,1)S(1)}, u32[]{:S(2)}, u32[]{:S(2)}) collective-permute-start(bf16[2,512,128]{2,1,0:T(8,128)(2,1)S(1)} %get-tuple-element.43), channel_id=1, source_target_pairs={{0,4},{1,9},{2,6},{3,11},{4,0},{5,13},{6,2},{7,15},{8,12},{9,1},{1... | collective-permute-start | bytes 786440 | tf_op jit(solution)/shard_map/ppermute | solution.py:69
  23.3 0.7 %shard_map.70 = (f32[256,512]{1,0:T(8,128)S(1)}, bf16[256,512]{1,0:T(8,128)(2,1)S(1)}) custom-call(bf16[1,1024]{1,0:T(2,128)(2,1)S(1)} %reshape.35.gain_ref, bf16[1024,512]{1,0:T(8,128)(2,1)S(1)} %copy-done, bf16[128,1024]{1,0:T(8,128)(2,1)S(1)} %get-tuple-element.37.own_ref, bf16[128,1536]{1,0:T(8,128)(2,1)S(1)} %collective-permute-done.core_ref, ...), custom_call_target="tpu_custom_call" | custom-call | tf_op jit(solution)/shard_map/pallas_call | solution.py:83
  24.1 2.7 %collective-permute-start.11 = (bf16[512,128]{1,0:T(8,128)(2,1)S(1)}, bf16[512,128]{1,0:T(8,128)(2,1)S(1)}, u32[]{:S(2)}, u32[]{:S(2)}) collective-permute-start(bf16[512,128]{1,0:T(8,128)(2,1)S(1)} %fusion.3), channel_id=1, source_target_pairs={{0,16},{1,9},{2,18},{3,11},{4,20},{5,13},{6,22},{7,15},{8,24},{9,1... | collective-permute-start | bytes 393224 | tf_op jit(solution)/shard_map/ppermute | solution.py:69
  26.8 1.1 %collective-permute-done.8 = bf16[2,512,128]{2,1,0:T(8,128)(2,1)S(1)} collective-permute-done((bf16[2,512,128]{2,1,0:T(8,128)(2,1)S(1)}, bf16[2,512,128]{2,1,0:T(8,128)(2,1)S(1)}, u32[]{:S(2)}, u32[]{:S(2)}) %collective-permute-start.8) | collective-permute-done | bytes 262176 | tf_op jit(solution)/shard_map/ppermute | solution.py:69
  27.9 1.9 %collective-permute-start.10 = (bf16[512,128]{1,0:T(8,128)(2,1)S(1)}, bf16[512,128]{1,0:T(8,128)(2,1)S(1)}, u32[]{:S(2)}, u32[]{:S(2)}) collective-permute-start(bf16[512,128]{1,0:T(8,128)(2,1)S(1)} %fusion.2), channel_id=1, source_target_pairs={{0,8},{1,5},{2,10},{3,7},{4,12},{5,1},{6,14},{7,3},{8,0},{9,13},{1... | collective-permute-start | bytes 393224 | tf_op jit(solution)/shard_map/ppermute | solution.py:69
  29.8 0.6 %collective-permute-done.11 = bf16[512,128]{1,0:T(8,128)(2,1)S(1)} collective-permute-done((bf16[512,128]{1,0:T(8,128)(2,1)S(1)}, bf16[512,128]{1,0:T(8,128)(2,1)S(1)}, u32[]{:S(2)}, u32[]{:S(2)}) %collective-permute-start.11) | collective-permute-done | bytes 131104 | tf_op jit(solution)/shard_map/ppermute | solution.py:69
  30.4 1.7 %collective-permute-start.14 = (bf16[512,128]{1,0:T(8,128)(2,1)S(1)}, bf16[512,128]{1,0:T(8,128)(2,1)S(1)}, u32[]{:S(2)}, u32[]{:S(2)}) collective-permute-start(bf16[512,128]{1,0:T(8,128)(2,1)S(1)} %fusion), channel_id=1, source_target_pairs={{0,4},{1,17},{2,6},{3,19},{4,0},{5,21},{6,2},{7,23},{8,12},{9,25},... | collective-permute-start | bytes 393224 | tf_op jit(solution)/shard_map/ppermute | solution.py:69
  32.1 0.9 %collective-permute-done.10 = bf16[512,128]{1,0:T(8,128)(2,1)S(1)} collective-permute-done((bf16[512,128]{1,0:T(8,128)(2,1)S(1)}, bf16[512,128]{1,0:T(8,128)(2,1)S(1)}, u32[]{:S(2)}, u32[]{:S(2)}) %collective-permute-start.10) | collective-permute-done | bytes 131104 | tf_op jit(solution)/shard_map/ppermute | solution.py:69
  33.0 4.0 %collective-permute-start.13 = (bf16[512,128]{1,0:T(8,128)(2,1)S(1)}, bf16[512,128]{1,0:T(8,128)(2,1)S(1)}, u32[]{:S(2)}, u32[]{:S(2)}) collective-permute-start(bf16[512,128]{1,0:T(8,128)(2,1)S(1)} %fusion.1), channel_id=1, source_target_pairs={{0,16},{1,17},{2,18},{3,19},{4,20},{5,21},{6,22},{7,23},{8,24},{9,... | collective-permute-start | bytes 393224 | tf_op jit(solution)/shard_map/ppermute | solution.py:69
  37.1 0.8 %collective-permute-start.16 = (bf16[512,128]{1,0:T(8,128)(2,1)S(1)}, bf16[512,128]{1,0:T(8,128)(2,1)S(1)}, u32[]{:S(2)}, u32[]{:S(2)}) collective-permute-start(bf16[512,128]{1,0:T(8,128)(2,1)S(1)} %fusion.7.rest_0_), channel_id=1, source_target_pairs={{0,16},{1,9},{2,18},{3,11},{4,20},{5,13},{6,22},{7,15},{8,24},{9,1... | collective-permute-start | bytes 393224 | tf_op jit(solution)/shard_map/ppermute | solution.py:69
  37.9 2.8 %collective-permute-start.17 = (bf16[512,128]{1,0:T(8,128)(2,1)S(1)}, bf16[512,128]{1,0:T(8,128)(2,1)S(1)}, u32[]{:S(2)}, u32[]{:S(2)}) collective-permute-start(bf16[512,128]{1,0:T(8,128)(2,1)S(1)} %fusion.7.rest_0_), channel_id=1, source_target_pairs={{0,8},{1,5},{2,10},{3,7},{4,12},{5,1},{6,14},{7,3},{8,0},{9,13},{1... | collective-permute-start | bytes 393224 | tf_op jit(solution)/shard_map/ppermute | solution.py:69
  40.7 1.0 %collective-permute-done.13 = bf16[512,128]{1,0:T(8,128)(2,1)S(1)} collective-permute-done((bf16[512,128]{1,0:T(8,128)(2,1)S(1)}, bf16[512,128]{1,0:T(8,128)(2,1)S(1)}, u32[]{:S(2)}, u32[]{:S(2)}) %collective-permute-start.13) | collective-permute-done | bytes 131104 | tf_op jit(solution)/shard_map/ppermute | solution.py:69
  41.8 1.5 %collective-permute-start.15 = (bf16[512,128]{1,0:T(8,128)(2,1)S(1)}, bf16[512,128]{1,0:T(8,128)(2,1)S(1)}, u32[]{:S(2)}, u32[]{:S(2)}) collective-permute-start(bf16[512,128]{1,0:T(8,128)(2,1)S(1)} %fusion.8.rest_0_), channel_id=1, source_target_pairs={{0,8},{1,5},{2,10},{3,7},{4,12},{5,1},{6,14},{7,3},{8,0},{9,13},{1... | collective-permute-start | bytes 393224 | tf_op jit(solution)/shard_map/ppermute | solution.py:69
  43.8 1.6 %collective-permute-start.12 = (bf16[128,512]{1,0:T(8,128)(2,1)S(1)}, bf16[128,512]{1,0:T(8,128)(2,1)S(1)}, u32[]{:S(2)}, u32[]{:S(2)}) collective-permute-start(bf16[128,512]{1,0:T(8,128)(2,1)S(1)} %slice.55), channel_id=1, source_target_pairs={{0,2},{1,3},{2,0},{3,1},{4,6},{5,7},{6,4},{7,5},{8,10},{9,11},{10,... | collective-permute-start | bytes 393224 | tf_op jit(solution)/shard_map/ppermute | solution.py:73
  45.3 1.8 %collective-permute-start.19 = (bf16[512,128]{1,0:T(8,128)(2,1)S(1)}, bf16[512,128]{1,0:T(8,128)(2,1)S(1)}, u32[]{:S(2)}, u32[]{:S(2)}) collective-permute-start(bf16[512,128]{1,0:T(8,128)(2,1)S(1)} %collective-permute-done.16.rest_1_), channel_id=1, source_target_pairs={{0,8},{1,5},{2,10},{3,7},{4,12},{5,1},{6,14},{7,3},{8,0},{9,13},{1... | collective-permute-start | bytes 393224 | tf_op jit(solution)/shard_map/ppermute | solution.py:69
  47.2 1.9 %collective-permute-start.20 = (bf16[512,128]{1,0:T(8,128)(2,1)S(1)}, bf16[512,128]{1,0:T(8,128)(2,1)S(1)}, u32[]{:S(2)}, u32[]{:S(2)}) collective-permute-start(bf16[512,128]{1,0:T(8,128)(2,1)S(1)} %fusion.8.rest_0_), channel_id=1, source_target_pairs={{0,12},{1,13},{2,14},{3,15},{4,8},{5,9},{6,10},{7,11},{8,4},{9,5},... | collective-permute-start | bytes 393224 | tf_op jit(solution)/shard_map/ppermute | solution.py:69
  49.1 1.1 %shard_map.71 = (f32[1024,512]{1,0:T(8,128)}, f32[8,128]{1,0:T(8,128)S(1)}) custom-call(bf16[1,1024]{1,0:T(2,128)(2,1)S(1)} %reshape.35.gain_ref, bf16[1024,512]{1,0:T(8,128)(2,1)S(1)} %copy-done, bf16[512,128]{1,0:T(8,128)(2,1)S(1)} %fusion.7.rest_0_, bf16[512,128]{1,0:T(8,128)(2,1)S(1)} %collective-permute-done.16.rest_1_, ...), custom_call_target="tpu_custom_call" | custom-call | tf_op jit(solution)/shard_map/pallas_call | solution.py:83
  50.2 1.1 %shard_map.72 = (f32[1024,512]{1,0:T(8,128)}, f32[8,128]{1,0:T(8,128)S(1)}) custom-call(bf16[1,1024]{1,0:T(2,128)(2,1)S(1)} %reshape.35.gain_ref, bf16[1024,512]{1,0:T(8,128)(2,1)S(1)} %copy-done, bf16[512,128]{1,0:T(8,128)(2,1)S(1)} %fusion.8.rest_0_, bf16[512,128]{1,0:T(8,128)(2,1)S(1)} %collective-permute-done.15.rest_1_, ...), custom_call_target="tpu_custom_call", output_to_operand_aliasing={{0}: (5, {})} | custom-call | tf_op jit(solution)/shard_map/pallas_call | solution.py:83
  51.3 0.8 %shard_map.73 = bf16[128,512]{1,0:T(8,128)(2,1)} custom-call(f32[128,512]{1,0:T(8,128)S(1)} %slice.40.mine_ref, bf16[128,512]{1,0:T(8,128)(2,1)S(1)} %collective-permute-done.12.got_ref, f32[128,128]{1,0:T(8,128)S(1)} %get-tuple-element.64.inv_ref, f32[128,128]{1,0:T(8,128)S(1)} %get-tuple-element.74.cos_ref, f32[128,128]{1,0:T(8,128)S(1)} %get-tuple-element.75.sin_ref), custom_call_target="tpu_custom_call" | custom-call | tf_op jit(solution)/shard_map/pallas_call | solution.py:83
  52.1 0.9 %collective-permute-done.20.rest_1_ = bf16[512,128]{1,0:T(8,128)(2,1)S(1)} collective-permute-done((bf16[512,128]{1,0:T(8,128)(2,1)S(1)}, bf16[512,128]{1,0:T(8,128)(2,1)S(1)}, u32[]{:S(2)}, u32[]{:S(2)}) %collective-permute-start.20) | collective-permute-done | bytes 131104 | tf_op jit(solution)/shard_map/ppermute | solution.py:69
  53.0 1.1 %shard_map.74 = (f32[1024,512]{1,0:T(8,128)}, f32[8,128]{1,0:T(8,128)}) custom-call(bf16[1,1024]{1,0:T(2,128)(2,1)S(1)} %reshape.35.gain_ref, bf16[1024,512]{1,0:T(8,128)(2,1)S(1)} %copy-done, bf16[512,128]{1,0:T(8,128)(2,1)S(1)} %collective-permute-done.19.rest_0_, ...), custom_call_target="tpu_custom_call", output_to_operand_aliasing={{0}: (4, {})} | custom-call | tf_op jit(solution)/shard_map/pallas_call | solution.py:83
  (46 shorter events, 2.7 us)
Async XLA Ops:
  0.6 4.6 %copy-start.1 = (bf16[128,4096]{1,0:T(8,128)(2,1)S(1)}, bf16[128,4096]{1,0:T(8,128)(2,1)}, u32[]{:S(2)}) copy-start(bf16[128,4096]{1,0:T(8,128)(2,1)} %tok_ref) | copy-start | bytes 3145732
  1.7 17.9 %copy-start.3 = (bf16[1024]{0:T(1024)(128)(2,1)S(1)}, bf16[1024]{0:T(1024)(128)(2,1)}, u32[]{:S(2)}) copy-start(bf16[1024]{0:T(1024)(128)(2,1)} %param.5) | copy-start | bytes 6148
  1.8 13.0 %collective-permute-start.2 = (bf16[128,1024]{1,0:T(8,128)(2,1)S(1)}, bf16[128,1024]{1,0:T(8,128)(2,1)S(1)}, u32[]{:S(2)}, u32[]{:S(2)}) collective-permute-start(bf16[128,1024]{1,0:T(8,128)(2,1)S(1)} %pad_maximum_fusion), channel_id=1, source_target_pairs={{0,2},{1,3},{2,0},{3,1},{4,6},{5,7},{6,4},{7,5},{8,10},{9,11},{10,... | collective-permute-start | bytes 786440 | tf_op jit(solution)/shard_map/ppermute | solution.py:73
  5.2 0.9 %copy-start.2 = (bf16[128,512]{1,0:T(8,128)(2,1)S(1)}, bf16[128,512]{1,0:T(8,128)(2,1)}, u32[]{:S(2)}) copy-start(bf16[128,512]{1,0:T(8,128)(2,1)} %grad_ref.1) | copy-start | bytes 393220
  6.1 17.1 %copy-start = (bf16[1024,512]{1,0:T(8,128)(2,1)S(1)}, bf16[1024,512]{1,0:T(8,128)(2,1)}, u32[]{:S(2)}) copy-start(bf16[1024,512]{1,0:T(8,128)(2,1)} %weight_ref.6) | copy-start | bytes 3145732
  6.5 9.8 %collective-permute-start = (bf16[128,1536]{1,0:T(8,128)(2,1)S(1)}, bf16[128,1536]{1,0:T(8,128)(2,1)S(1)}, u32[]{:S(2)}, u32[]{:S(2)}) collective-permute-start(bf16[128,1536]{1,0:T(8,128)(2,1)S(1)} %get-tuple-element.38), channel_id=1, source_target_pairs={{0,1},{1,0},{2,3},{3,2},{4,5},{5,4},{6,7},{7,6},{8,9},{9,8},{10,11... | collective-permute-start | bytes 1179656 | tf_op jit(solution)/shard_map/ppermute | solution.py:73
  6.6 8.1 %collective-permute-start.4 = (bf16[128,512]{1,0:T(8,128)(2,1)S(1)}, bf16[128,512]{1,0:T(8,128)(2,1)S(1)}, u32[]{:S(2)}, u32[]{:S(2)}) collective-permute-start(bf16[128,512]{1,0:T(8,128)(2,1)S(1)} %get-tuple-element.40.scaled_ref), channel_id=1, source_target_pairs={{0,2},{1,3},{2,0},{3,1},{4,6},{5,7},{6,4},{7,5},{8,10},{9,11},{10,... | collective-permute-start | bytes 393224 | tf_op jit(solution)/shard_map/ppermute | solution.py:73
  6.7 12.8 %collective-permute-start.1 = (bf16[128,1024]{1,0:T(8,128)(2,1)S(1)}, bf16[128,1024]{1,0:T(8,128)(2,1)S(1)}, u32[]{:S(2)}, u32[]{:S(2)}) collective-permute-start(bf16[128,1024]{1,0:T(8,128)(2,1)S(1)} %get-tuple-element.39), channel_id=1, source_target_pairs={{0,2},{1,3},{2,0},{3,1},{4,6},{5,7},{6,4},{7,5},{8,10},{9,11},{10,... | collective-permute-start | bytes 786440 | tf_op jit(solution)/shard_map/ppermute | solution.py:73
  14.7 1.3 %collective-permute-start.5 = (bf16[128,512]{1,0:T(8,128)(2,1)S(1)}, bf16[128,512]{1,0:T(8,128)(2,1)S(1)}, u32[]{:S(2)}, u32[]{:S(2)}) collective-permute-start(bf16[128,512]{1,0:T(8,128)(2,1)S(1)} %collective-permute-done.4.x_grad), channel_id=1, source_target_pairs={{0,1},{1,0},{2,3},{3,2},{4,5},{5,4},{6,7},{7,6},{8,9},{9,8},{10,11... | collective-permute-start | bytes 393224 | tf_op jit(solution)/shard_map/ppermute | solution.py:73
  14.7 1.6 %collective-permute-start.3 = (bf16[128,512]{1,0:T(8,128)(2,1)S(1)}, bf16[128,512]{1,0:T(8,128)(2,1)S(1)}, u32[]{:S(2)}, u32[]{:S(2)}) collective-permute-start(bf16[128,512]{1,0:T(8,128)(2,1)S(1)} %slice.35), channel_id=1, source_target_pairs={{0,1},{1,0},{2,3},{3,2},{4,5},{5,4},{6,7},{7,6},{8,9},{9,8},{10,11... | collective-permute-start | bytes 393224 | tf_op jit(solution)/shard_map/ppermute | solution.py:73
  16.8 7.3 %collective-permute-start.9 = (bf16[2,512,128]{2,1,0:T(8,128)(2,1)S(1)}, bf16[2,512,128]{2,1,0:T(8,128)(2,1)S(1)}, u32[]{:S(2)}, u32[]{:S(2)}) collective-permute-start(bf16[2,512,128]{2,1,0:T(8,128)(2,1)S(1)} %get-tuple-element.41), channel_id=1, source_target_pairs={{0,8},{1,5},{2,10},{3,7},{4,12},{5,1},{6,14},{7,3},{8,0},{9,13},{1... | collective-permute-start | bytes 786440 | tf_op jit(solution)/shard_map/ppermute | solution.py:69
  19.5 1.4 %collective-permute-start.6 = (bf16[128,512]{1,0:T(8,128)(2,1)S(1)}, bf16[128,512]{1,0:T(8,128)(2,1)S(1)}, u32[]{:S(2)}, u32[]{:S(2)}) collective-permute-start(bf16[128,512]{1,0:T(8,128)(2,1)S(1)} %slice.28), channel_id=1, source_target_pairs={{0,1},{1,0},{2,3},{3,2},{4,5},{5,4},{6,7},{7,6},{8,9},{9,8},{10,11... | collective-permute-start | bytes 393224 | tf_op jit(solution)/shard_map/ppermute | solution.py:73
  21.4 6.4 %collective-permute-start.8 = (bf16[2,512,128]{2,1,0:T(8,128)(2,1)S(1)}, bf16[2,512,128]{2,1,0:T(8,128)(2,1)S(1)}, u32[]{:S(2)}, u32[]{:S(2)}) collective-permute-start(bf16[2,512,128]{2,1,0:T(8,128)(2,1)S(1)} %get-tuple-element.43), channel_id=1, source_target_pairs={{0,4},{1,9},{2,6},{3,11},{4,0},{5,13},{6,2},{7,15},{8,12},{9,1},{1... | collective-permute-start | bytes 786440 | tf_op jit(solution)/shard_map/ppermute | solution.py:69
  24.0 13.0 %collective-permute-start.7 = (bf16[256,512]{1,0:T(8,128)(2,1)S(1)}, bf16[256,512]{1,0:T(8,128)(2,1)S(1)}, u32[]{:S(2)}, u32[]{:S(2)}) collective-permute-start(bf16[256,512]{1,0:T(8,128)(2,1)S(1)} %get-tuple-element.46), channel_id=1, source_target_pairs={{0,1},{1,0},{2,3},{3,2},{4,5},{5,4},{6,7},{7,6},{8,9},{9,8},{10,11... | collective-permute-start | bytes 786440 | tf_op jit(solution)/shard_map/ppermute | solution.py:73
  24.1 6.2 %collective-permute-start.11 = (bf16[512,128]{1,0:T(8,128)(2,1)S(1)}, bf16[512,128]{1,0:T(8,128)(2,1)S(1)}, u32[]{:S(2)}, u32[]{:S(2)}) collective-permute-start(bf16[512,128]{1,0:T(8,128)(2,1)S(1)} %fusion.3), channel_id=1, source_target_pairs={{0,16},{1,9},{2,18},{3,11},{4,20},{5,13},{6,22},{7,15},{8,24},{9,1... | collective-permute-start | bytes 393224 | tf_op jit(solution)/shard_map/ppermute | solution.py:69
  27.9 5.0 %collective-permute-start.10 = (bf16[512,128]{1,0:T(8,128)(2,1)S(1)}, bf16[512,128]{1,0:T(8,128)(2,1)S(1)}, u32[]{:S(2)}, u32[]{:S(2)}) collective-permute-start(bf16[512,128]{1,0:T(8,128)(2,1)S(1)} %fusion.2), channel_id=1, source_target_pairs={{0,8},{1,5},{2,10},{3,7},{4,12},{5,1},{6,14},{7,3},{8,0},{9,13},{1... | collective-permute-start | bytes 393224 | tf_op jit(solution)/shard_map/ppermute | solution.py:69
  30.4 6.6 %collective-permute-start.14 = (bf16[512,128]{1,0:T(8,128)(2,1)S(1)}, bf16[512,128]{1,0:T(8,128)(2,1)S(1)}, u32[]{:S(2)}, u32[]{:S(2)}) collective-permute-start(bf16[512,128]{1,0:T(8,128)(2,1)S(1)} %fusion), channel_id=1, source_target_pairs={{0,4},{1,17},{2,6},{3,19},{4,0},{5,21},{6,2},{7,23},{8,12},{9,25},... | collective-permute-start | bytes 393224 | tf_op jit(solution)/shard_map/ppermute | solution.py:69
  33.0 8.7 %collective-permute-start.13 = (bf16[512,128]{1,0:T(8,128)(2,1)S(1)}, bf16[512,128]{1,0:T(8,128)(2,1)S(1)}, u32[]{:S(2)}, u32[]{:S(2)}) collective-permute-start(bf16[512,128]{1,0:T(8,128)(2,1)S(1)} %fusion.1), channel_id=1, source_target_pairs={{0,16},{1,17},{2,18},{3,19},{4,20},{5,21},{6,22},{7,23},{8,24},{9,... | collective-permute-start | bytes 393224 | tf_op jit(solution)/shard_map/ppermute | solution.py:69
  37.1 8.2 %collective-permute-start.16 = (bf16[512,128]{1,0:T(8,128)(2,1)S(1)}, bf16[512,128]{1,0:T(8,128)(2,1)S(1)}, u32[]{:S(2)}, u32[]{:S(2)}) collective-permute-start(bf16[512,128]{1,0:T(8,128)(2,1)S(1)} %fusion.7.rest_0_), channel_id=1, source_target_pairs={{0,16},{1,9},{2,18},{3,11},{4,20},{5,13},{6,22},{7,15},{8,24},{9,1... | collective-permute-start | bytes 393224 | tf_op jit(solution)/shard_map/ppermute | solution.py:69
  37.9 9.2 %collective-permute-start.17 = (bf16[512,128]{1,0:T(8,128)(2,1)S(1)}, bf16[512,128]{1,0:T(8,128)(2,1)S(1)}, u32[]{:S(2)}, u32[]{:S(2)}) collective-permute-start(bf16[512,128]{1,0:T(8,128)(2,1)S(1)} %fusion.7.rest_0_), channel_id=1, source_target_pairs={{0,8},{1,5},{2,10},{3,7},{4,12},{5,1},{6,14},{7,3},{8,0},{9,13},{1... | collective-permute-start | bytes 393224 | tf_op jit(solution)/shard_map/ppermute | solution.py:69
  41.8 8.4 %collective-permute-start.15 = (bf16[512,128]{1,0:T(8,128)(2,1)S(1)}, bf16[512,128]{1,0:T(8,128)(2,1)S(1)}, u32[]{:S(2)}, u32[]{:S(2)}) collective-permute-start(bf16[512,128]{1,0:T(8,128)(2,1)S(1)} %fusion.8.rest_0_), channel_id=1, source_target_pairs={{0,8},{1,5},{2,10},{3,7},{4,12},{5,1},{6,14},{7,3},{8,0},{9,13},{1... | collective-permute-start | bytes 393224 | tf_op jit(solution)/shard_map/ppermute | solution.py:69
  43.3 6.9 %collective-permute-start.18 = (bf16[512,128]{1,0:T(8,128)(2,1)S(1)}, bf16[512,128]{1,0:T(8,128)(2,1)S(1)}, u32[]{:S(2)}, u32[]{:S(2)}) collective-permute-start(bf16[512,128]{1,0:T(8,128)(2,1)S(1)} %fusion.8.rest_0_), channel_id=1, source_target_pairs={{0,4},{1,9},{2,6},{3,11},{4,0},{5,13},{6,2},{7,15},{8,12},{9,1},{1... | collective-permute-start | bytes 393224 | tf_op jit(solution)/shard_map/ppermute | solution.py:69
  43.8 7.5 %collective-permute-start.12 = (bf16[128,512]{1,0:T(8,128)(2,1)S(1)}, bf16[128,512]{1,0:T(8,128)(2,1)S(1)}, u32[]{:S(2)}, u32[]{:S(2)}) collective-permute-start(bf16[128,512]{1,0:T(8,128)(2,1)S(1)} %slice.55), channel_id=1, source_target_pairs={{0,2},{1,3},{2,0},{3,1},{4,6},{5,7},{6,4},{7,5},{8,10},{9,11},{10,... | collective-permute-start | bytes 393224 | tf_op jit(solution)/shard_map/ppermute | solution.py:73
  45.3 6.8 %collective-permute-start.19 = (bf16[512,128]{1,0:T(8,128)(2,1)S(1)}, bf16[512,128]{1,0:T(8,128)(2,1)S(1)}, u32[]{:S(2)}, u32[]{:S(2)}) collective-permute-start(bf16[512,128]{1,0:T(8,128)(2,1)S(1)} %collective-permute-done.16.rest_1_), channel_id=1, source_target_pairs={{0,8},{1,5},{2,10},{3,7},{4,12},{5,1},{6,14},{7,3},{8,0},{9,13},{1... | collective-permute-start | bytes 393224 | tf_op jit(solution)/shard_map/ppermute | solution.py:69
  47.2 5.9 %collective-permute-start.20 = (bf16[512,128]{1,0:T(8,128)(2,1)S(1)}, bf16[512,128]{1,0:T(8,128)(2,1)S(1)}, u32[]{:S(2)}, u32[]{:S(2)}) collective-permute-start(bf16[512,128]{1,0:T(8,128)(2,1)S(1)} %fusion.8.rest_0_), channel_id=1, source_target_pairs={{0,12},{1,13},{2,14},{3,15},{4,8},{5,9},{6,10},{7,11},{8,4},{9,5},... | collective-permute-start | bytes 393224 | tf_op jit(solution)/shard_map/ppermute | solution.py:69

commit v9 on v8

--- a/solution.py
+++ b/solution.py
@@ -319,9 +319,13 @@
     last = []
     straight = {1: summed(mine[1], 1, 0, 1)}
     for k in range(count):
-        near[k] = after(near[k], latest)
+        if k in straight:
+            far[k] = after(far[k], latest)
+            near[k] = after(near[k], far[k])
+        else:
+            near[k] = after(near[k], latest)
+            far[k] = after(far[k], near[k])
         last.append(straight[k] if k in straight else summed(near[k], k, 0))
-        far[k] = after(far[k], near[k])
         before = write((k,), 0, ((mine[k], near[k], far[k]),), False, before)
         latest = before[1]
     (keys,) = call(

time: 54.3 us -> 54.3 us (level)
  no operation moved by 1% of the time
where the time goes in v9:
time: 54.3 us; the launch traced here: 54.1 us
  starting transfers between devices  31 us (57%)
  waiting for transfers between devices  13.3 us (24%)
  Pallas kernels  6.06 us (11%)
  local copies, waits for them, and re-layouts  2.08 us (4%)
  between operations  0.92 us (2%)
  other arithmetic  0.77 us (1%)
    ppermute x12, starting transfers between devices, swap_wide(): return lax.ppermute(value, BOTH, pairs)  23.5 us
    ppermute x9, waiting for transfers between devices, swap_narrow(): lax.ppermute(value, 'narrow', [(i, i ^ mask) for i in range(narrow_size)])  8.86 us
    ppermute x9, starting transfers between devices, swap_narrow(): lax.ppermute(value, 'narrow', [(i, i ^ mask) for i in range(narrow_size)])  7.44 us
    pallas_call x8, Pallas kernels, call(): pl.pallas_call(body, out_shape=[jax.ShapeDtypeStruct(shape, kind) for sha...  6.06 us
    ppermute x12, waiting for transfers between devices, swap_wide(): return lax.ppermute(value, BOTH, pairs)  4.45 us
  transfers between devices with their start and end apart: 21, of which 10 were waited for; matrix products, arithmetic and copies ran while one was open for 2% of the time, Pallas kernels for 9%

profile of v9, /device:TPU:0, one launch (start us, length us, event | category | flops | bytes accessed | tf_op | source)
XLA Modules:
  0.0 54.1 jit_solution(269426377686226133)
XLA Ops:
  0.7 1.1 %constant_dynamic-slice_fusion.1 = (bf16[128,512]{1,0:T(8,128)(2,1)S(1)}, bf16[128,512]{1,0:T(8,128)(2,1)S(1)}) fusion(bf16[128,4096]{1,0:T(8,128)(2,1)} %tok_ref, s32[]{:T(128)S(6)} %select_n.17, s32[]{:T(128)S(6)} %select_n.18), kind=kLoop, calls=%fused_computation.27 | loop fusion | bytes 524296 | tf_op jit(solution)/shard_map/dynamic_slice | solution.py:246
  1.8 3.0 %collective-permute-start.2 = (bf16[128,1024]{1,0:T(8,128)(2,1)S(1)}, bf16[128,1024]{1,0:T(8,128)(2,1)S(1)}, u32[]{:S(2)}, u32[]{:S(2)}) collective-permute-start(bf16[128,1024]{1,0:T(8,128)(2,1)S(1)} %pad_maximum_fusion), channel_id=1, source_target_pairs={{0,2},{1,3},{2,0},{3,1},{4,6},{5,7},{6,4},{7,5},{8,10},{9,11},{10,... | collective-permute-start | bytes 786440 | tf_op jit(solution)/shard_map/ppermute | solution.py:73
  5.3 0.9 %copy-done.2 = bf16[128,512]{1,0:T(8,128)(2,1)S(1)} copy-done((bf16[128,512]{1,0:T(8,128)(2,1)S(1)}, bf16[128,512]{1,0:T(8,128)(2,1)}, u32[]{:S(2)}) %copy-start.2) | copy-done | bytes 131096
  6.7 2.0 %collective-permute-start.1 = (bf16[128,1024]{1,0:T(8,128)(2,1)S(1)}, bf16[128,1024]{1,0:T(8,128)(2,1)S(1)}, u32[]{:S(2)}, u32[]{:S(2)}) collective-permute-start(bf16[128,1024]{1,0:T(8,128)(2,1)S(1)} %get-tuple-element.39), channel_id=1, source_target_pairs={{0,2},{1,3},{2,0},{3,1},{4,6},{5,7},{6,4},{7,5},{8,10},{9,11},{10,... | collective-permute-start | bytes 786440 | tf_op jit(solution)/shard_map/ppermute | solution.py:73
  8.7 6.0 %collective-permute-done.4.x_grad = bf16[128,512]{1,0:T(8,128)(2,1)S(1)} collective-permute-done((bf16[128,512]{1,0:T(8,128)(2,1)S(1)}, bf16[128,512]{1,0:T(8,128)(2,1)S(1)}, u32[]{:S(2)}, u32[]{:S(2)}) %collective-permute-start.4) | collective-permute-done | bytes 131104 | tf_op jit(solution)/shard_map/ppermute | solution.py:73
  14.7 0.6 %collective-permute-start.3 = (bf16[128,512]{1,0:T(8,128)(2,1)S(1)}, bf16[128,512]{1,0:T(8,128)(2,1)S(1)}, u32[]{:S(2)}, u32[]{:S(2)}) collective-permute-start(bf16[128,512]{1,0:T(8,128)(2,1)S(1)} %slice.35), channel_id=1, source_target_pairs={{0,1},{1,0},{2,3},{3,2},{4,5},{5,4},{6,7},{7,6},{8,9},{9,8},{10,11... | collective-permute-start | bytes 393224 | tf_op jit(solution)/shard_map/ppermute | solution.py:73
  15.3 0.8 %collective-permute-done.5.last_grad = bf16[128,512]{1,0:T(8,128)(2,1)S(1)} collective-permute-done((bf16[128,512]{1,0:T(8,128)(2,1)S(1)}, bf16[128,512]{1,0:T(8,128)(2,1)S(1)}, u32[]{:S(2)}, u32[]{:S(2)}) %collective-permute-start.5) | collective-permute-done | bytes 131104 | tf_op jit(solution)/shard_map/ppermute | solution.py:73
  16.3 0.5 shard_map.68
  16.8 2.2 %collective-permute-start.9 = (bf16[2,512,128]{2,1,0:T(8,128)(2,1)S(1)}, bf16[2,512,128]{2,1,0:T(8,128)(2,1)S(1)}, u32[]{:S(2)}, u32[]{:S(2)}) collective-permute-start(bf16[2,512,128]{2,1,0:T(8,128)(2,1)S(1)} %get-tuple-element.41), channel_id=1, source_target_pairs={{0,8},{1,5},{2,10},{3,7},{4,12},{5,1},{6,14},{7,3},{8,0},{9,13},{1... | collective-permute-start | bytes 786440 | tf_op jit(solution)/shard_map/ppermute | solution.py:69
  19.0 0.5 collective-permute-done.1.x_ref.rest_1_
  19.6 1.3 %collective-permute-done.6.last_ref.rest_3_ = bf16[128,512]{1,0:T(8,128)(2,1)S(1)} collective-permute-done((bf16[128,512]{1,0:T(8,128)(2,1)S(1)}, bf16[128,512]{1,0:T(8,128)(2,1)S(1)}, u32[]{:S(2)}, u32[]{:S(2)}) %collective-permute-start.6) | collective-permute-done | bytes 131104 | tf_op jit(solution)/shard_map/ppermute | solution.py:73
  21.4 1.8 %collective-permute-start.8 = (bf16[2,512,128]{2,1,0:T(8,128)(2,1)S(1)}, bf16[2,512,128]{2,1,0:T(8,128)(2,1)S(1)}, u32[]{:S(2)}, u32[]{:S(2)}) collective-permute-start(bf16[2,512,128]{2,1,0:T(8,128)(2,1)S(1)} %get-tuple-element.43), channel_id=1, source_target_pairs={{0,4},{1,9},{2,6},{3,11},{4,0},{5,13},{6,2},{7,15},{8,12},{9,1},{1... | collective-permute-start | bytes 786440 | tf_op jit(solution)/shard_map/ppermute | solution.py:69
  23.3 0.7 %shard_map.70 = (f32[256,512]{1,0:T(8,128)S(1)}, bf16[256,512]{1,0:T(8,128)(2,1)S(1)}) custom-call(bf16[1,1024]{1,0:T(2,128)(2,1)S(1)} %reshape.35.gain_ref, bf16[1024,512]{1,0:T(8,128)(2,1)S(1)} %copy-done, bf16[128,1024]{1,0:T(8,128)(2,1)S(1)} %get-tuple-element.37.own_ref, bf16[128,1536]{1,0:T(8,128)(2,1)S(1)} %collective-permute-done.core_ref, ...), custom_call_target="tpu_custom_call" | custom-call | tf_op jit(solution)/shard_map/pallas_call | solution.py:83
  24.1 2.7 %collective-permute-start.11 = (bf16[512,128]{1,0:T(8,128)(2,1)S(1)}, bf16[512,128]{1,0:T(8,128)(2,1)S(1)}, u32[]{:S(2)}, u32[]{:S(2)}) collective-permute-start(bf16[512,128]{1,0:T(8,128)(2,1)S(1)} %fusion.3), channel_id=1, source_target_pairs={{0,16},{1,9},{2,18},{3,11},{4,20},{5,13},{6,22},{7,15},{8,24},{9,1... | collective-permute-start | bytes 393224 | tf_op jit(solution)/shard_map/ppermute | solution.py:69
  26.8 1.1 %collective-permute-done.8 = bf16[2,512,128]{2,1,0:T(8,128)(2,1)S(1)} collective-permute-done((bf16[2,512,128]{2,1,0:T(8,128)(2,1)S(1)}, bf16[2,512,128]{2,1,0:T(8,128)(2,1)S(1)}, u32[]{:S(2)}, u32[]{:S(2)}) %collective-permute-start.8) | collective-permute-done | bytes 262176 | tf_op jit(solution)/shard_map/ppermute | solution.py:69
  27.9 1.9 %collective-permute-start.10 = (bf16[512,128]{1,0:T(8,128)(2,1)S(1)}, bf16[512,128]{1,0:T(8,128)(2,1)S(1)}, u32[]{:S(2)}, u32[]{:S(2)}) collective-permute-start(bf16[512,128]{1,0:T(8,128)(2,1)S(1)} %fusion.2), channel_id=1, source_target_pairs={{0,8},{1,5},{2,10},{3,7},{4,12},{5,1},{6,14},{7,3},{8,0},{9,13},{1... | collective-permute-start | bytes 393224 | tf_op jit(solution)/shard_map/ppermute | solution.py:69
  29.8 0.6 %collective-permute-done.11 = bf16[512,128]{1,0:T(8,128)(2,1)S(1)} collective-permute-done((bf16[512,128]{1,0:T(8,128)(2,1)S(1)}, bf16[512,128]{1,0:T(8,128)(2,1)S(1)}, u32[]{:S(2)}, u32[]{:S(2)}) %collective-permute-start.11) | collective-permute-done | bytes 131104 | tf_op jit(solution)/shard_map/ppermute | solution.py:69
  30.4 1.7 %collective-permute-start.14 = (bf16[512,128]{1,0:T(8,128)(2,1)S(1)}, bf16[512,128]{1,0:T(8,128)(2,1)S(1)}, u32[]{:S(2)}, u32[]{:S(2)}) collective-permute-start(bf16[512,128]{1,0:T(8,128)(2,1)S(1)} %fusion), channel_id=1, source_target_pairs={{0,4},{1,17},{2,6},{3,19},{4,0},{5,21},{6,2},{7,23},{8,12},{9,25},... | collective-permute-start | bytes 393224 | tf_op jit(solution)/shard_map/ppermute | solution.py:69
  32.1 0.9 %collective-permute-done.10 = bf16[512,128]{1,0:T(8,128)(2,1)S(1)} collective-permute-done((bf16[512,128]{1,0:T(8,128)(2,1)S(1)}, bf16[512,128]{1,0:T(8,128)(2,1)S(1)}, u32[]{:S(2)}, u32[]{:S(2)}) %collective-permute-start.10) | collective-permute-done | bytes 131104 | tf_op jit(solution)/shard_map/ppermute | solution.py:69
  33.0 4.0 %collective-permute-start.13 = (bf16[512,128]{1,0:T(8,128)(2,1)S(1)}, bf16[512,128]{1,0:T(8,128)(2,1)S(1)}, u32[]{:S(2)}, u32[]{:S(2)}) collective-permute-start(bf16[512,128]{1,0:T(8,128)(2,1)S(1)} %fusion.1), channel_id=1, source_target_pairs={{0,16},{1,17},{2,18},{3,19},{4,20},{5,21},{6,22},{7,23},{8,24},{9,... | collective-permute-start | bytes 393224 | tf_op jit(solution)/shard_map/ppermute | solution.py:69
  37.1 0.8 %collective-permute-start.17 = (bf16[512,128]{1,0:T(8,128)(2,1)S(1)}, bf16[512,128]{1,0:T(8,128)(2,1)S(1)}, u32[]{:S(2)}, u32[]{:S(2)}) collective-permute-start(bf16[512,128]{1,0:T(8,128)(2,1)S(1)} %fusion.7.rest_0_), channel_id=1, source_target_pairs={{0,16},{1,9},{2,18},{3,11},{4,20},{5,13},{6,22},{7,15},{8,24},{9,1... | collective-permute-start | bytes 393224 | tf_op jit(solution)/shard_map/ppermute | solution.py:69
  37.9 2.8 %collective-permute-start.18 = (bf16[512,128]{1,0:T(8,128)(2,1)S(1)}, bf16[512,128]{1,0:T(8,128)(2,1)S(1)}, u32[]{:S(2)}, u32[]{:S(2)}) collective-permute-start(bf16[512,128]{1,0:T(8,128)(2,1)S(1)} %fusion.7.rest_0_), channel_id=1, source_target_pairs={{0,8},{1,5},{2,10},{3,7},{4,12},{5,1},{6,14},{7,3},{8,0},{9,13},{1... | collective-permute-start | bytes 393224 | tf_op jit(solution)/shard_map/ppermute | solution.py:69
  40.7 1.0 %collective-permute-done.13 = bf16[512,128]{1,0:T(8,128)(2,1)S(1)} collective-permute-done((bf16[512,128]{1,0:T(8,128)(2,1)S(1)}, bf16[512,128]{1,0:T(8,128)(2,1)S(1)}, u32[]{:S(2)}, u32[]{:S(2)}) %collective-permute-start.13) | collective-permute-done | bytes 131104 | tf_op jit(solution)/shard_map/ppermute | solution.py:69
  41.8 1.8 %collective-permute-start.16 = (bf16[512,128]{1,0:T(8,128)(2,1)S(1)}, bf16[512,128]{1,0:T(8,128)(2,1)S(1)}, u32[]{:S(2)}, u32[]{:S(2)}) collective-permute-start(bf16[512,128]{1,0:T(8,128)(2,1)S(1)} %fusion.8.rest_0_), channel_id=1, source_target_pairs={{0,4},{1,9},{2,6},{3,11},{4,0},{5,13},{6,2},{7,15},{8,12},{9,1},{1... | collective-permute-start | bytes 393224 | tf_op jit(solution)/shard_map/ppermute | solution.py:69
  43.8 1.6 %collective-permute-start.12 = (bf16[128,512]{1,0:T(8,128)(2,1)S(1)}, bf16[128,512]{1,0:T(8,128)(2,1)S(1)}, u32[]{:S(2)}, u32[]{:S(2)}) collective-permute-start(bf16[128,512]{1,0:T(8,128)(2,1)S(1)} %slice.55), channel_id=1, source_target_pairs={{0,2},{1,3},{2,0},{3,1},{4,6},{5,7},{6,4},{7,5},{8,10},{9,11},{10,... | collective-permute-start | bytes 393224 | tf_op jit(solution)/shard_map/ppermute | solution.py:73
  45.3 1.8 %collective-permute-start.19 = (bf16[512,128]{1,0:T(8,128)(2,1)S(1)}, bf16[512,128]{1,0:T(8,128)(2,1)S(1)}, u32[]{:S(2)}, u32[]{:S(2)}) collective-permute-start(bf16[512,128]{1,0:T(8,128)(2,1)S(1)} %collective-permute-done.17.rest_1_), channel_id=1, source_target_pairs={{0,8},{1,5},{2,10},{3,7},{4,12},{5,1},{6,14},{7,3},{8,0},{9,13},{1... | collective-permute-start | bytes 393224 | tf_op jit(solution)/shard_map/ppermute | solution.py:69
  47.2 1.9 %collective-permute-start.20 = (bf16[512,128]{1,0:T(8,128)(2,1)S(1)}, bf16[512,128]{1,0:T(8,128)(2,1)S(1)}, u32[]{:S(2)}, u32[]{:S(2)}) collective-permute-start(bf16[512,128]{1,0:T(8,128)(2,1)S(1)} %fusion.8.rest_0_), channel_id=1, source_target_pairs={{0,12},{1,13},{2,14},{3,15},{4,8},{5,9},{6,10},{7,11},{8,4},{9,5},... | collective-permute-start | bytes 393224 | tf_op jit(solution)/shard_map/ppermute | solution.py:69
  49.1 1.1 %shard_map.71 = (f32[1024,512]{1,0:T(8,128)}, f32[8,128]{1,0:T(8,128)S(1)}) custom-call(bf16[1,1024]{1,0:T(2,128)(2,1)S(1)} %reshape.35.gain_ref, bf16[1024,512]{1,0:T(8,128)(2,1)S(1)} %copy-done, bf16[512,128]{1,0:T(8,128)(2,1)S(1)} %fusion.7.rest_0_, bf16[512,128]{1,0:T(8,128)(2,1)S(1)} %collective-permute-done.17.rest_1_, ...), custom_call_target="tpu_custom_call" | custom-call | tf_op jit(solution)/shard_map/pallas_call | solution.py:83
  50.2 1.1 %shard_map.72 = (f32[1024,512]{1,0:T(8,128)}, f32[8,128]{1,0:T(8,128)S(1)}) custom-call(bf16[1,1024]{1,0:T(2,128)(2,1)S(1)} %reshape.35.gain_ref, bf16[1024,512]{1,0:T(8,128)(2,1)S(1)} %copy-done, bf16[512,128]{1,0:T(8,128)(2,1)S(1)} %fusion.8.rest_0_, bf16[512,128]{1,0:T(8,128)(2,1)S(1)} %collective-permute-done.15.rest_1_, ...), custom_call_target="tpu_custom_call", output_to_operand_aliasing={{0}: (5, {})} | custom-call | tf_op jit(solution)/shard_map/pallas_call | solution.py:83
  51.3 0.8 %shard_map.73 = bf16[128,512]{1,0:T(8,128)(2,1)} custom-call(f32[128,512]{1,0:T(8,128)S(1)} %slice.40.mine_ref, bf16[128,512]{1,0:T(8,128)(2,1)S(1)} %collective-permute-done.12.got_ref, f32[128,128]{1,0:T(8,128)S(1)} %get-tuple-element.64.inv_ref, f32[128,128]{1,0:T(8,128)S(1)} %get-tuple-element.74.cos_ref, f32[128,128]{1,0:T(8,128)S(1)} %get-tuple-element.75.sin_ref), custom_call_target="tpu_custom_call" | custom-call | tf_op jit(solution)/shard_map/pallas_call | solution.py:83
  52.2 0.9 %collective-permute-done.20.rest_1_ = bf16[512,128]{1,0:T(8,128)(2,1)S(1)} collective-permute-done((bf16[512,128]{1,0:T(8,128)(2,1)S(1)}, bf16[512,128]{1,0:T(8,128)(2,1)S(1)}, u32[]{:S(2)}, u32[]{:S(2)}) %collective-permute-start.20) | collective-permute-done | bytes 131104 | tf_op jit(solution)/shard_map/ppermute | solution.py:69
  53.0 1.1 %shard_map.74 = (f32[1024,512]{1,0:T(8,128)}, f32[8,128]{1,0:T(8,128)}) custom-call(bf16[1,1024]{1,0:T(2,128)(2,1)S(1)} %reshape.35.gain_ref, bf16[1024,512]{1,0:T(8,128)(2,1)S(1)} %copy-done, bf16[512,128]{1,0:T(8,128)(2,1)S(1)} %collective-permute-done.19.rest_0_, ...), custom_call_target="tpu_custom_call", output_to_operand_aliasing={{0}: (4, {})} | custom-call | tf_op jit(solution)/shard_map/pallas_call | solution.py:83
  (46 shorter events, 2.4 us)
Async XLA Ops:
  0.6 4.6 %copy-start.1 = (bf16[128,4096]{1,0:T(8,128)(2,1)S(1)}, bf16[128,4096]{1,0:T(8,128)(2,1)}, u32[]{:S(2)}) copy-start(bf16[128,4096]{1,0:T(8,128)(2,1)} %tok_ref) | copy-start | bytes 3145732
  1.7 17.9 %copy-start.3 = (bf16[1024]{0:T(1024)(128)(2,1)S(1)}, bf16[1024]{0:T(1024)(128)(2,1)}, u32[]{:S(2)}) copy-start(bf16[1024]{0:T(1024)(128)(2,1)} %param.5) | copy-start | bytes 6148
  1.8 13.0 %collective-permute-start.2 = (bf16[128,1024]{1,0:T(8,128)(2,1)S(1)}, bf16[128,1024]{1,0:T(8,128)(2,1)S(1)}, u32[]{:S(2)}, u32[]{:S(2)}) collective-permute-start(bf16[128,1024]{1,0:T(8,128)(2,1)S(1)} %pad_maximum_fusion), channel_id=1, source_target_pairs={{0,2},{1,3},{2,0},{3,1},{4,6},{5,7},{6,4},{7,5},{8,10},{9,11},{10,... | collective-permute-start | bytes 786440 | tf_op jit(solution)/shard_map/ppermute | solution.py:73
  5.2 0.9 %copy-start.2 = (bf16[128,512]{1,0:T(8,128)(2,1)S(1)}, bf16[128,512]{1,0:T(8,128)(2,1)}, u32[]{:S(2)}) copy-start(bf16[128,512]{1,0:T(8,128)(2,1)} %grad_ref.1) | copy-start | bytes 393220
  6.1 17.1 %copy-start = (bf16[1024,512]{1,0:T(8,128)(2,1)S(1)}, bf16[1024,512]{1,0:T(8,128)(2,1)}, u32[]{:S(2)}) copy-start(bf16[1024,512]{1,0:T(8,128)(2,1)} %weight_ref.6) | copy-start | bytes 3145732
  6.5 9.8 %collective-permute-start = (bf16[128,1536]{1,0:T(8,128)(2,1)S(1)}, bf16[128,1536]{1,0:T(8,128)(2,1)S(1)}, u32[]{:S(2)}, u32[]{:S(2)}) collective-permute-start(bf16[128,1536]{1,0:T(8,128)(2,1)S(1)} %get-tuple-element.38), channel_id=1, source_target_pairs={{0,1},{1,0},{2,3},{3,2},{4,5},{5,4},{6,7},{7,6},{8,9},{9,8},{10,11... | collective-permute-start | bytes 1179656 | tf_op jit(solution)/shard_map/ppermute | solution.py:73
  6.6 8.1 %collective-permute-start.4 = (bf16[128,512]{1,0:T(8,128)(2,1)S(1)}, bf16[128,512]{1,0:T(8,128)(2,1)S(1)}, u32[]{:S(2)}, u32[]{:S(2)}) collective-permute-start(bf16[128,512]{1,0:T(8,128)(2,1)S(1)} %get-tuple-element.40.scaled_ref), channel_id=1, source_target_pairs={{0,2},{1,3},{2,0},{3,1},{4,6},{5,7},{6,4},{7,5},{8,10},{9,11},{10,... | collective-permute-start | bytes 393224 | tf_op jit(solution)/shard_map/ppermute | solution.py:73
  6.7 12.8 %collective-permute-start.1 = (bf16[128,1024]{1,0:T(8,128)(2,1)S(1)}, bf16[128,1024]{1,0:T(8,128)(2,1)S(1)}, u32[]{:S(2)}, u32[]{:S(2)}) collective-permute-start(bf16[128,1024]{1,0:T(8,128)(2,1)S(1)} %get-tuple-element.39), channel_id=1, source_target_pairs={{0,2},{1,3},{2,0},{3,1},{4,6},{5,7},{6,4},{7,5},{8,10},{9,11},{10,... | collective-permute-start | bytes 786440 | tf_op jit(solution)/shard_map/ppermute | solution.py:73
  14.7 1.3 %collective-permute-start.5 = (bf16[128,512]{1,0:T(8,128)(2,1)S(1)}, bf16[128,512]{1,0:T(8,128)(2,1)S(1)}, u32[]{:S(2)}, u32[]{:S(2)}) collective-permute-start(bf16[128,512]{1,0:T(8,128)(2,1)S(1)} %collective-permute-done.4.x_grad), channel_id=1, source_target_pairs={{0,1},{1,0},{2,3},{3,2},{4,5},{5,4},{6,7},{7,6},{8,9},{9,8},{10,11... | collective-permute-start | bytes 393224 | tf_op jit(solution)/shard_map/ppermute | solution.py:73
  14.7 1.6 %collective-permute-start.3 = (bf16[128,512]{1,0:T(8,128)(2,1)S(1)}, bf16[128,512]{1,0:T(8,128)(2,1)S(1)}, u32[]{:S(2)}, u32[]{:S(2)}) collective-permute-start(bf16[128,512]{1,0:T(8,128)(2,1)S(1)} %slice.35), channel_id=1, source_target_pairs={{0,1},{1,0},{2,3},{3,2},{4,5},{5,4},{6,7},{7,6},{8,9},{9,8},{10,11... | collective-permute-start | bytes 393224 | tf_op jit(solution)/shard_map/ppermute | solution.py:73
  16.8 7.3 %collective-permute-start.9 = (bf16[2,512,128]{2,1,0:T(8,128)(2,1)S(1)}, bf16[2,512,128]{2,1,0:T(8,128)(2,1)S(1)}, u32[]{:S(2)}, u32[]{:S(2)}) collective-permute-start(bf16[2,512,128]{2,1,0:T(8,128)(2,1)S(1)} %get-tuple-element.41), channel_id=1, source_target_pairs={{0,8},{1,5},{2,10},{3,7},{4,12},{5,1},{6,14},{7,3},{8,0},{9,13},{1... | collective-permute-start | bytes 786440 | tf_op jit(solution)/shard_map/ppermute | solution.py:69
  19.5 1.4 %collective-permute-start.6 = (bf16[128,512]{1,0:T(8,128)(2,1)S(1)}, bf16[128,512]{1,0:T(8,128)(2,1)S(1)}, u32[]{:S(2)}, u32[]{:S(2)}) collective-permute-start(bf16[128,512]{1,0:T(8,128)(2,1)S(1)} %slice.28), channel_id=1, source_target_pairs={{0,1},{1,0},{2,3},{3,2},{4,5},{5,4},{6,7},{7,6},{8,9},{9,8},{10,11... | collective-permute-start | bytes 393224 | tf_op jit(solution)/shard_map/ppermute | solution.py:73
  21.4 6.4 %collective-permute-start.8 = (bf16[2,512,128]{2,1,0:T(8,128)(2,1)S(1)}, bf16[2,512,128]{2,1,0:T(8,128)(2,1)S(1)}, u32[]{:S(2)}, u32[]{:S(2)}) collective-permute-start(bf16[2,512,128]{2,1,0:T(8,128)(2,1)S(1)} %get-tuple-element.43), channel_id=1, source_target_pairs={{0,4},{1,9},{2,6},{3,11},{4,0},{5,13},{6,2},{7,15},{8,12},{9,1},{1... | collective-permute-start | bytes 786440 | tf_op jit(solution)/shard_map/ppermute | solution.py:69
  24.0 13.0 %collective-permute-start.7 = (bf16[256,512]{1,0:T(8,128)(2,1)S(1)}, bf16[256,512]{1,0:T(8,128)(2,1)S(1)}, u32[]{:S(2)}, u32[]{:S(2)}) collective-permute-start(bf16[256,512]{1,0:T(8,128)(2,1)S(1)} %get-tuple-element.46), channel_id=1, source_target_pairs={{0,1},{1,0},{2,3},{3,2},{4,5},{5,4},{6,7},{7,6},{8,9},{9,8},{10,11... | collective-permute-start | bytes 786440 | tf_op jit(solution)/shard_map/ppermute | solution.py:73
  24.1 6.2 %collective-permute-start.11 = (bf16[512,128]{1,0:T(8,128)(2,1)S(1)}, bf16[512,128]{1,0:T(8,128)(2,1)S(1)}, u32[]{:S(2)}, u32[]{:S(2)}) collective-permute-start(bf16[512,128]{1,0:T(8,128)(2,1)S(1)} %fusion.3), channel_id=1, source_target_pairs={{0,16},{1,9},{2,18},{3,11},{4,20},{5,13},{6,22},{7,15},{8,24},{9,1... | collective-permute-start | bytes 393224 | tf_op jit(solution)/shard_map/ppermute | solution.py:69
  27.9 5.0 %collective-permute-start.10 = (bf16[512,128]{1,0:T(8,128)(2,1)S(1)}, bf16[512,128]{1,0:T(8,128)(2,1)S(1)}, u32[]{:S(2)}, u32[]{:S(2)}) collective-permute-start(bf16[512,128]{1,0:T(8,128)(2,1)S(1)} %fusion.2), channel_id=1, source_target_pairs={{0,8},{1,5},{2,10},{3,7},{4,12},{5,1},{6,14},{7,3},{8,0},{9,13},{1... | collective-permute-start | bytes 393224 | tf_op jit(solution)/shard_map/ppermute | solution.py:69
  30.4 6.6 %collective-permute-start.14 = (bf16[512,128]{1,0:T(8,128)(2,1)S(1)}, bf16[512,128]{1,0:T(8,128)(2,1)S(1)}, u32[]{:S(2)}, u32[]{:S(2)}) collective-permute-start(bf16[512,128]{1,0:T(8,128)(2,1)S(1)} %fusion), channel_id=1, source_target_pairs={{0,4},{1,17},{2,6},{3,19},{4,0},{5,21},{6,2},{7,23},{8,12},{9,25},... | collective-permute-start | bytes 393224 | tf_op jit(solution)/shard_map/ppermute | solution.py:69
  33.0 8.7 %collective-permute-start.13 = (bf16[512,128]{1,0:T(8,128)(2,1)S(1)}, bf16[512,128]{1,0:T(8,128)(2,1)S(1)}, u32[]{:S(2)}, u32[]{:S(2)}) collective-permute-start(bf16[512,128]{1,0:T(8,128)(2,1)S(1)} %fusion.1), channel_id=1, source_target_pairs={{0,16},{1,17},{2,18},{3,19},{4,20},{5,21},{6,22},{7,23},{8,24},{9,... | collective-permute-start | bytes 393224 | tf_op jit(solution)/shard_map/ppermute | solution.py:69
  37.1 8.2 %collective-permute-start.17 = (bf16[512,128]{1,0:T(8,128)(2,1)S(1)}, bf16[512,128]{1,0:T(8,128)(2,1)S(1)}, u32[]{:S(2)}, u32[]{:S(2)}) collective-permute-start(bf16[512,128]{1,0:T(8,128)(2,1)S(1)} %fusion.7.rest_0_), channel_id=1, source_target_pairs={{0,16},{1,9},{2,18},{3,11},{4,20},{5,13},{6,22},{7,15},{8,24},{9,1... | collective-permute-start | bytes 393224 | tf_op jit(solution)/shard_map/ppermute | solution.py:69
  37.9 9.2 %collective-permute-start.18 = (bf16[512,128]{1,0:T(8,128)(2,1)S(1)}, bf16[512,128]{1,0:T(8,128)(2,1)S(1)}, u32[]{:S(2)}, u32[]{:S(2)}) collective-permute-start(bf16[512,128]{1,0:T(8,128)(2,1)S(1)} %fusion.7.rest_0_), channel_id=1, source_target_pairs={{0,8},{1,5},{2,10},{3,7},{4,12},{5,1},{6,14},{7,3},{8,0},{9,13},{1... | collective-permute-start | bytes 393224 | tf_op jit(solution)/shard_map/ppermute | solution.py:69
  41.8 8.4 %collective-permute-start.16 = (bf16[512,128]{1,0:T(8,128)(2,1)S(1)}, bf16[512,128]{1,0:T(8,128)(2,1)S(1)}, u32[]{:S(2)}, u32[]{:S(2)}) collective-permute-start(bf16[512,128]{1,0:T(8,128)(2,1)S(1)} %fusion.8.rest_0_), channel_id=1, source_target_pairs={{0,4},{1,9},{2,6},{3,11},{4,0},{5,13},{6,2},{7,15},{8,12},{9,1},{1... | collective-permute-start | bytes 393224 | tf_op jit(solution)/shard_map/ppermute | solution.py:69
  43.6 6.6 %collective-permute-start.15 = (bf16[512,128]{1,0:T(8,128)(2,1)S(1)}, bf16[512,128]{1,0:T(8,128)(2,1)S(1)}, u32[]{:S(2)}, u32[]{:S(2)}) collective-permute-start(bf16[512,128]{1,0:T(8,128)(2,1)S(1)} %fusion.8.rest_0_), channel_id=1, source_target_pairs={{0,8},{1,5},{2,10},{3,7},{4,12},{5,1},{6,14},{7,3},{8,0},{9,13},{1... | collective-permute-start | bytes 393224 | tf_op jit(solution)/shard_map/ppermute | solution.py:69
  43.8 7.6 %collective-permute-start.12 = (bf16[128,512]{1,0:T(8,128)(2,1)S(1)}, bf16[128,512]{1,0:T(8,128)(2,1)S(1)}, u32[]{:S(2)}, u32[]{:S(2)}) collective-permute-start(bf16[128,512]{1,0:T(8,128)(2,1)S(1)} %slice.55), channel_id=1, source_target_pairs={{0,2},{1,3},{2,0},{3,1},{4,6},{5,7},{6,4},{7,5},{8,10},{9,11},{10,... | collective-permute-start | bytes 393224 | tf_op jit(solution)/shard_map/ppermute | solution.py:73
  45.3 6.8 %collective-permute-start.19 = (bf16[512,128]{1,0:T(8,128)(2,1)S(1)}, bf16[512,128]{1,0:T(8,128)(2,1)S(1)}, u32[]{:S(2)}, u32[]{:S(2)}) collective-permute-start(bf16[512,128]{1,0:T(8,128)(2,1)S(1)} %collective-permute-done.17.rest_1_), channel_id=1, source_target_pairs={{0,8},{1,5},{2,10},{3,7},{4,12},{5,1},{6,14},{7,3},{8,0},{9,13},{1... | collective-permute-start | bytes 393224 | tf_op jit(solution)/shard_map/ppermute | solution.py:69
  47.2 5.9 %collective-permute-start.20 = (bf16[512,128]{1,0:T(8,128)(2,1)S(1)}, bf16[512,128]{1,0:T(8,128)(2,1)S(1)}, u32[]{:S(2)}, u32[]{:S(2)}) collective-permute-start(bf16[512,128]{1,0:T(8,128)(2,1)S(1)} %fusion.8.rest_0_), channel_id=1, source_target_pairs={{0,12},{1,13},{2,14},{3,15},{4,8},{5,9},{6,10},{7,11},{8,4},{9,5},... | collective-permute-start | bytes 393224 | tf_op jit(solution)/shard_map/ppermute | solution.py:69
